TPU v7x, 32 devices: a whole 2x2x4 slice. The times are simulated.
32 devices in a mesh: groups: 2 (over y), term: 4 (over z), sector: 4 (over x, core).
Axes of the slice: x: 2, y: 2, z: 4, core: 2. Of those that a mesh axis runs over, the one named last changes fastest.
Arguments:
- wave_blocks: bfloat16 [8, 512, 512], P(('groups', 'sector')), parts along dimension 0, may hold values from -6 to 6
- sector_rows: int32 [8], P(('groups', 'sector')), parts along dimension 0, may hold values from 64 to 512, as said below
- term_class: int32 [32], P(('groups', 'term')), parts along dimension 0, may hold values from 0 to 4, as said below
- left_env: bfloat16 [32, 4, 512, 512], P(('groups', 'term'), 'sector'), parts along dimension 0, may hold values from -0.25 to 0.25
- right_env: bfloat16 [32, 4, 512, 512], P(('groups', 'term'), 'sector'), parts along dimension 0, may hold values from -0.0625 to 0.0625
Outputs:
- applied: bfloat16 [8, 512, 512], P(('groups', 'sector'), 'term'), parts along dimension 0
There are 2 independent parts, one for each index of `groups`. A program takes and returns all parts, laid end to end along the dimension named above; each array names one. Nothing has to cross between parts.
Inputs may be any that keep to these rules, and one draw needn't show every extreme that they name: `sector_rows`: some sector has all 512 rows live in every draw. `term_class`: each of the five classes is held by at least one term.
All inputs are finite; a program needn't handle non-finite values.
Results may differ from a plain program's by a relative error of at most 0.0049.
Values may be sent and summed in bfloat16 or wider, within the bound.
No kernel may reach another device: no remote copies, remote signals or barrier semaphores. Data moves between devices by JAX's collectives and lax.ppermute only.
A program may use at most 64 MiB of HBM per device.

v0:
```python
import jax
import jax.numpy as jnp
from jax import lax
from jax.sharding import PartitionSpec as P


def per_device(wave_blocks, sector_rows, term_class, left_env, right_env):
    pad_rows = wave_blocks.shape[1]
    row_index = jnp.arange(pad_rows, dtype=jnp.int32)
    zero_block = jnp.zeros((), wave_blocks.dtype)
    masked = jnp.where(
        row_index[None, :, None] < sector_rows[:, None, None], wave_blocks, zero_block
    )
    sectors = lax.axis_size("sector")
    grid = max(2, sectors // 4)
    own = lax.axis_index("sector")
    column = own % grid
    lefts = left_env[:, 0]
    rights = right_env[:, 0]
    whole = lax.all_gather(masked, "sector", axis=0, tiled=True)
    offset_table = jnp.array([0, 1, -1, grid, -grid], dtype=jnp.int32)
    class_ids = jnp.arange(5, dtype=jnp.int32)
    picked_list = []
    for position in range(term_class.shape[0]):
        current = term_class[position]
        offset_now = jnp.sum(jnp.where(class_ids == current, offset_table, 0))
        source = own - offset_now
        usable = (source >= 0) & (source < sectors)
        usable = usable & jnp.logical_not((current == 1) & (column == 0))
        usable = usable & jnp.logical_not((current == 2) & (column == grid - 1))
        clipped = jnp.clip(source, 0, sectors - 1)
        block_now = lax.dynamic_index_in_dim(whole, clipped, 0, keepdims=False)
        picked_list.append(jnp.where(usable, block_now, zero_block))
    sources = jnp.stack(picked_list)
    halfway = jnp.einsum("kij,kjc->kic", lefts, sources, preferred_element_type=jnp.float32).astype(
        jnp.bfloat16
    )
    share = pad_rows // lax.axis_size("term")
    summed = lax.psum_scatter(
        jnp.einsum("kic,kdc->id", halfway, rights, preferred_element_type=jnp.float32),
        "term",
        scatter_dimension=0,
        tiled=True,
    )
    global_rows = lax.axis_index("term") * share + jnp.arange(share, dtype=jnp.int32)
    kept = global_rows[:, None] < sector_rows[0]
    applied = jnp.where(kept, summed, jnp.zeros((), summed.dtype)).astype(jnp.bfloat16)
    return applied[None]


def solution(mesh):
    placed = (
        P(("groups", "sector"), None, None),
        P(("groups", "sector")),
        P(("groups", "term")),
        P(("groups", "term"), "sector", None, None),
        P(("groups", "term"), "sector", None, None),
    )
    return jax.shard_map(
        per_device,
        mesh=mesh,
        in_specs=placed,
        out_specs=P(("groups", "sector"), "term", None),
        check_vma=False,
    )
```

profile of v0, /device:TPU:0, one launch (start us, length us, event | category | flops | bytes accessed | tf_op | source)
XLA Modules:
  0.0 78.8 jit_solution(15100693817841753113)
XLA Ops:
  6.5 0.0 copy-start
  6.5 0.0 all-gather.2.cloned.1.call-start
  7.4 2.0 %broadcast_select_fusion = bf16[1,512,512]{2,1,0:T(8,128)(2,1)} fusion(bf16[1,512,512]{2,1,0:T(8,128)(2,1)} %param.6, pred[512]{0:T(512)(128)(4,1)S(1)} %iota_compare_fusion), kind=kLoop, calls=%fused_computation.18 | loop fusion | flops 262144 | bytes 1049088 | tf_op jit(solution)/shard_map/jit(_where)/select_n | solution.py:11
  9.3 0.0 all-gather.2.cloned.1.call-update
  9.4 0.0 reduce-scatter.2.cloned.1.call-start
  9.4 1.5 %fusion.33 = (s32[1]{0:T(128)}, s32[1]{0:T(128)}, s32[1]{0:T(128)}, s32[1]{0:T(128)}) fusion(s32[4]{0:T(128)} %param.8), kind=kLoop, calls=%fused_computation.32 | loop fusion | bytes 32 | tf_op jit(solution)/shard_map/slice | solution.py:25
  15.9 3.9 %fusion.27 = (s32[]{:T(128)}, s32[]{:T(128)}, s32[]{:T(128)}, s32[]{:T(128)}) fusion(s32[5]{0:T(128)} %constant.48.clone, s32[]{:T(128)} %bitcast.1, s32[]{:T(128)} %bitcast.2, s32[]{:T(128)} %bitcast.4, s32[]{:T(128)} %bitcast.3), kind=kLoop, calls=%fused_computation.26 | loop fusion | flops 56 | bytes 52 | tf_op jit(solution)/shard_map/reduce_sum | solution.py:26
  22.6 12.2 %all-gather.2.cloned.1.call-done = bf16[4,512,512]{2,1,0:T(8,128)(2,1)} async-done(((bf16[1,512,512]{2,1,0:T(8,128)(2,1)}), bf16[4,512,512]{2,1,0:T(8,128)(2,1)}) %all-gather.2.cloned.1.call-update) | async-done | bytes 2097168 | tf_op jit(solution)/shard_map/all_gather | solution.py:20
  34.8 2.6 %dynamic-slice_select_fusion.3 = (bf16[1,512,512]{2,1,0:T(8,128)(2,1)S(1)}, bf16[1,512,512]{2,1,0:T(8,128)(2,1)S(1)}, bf16[1,512,512]{2,1,0:T(8,128)(2,1)}, bf16[1,512,512]{2,1,0:T(8,128)(2,1)}) fusion(bf16[4,512,512]{2,1,0:T(8,128)(2,1)} %all-gather.2.cloned.1.call-done, s32[]{:T(128)S(6)} %min.13, pred[]{:T(512)S(6)} %and.72, s32[]{:T(128)S(6)} %min.16, ...), kind=kLoop, calls=%fused_computation.17 | loop fusion | flops 1048576 | bytes 4194324 | tf_op jit(solution)/shard_map/jit(_where)/select_n | solution.py:33
  37.4 0.0 copy-done
  37.5 5.2 %fusion.13 = f32[512,512]{1,0:T(8,128)} fusion(bf16[4,1,512,512]{3,2,1,0:T(8,128)(2,1)S(1)} %copy-done, bf16[1,512,512]{2,1,0:T(8,128)(2,1)S(1)} %get-tuple-element.10, bf16[1,512,512]{2,1,0:T(8,128)(2,1)} %get-tuple-element.11, bf16[1,512,512]{2,1,0:T(8,128)(2,1)} %get-tuple-element.12, bf16[1,512,512]{2,1,0:T(8,128)(2,1)S(1)} %get-tuple-element.9, ...), kind=kOutput, calls=%fused_computation.13 | convolution fusion | flops 2156920832 | bytes 7340032 | tf_op jit(solution)/shard_map/kic,kdc->id/dot_general | solution.py:40
  42.6 0.0 reduce-scatter.2.cloned.1.call-update
  42.7 27.6 %reduce-scatter.2.cloned.1.call-done = f32[128,512]{1,0:T(8,128)} async-done(((f32[512,512]{1,0:T(8,128)}), f32[128,512]{1,0:T(8,128)}) %reduce-scatter.2.cloned.1.call-update) | async-done | bytes 262160 | tf_op jit(solution)/shard_map/reduce_scatter | solution.py:39
  70.3 1.7 %fusion.26 = bf16[1,128,512]{2,1,0:T(8,128)(2,1)} fusion(f32[128,512]{1,0:T(8,128)} %reduce-scatter.2.cloned.1.call-done, pred[128]{0:T(512)(128)(4,1)S(1)} %add_compare_fusion), kind=kLoop, calls=%fused_computation.20 | loop fusion | flops 65536 | bytes 393344 | tf_op jit(solution)/shard_map/broadcast_in_dim | solution.py:48
  (2 shorter events, 0.0 us)
Async XLA Ops:
  6.5 30.9 %copy-start = (bf16[4,1,512,512]{3,2,1,0:T(8,128)(2,1)S(1)}, bf16[4,1,512,512]{3,2,1,0:T(8,128)(2,1)}, u32[]{:S(2)}) copy-start(bf16[4,1,512,512]{3,2,1,0:T(8,128)(2,1)} %param.10) | copy-start | bytes 6291460
  6.5 28.3 %all-gather.2.cloned.1.call-start = ((), (), s32[]{:S(2)}) async-start(), calls=%async_computation.1 | async-start | bytes 2621440 | tf_op jit(solution)/shard_map/all_gather | solution.py:20
  9.4 60.9 %reduce-scatter.2.cloned.1.call-start = ((), (), s32[]{:S(2)}) async-start(), calls=%async_computation.2 | async-start | bytes 1310720 | tf_op jit(solution)/shard_map/reduce_scatter | solution.py:39
Sparse Core Ops, SparseCore 0:
  9.5 25.2 all-gather.1
  42.8 27.4 reduce-scatter.1
where the time goes:
time: 79 us; the launch traced here: 78.8 us
  waiting for transfers between devices  39.9 us (51%)
  between operations  22 us (28%)
  other arithmetic  10.2 us (13%)
  matrix products  5.16 us (7%)
  local copies, waits for them, and re-layouts  1.46 us (2%)
    reduce_scatter x1, waiting for transfers between devices, per_device(): lax.psum_scatter(jnp.einsum('kic,kdc->id', halfway, rights, preferred_ele...  27.6 us
    all_gather x1, waiting for transfers between devices, per_device(): whole = lax.all_gather(masked, 'sector', axis=0, tiled=True)  12.2 us
    dot_general x1, matrix products, per_device(): jnp.einsum('kic,kdc->id', halfway, rights, preferred_element_type=jnp.flo...  5.16 us
    reduce_sum x1, other arithmetic, per_device(): offset_now = jnp.sum(jnp.where(class_ids == current, offset_table, 0))  3.89 us
    select_n x1, other arithmetic, per_device(): picked_list.append(jnp.where(usable, block_now, zero_block))  2.64 us
    select_n x1, other arithmetic, per_device(): jnp.where(row_index[None, :, None] < sector_rows[:, None, None], wave_blo...  1.98 us
    broadcast_in_dim x1, other arithmetic, per_device(): return applied[None]  1.69 us
  transfers between devices with their start and end apart: 2, of which 2 were waited for; matrix products, arithmetic and copies ran while one was open for 7% of the time, Pallas kernels for 0%

commit v1 on v0

v1 whole, which is shorter than its diff:
```python
import functools

import jax
import jax.numpy as jnp
from jax import lax
from jax.experimental import pallas as pl
from jax.experimental.pallas import tpu as pltpu
from jax.sharding import PartitionSpec as P

SMEM = pl.BlockSpec(memory_space=pltpu.SMEM)
VMEM = pl.BlockSpec(memory_space=pltpu.VMEM)


def neighbour_moves(sectors, grid):
    down_in = [(s, s + 1) for s in range(sectors - 1) if (s + 1) % grid != 0]
    down_out = [(s, s - 1) for s in range(1, sectors) if s % grid != 0]
    up_in = [(s, s + grid) for s in range(sectors - grid)]
    up_out = [(s, s - grid) for s in range(grid, sectors)]
    moves = []
    for first, second in ((down_in, down_out), (up_in, up_out)):
        targets = [t for _, t in first + second]
        if len(set(targets)) == len(targets):
            moves.append([first + second])
        else:
            moves.append([first, second])
    return moves


def usable_of(kind, own, sectors, grid):
    column = lax.rem(own, grid)
    usable = kind == 0
    usable = usable | ((kind == 1) & (column != 0))
    usable = usable | ((kind == 2) & (column != grid - 1))
    usable = usable | ((kind == 3) & (own >= grid))
    return usable | ((kind == 4) & (own < sectors - grid))


def add_terms(classes, rows_refs, block_refs, slots, left, right, masked, total, sectors, grid):
    own = lax.axis_index("sector")
    pad = total.shape[0]
    row = lax.broadcasted_iota(jnp.int32, (pad, pad), 0)
    for place, (rows_ref, block_ref) in enumerate(zip(rows_refs, block_refs)):
        masked[place] = jnp.where(row < rows_ref[0], block_ref[0], jnp.zeros((), jnp.bfloat16))
    for term in range(left.shape[0]):
        kind = classes[term]
        member = functools.reduce(jnp.logical_or, [kind == k for k in slots])
        slot = sum(jnp.where(kind == k, place, 0) for k, place in slots.items())

        @pl.when(member & usable_of(kind, own, sectors, grid))
        def _():
            half = jnp.dot(left[term, 0], masked[slot], preferred_element_type=jnp.float32)
            total[...] += lax.dot_general(
                half.astype(jnp.bfloat16),
                right[term, 0],
                (((1,), (1,)), ((), ())),
                preferred_element_type=jnp.float32,
            )


def first_kernel(slots, count, sectors, grid, classes, *refs):
    rows_refs, block_refs = refs[:count], refs[count : 2 * count]
    left, right, total, masked = refs[2 * count :]
    total[...] = jnp.zeros_like(total)
    add_terms(classes, rows_refs, block_refs, slots, left, right, masked, total, sectors, grid)


def second_kernel(slots, count, sectors, grid, classes, *refs):
    rows_refs, block_refs = refs[:count], refs[count : 2 * count]
    left, right, before, kept = refs[2 * count : 2 * count + 4]
    sent = refs[2 * count + 4 : -2]
    masked, total = refs[-2:]
    total[...] = before[...]
    add_terms(classes, rows_refs, block_refs, slots, left, right, masked, total, sectors, grid)
    share = kept.shape[0]
    parts = len(sent) + 1
    me = lax.axis_index("term")
    kept[...] = total[pl.ds(pl.multiple_of(me * share, share), share), :]
    for step in range(1, parts):
        to = lax.rem(me + step, parts)
        sent[step - 1][...] = total[pl.ds(pl.multiple_of(to * share, share), share), :].astype(jnp.bfloat16)


def last_kernel(rows_ref, kept, *refs):
    got, out = refs[:-1], refs[-1]
    share = kept.shape[0]
    total = kept[...]
    for part in got:
        total = total + part[...].astype(jnp.float32)
    row = lax.axis_index("term") * share + lax.broadcasted_iota(jnp.int32, total.shape, 0)
    out[0] = jnp.where(row < rows_ref[0], total, 0.0).astype(jnp.bfloat16)


def per_device(wave_blocks, sector_rows, term_class, left_env, right_env):
    pad = wave_blocks.shape[1]
    sectors, parts = lax.axis_size("sector"), lax.axis_size("term")
    grid = max(2, sectors // 4)
    share = pad // parts
    down, up = neighbour_moves(sectors, grid)
    send = lambda array, pairs: lax.ppermute(array, "sector", pairs)
    down_blocks = [send(wave_blocks, pairs) for pairs in down]
    up_blocks = [send(wave_blocks, pairs) for pairs in up]
    down_rows = [send(sector_rows, pairs) for pairs in down]
    up_rows = [send(sector_rows, pairs) for pairs in up]
    limit = pltpu.CompilerParams(vmem_limit_bytes=24 * 2**20)

    first = [wave_blocks] + down_blocks
    count = len(first)
    total = pl.pallas_call(
        functools.partial(first_kernel, {0: 0, 1: 1, 2: len(down)}, count, sectors, grid),
        out_shape=jax.ShapeDtypeStruct((pad, pad), jnp.float32),
        in_specs=[SMEM] * (1 + count) + [VMEM] * (count + 2),
        out_specs=VMEM,
        scratch_shapes=[pltpu.VMEM((count, pad, pad), jnp.bfloat16)],
        compiler_params=limit,
        name="near_terms",
    )(term_class, sector_rows, *down_rows, *first, left_env, right_env)

    count = len(up_blocks)
    kept, *sent = pl.pallas_call(
        functools.partial(second_kernel, {3: 0, 4: len(up) - 1}, count, sectors, grid),
        out_shape=[jax.ShapeDtypeStruct((share, pad), jnp.float32)]
        + [jax.ShapeDtypeStruct((share, pad), jnp.bfloat16)] * (parts - 1),
        in_specs=[SMEM] * (1 + count) + [VMEM] * (count + 3),
        out_specs=[VMEM] * parts,
        scratch_shapes=[pltpu.VMEM((count, pad, pad), jnp.bfloat16), pltpu.VMEM((pad, pad), jnp.float32)],
        compiler_params=limit,
        name="far_terms",
    )(term_class, *up_rows, *up_blocks, left_env, right_env, total)

    got = [
        lax.ppermute(part, "term", [(i, (i + step) % parts) for i in range(parts)])
        for step, part in enumerate(sent, 1)
    ]
    return pl.pallas_call(
        last_kernel,
        out_shape=jax.ShapeDtypeStruct((1, share, pad), jnp.bfloat16),
        in_specs=[SMEM] + [VMEM] * parts,
        out_specs=VMEM,
        compiler_params=limit,
        name="sum_parts",
    )(sector_rows, kept, *got)


def solution(mesh):
    placed = (
        P(("groups", "sector"), None, None),
        P(("groups", "sector")),
        P(("groups", "term")),
        P(("groups", "term"), "sector", None, None),
        P(("groups", "term"), "sector", None, None),
    )
    return jax.shard_map(
        per_device,
        mesh=mesh,
        in_specs=placed,
        out_specs=P(("groups", "sector"), "term", None),
        check_vma=False,
    )
```

time: 79 us -> 32.4 us (0.41)
  the two profiles are of different devices: /device:TPU:0 before, /device:TPU:11 now
where the time goes in v1:
time: 32.4 us; the launch traced here: 32 us
  waiting for transfers between devices  14.2 us (44%)
  starting transfers between devices  7.24 us (22%)
  Pallas kernels  5.01 us (15%)
  local copies, waits for them, and re-layouts  4.89 us (15%)
  between operations  0.68 us (2%)
    ppermute x3, waiting for transfers between devices, per_device(): lax.ppermute(part, 'term', [(i, (i + step) % parts) for i in range(parts)])  11 us
    unnamed x12, local copies, waits for them, and re-layouts  4.89 us
    ppermute x3, starting transfers between devices, per_device(): lax.ppermute(part, 'term', [(i, (i + step) % parts) for i in range(parts)])  4.53 us
    ppermute x4, waiting for transfers between devices, per_device(): send = lambda array, pairs: lax.ppermute(array, 'sector', pairs)  3.25 us
    pallas_call x1, Pallas kernels, per_device(): pl.pallas_call(functools.partial(first_kernel, {0: 0, 1: 1, 2: len(down)}...  2.94 us
    ppermute x4, starting transfers between devices, per_device(): send = lambda array, pairs: lax.ppermute(array, 'sector', pairs)  2.7 us
    pallas_call x1, Pallas kernels, per_device(): pl.pallas_call(functools.partial(second_kernel, {3: 0, 4: len(up) - 1}, c...  1.32 us
    pallas_call x1, Pallas kernels, per_device(): pl.pallas_call(last_kernel, out_shape=jax.ShapeDtypeStruct((1, share, pad...  0.74 us
  transfers between devices with their start and end apart: 7, of which 4 were waited for; matrix products, arithmetic and copies ran while one was open for 0% of the time, Pallas kernels for 9%

profile of v1, /device:TPU:11, one launch (start us, length us, event | category | flops | bytes accessed | tf_op | source)
XLA Modules:
  0.0 32.0 jit_solution(15827105291662879504)
XLA Ops:
  0.0 0.7 %collective-permute-start.3 = (bf16[1,512,512]{2,1,0:T(8,128)(2,1)}, bf16[1,512,512]{2,1,0:T(8,128)(2,1)S(1)}, u32[]{:S(2)}, u32[]{:S(2)}) collective-permute-start(bf16[1,512,512]{2,1,0:T(8,128)(2,1)} %refs_2_.2), channel_id=1, source_target_pairs={{0,1},{2,3},{1,0},{3,2},{4,5},{6,7},{5,4},{7,6},{8,9},{10,11},{9,8... | collective-permute-start | bytes 1572872 | tf_op jit(solution)/shard_map/ppermute | solution.py:99
  0.7 0.3 collective-permute-start.1
  0.9 1.2 %collective-permute-start = (s32[1]{0:T(128)}, s32[1]{0:T(128)}, u32[]{:S(2)}, u32[]{:S(2)}) collective-permute-start(s32[1]{0:T(128)} %param.6), channel_id=1, source_target_pairs={{0,2},{1,3},{2,0},{3,1},{4,6},{5,7},{6,4},{7,5},{8,10},{9,11},{10,... | collective-permute-start | bytes 20 | tf_op jit(solution)/shard_map/ppermute | solution.py:99
  2.1 0.6 %collective-permute-start.2 = (s32[1]{0:T(128)}, s32[1]{0:T(128)}, u32[]{:S(2)}, u32[]{:S(2)}) collective-permute-start(s32[1]{0:T(128)} %param.6), channel_id=1, source_target_pairs={{0,1},{2,3},{1,0},{3,2},{4,5},{6,7},{5,4},{7,6},{8,9},{10,11},{9,8... | collective-permute-start | bytes 20 | tf_op jit(solution)/shard_map/ppermute | solution.py:99
  3.4 0.3 collective-permute-done.2.refs_1_
  3.7 0.0 collective-permute-done.3.refs_3_
  3.7 0.0 copy-start
  3.7 1.6 %copy-done = bf16[4,1,512,512]{3,2,1,0:T(8,128)(2,1)S(1)} copy-done((bf16[4,1,512,512]{3,2,1,0:T(8,128)(2,1)S(1)}, bf16[4,1,512,512]{3,2,1,0:T(8,128)(2,1)}, u32[]{:S(2)}) %copy-start) | copy-done | bytes 2097176
  5.3 0.0 copy-start.2
  5.3 1.6 %copy-done.2 = bf16[4,1,512,512]{3,2,1,0:T(8,128)(2,1)S(1)} copy-done((bf16[4,1,512,512]{3,2,1,0:T(8,128)(2,1)S(1)}, bf16[4,1,512,512]{3,2,1,0:T(8,128)(2,1)}, u32[]{:S(2)}) %copy-start.2) | copy-done | bytes 2097176
  6.8 0.0 copy-start.4
  6.8 1.0 %copy-done.4 = bf16[1,512,512]{2,1,0:T(8,128)(2,1)S(1)} copy-done((bf16[1,512,512]{2,1,0:T(8,128)(2,1)S(1)}, bf16[1,512,512]{2,1,0:T(8,128)(2,1)}, u32[]{:S(2)}) %copy-start.4) | copy-done | bytes 524312
  7.9 0.0 copy-start.5
  7.9 0.7 %copy-done.5 = s32[4]{0:T(128)S(1)} copy-done((s32[4]{0:T(128)S(1)}, s32[4]{0:T(128)}, u32[]{:S(2)}) %copy-start.5) | copy-done | bytes 40
  8.5 0.0 copy-start.1
  8.5 0.0 copy-start.3
  8.5 2.9 %near_terms.1.refs_4_ = f32[512,512]{1,0:T(8,128)S(1)} custom-call(s32[4]{0:T(128)S(1)} %copy-done.5, s32[1]{0:T(128)S(6)} %copy.6.refs_0_.rows_ref, s32[1]{0:T(128)} %collective-permute-done.2.refs_1_, bf16[1,512,512]{2,1,0:T(8,128)(2,1)S(1)} %copy-done.4, bf16[1,512,512]{2,1,0:T(8,128)(2,1)S(1)} %collective-permute-done.3.refs_3_, ...), custom_call_target="tpu_custom_call" | custom-call | tf_op jit(solution)/shard_map/near_terms/pallas_call | solution.py:108
  11.5 2.9 %collective-permute-done.refs_0_ = s32[1]{0:T(128)} collective-permute-done((s32[1]{0:T(128)}, s32[1]{0:T(128)}, u32[]{:S(2)}, u32[]{:S(2)}) %collective-permute-start) | collective-permute-done | bytes 36 | tf_op jit(solution)/shard_map/ppermute | solution.py:99
  14.4 0.0 collective-permute-done.1.refs_1_
  14.4 0.0 copy-done.1
  14.4 0.0 copy-done.3
  14.5 1.3 %far_terms.1 = (f32[128,512]{1,0:T(8,128)S(1)}, bf16[128,512]{1,0:T(8,128)(2,1)S(1)}, bf16[128,512]{1,0:T(8,128)(2,1)S(1)}, bf16[128,512]{1,0:T(8,128)(2,1)S(1)}) custom-call(s32[4]{0:T(128)S(1)} %copy-done.5, s32[1]{0:T(128)} %collective-permute-done.refs_0_, bf16[1,512,512]{2,1,0:T(8,128)(2,1)S(1)} %collective-permute-done.1.refs_1_, ...), custom_call_target="tpu_custom_call" | custom-call | tf_op jit(solution)/shard_map/far_terms/pallas_call | solution.py:119
  15.8 2.1 %collective-permute-start.4 = (bf16[128,512]{1,0:T(8,128)(2,1)S(1)}, bf16[128,512]{1,0:T(8,128)(2,1)S(1)}, u32[]{:S(2)}, u32[]{:S(2)}) collective-permute-start(bf16[128,512]{1,0:T(8,128)(2,1)S(1)} %get-tuple-element.10), channel_id=1, source_target_pairs={{0,4},{4,8},{8,12},{12,0},{1,5},{5,9},{9,13},{13,1},{2,6},{6,10},{... | collective-permute-start | bytes 393224 | tf_op jit(solution)/shard_map/ppermute | solution.py:131
  17.8 1.1 %collective-permute-start.5 = (bf16[128,512]{1,0:T(8,128)(2,1)S(1)}, bf16[128,512]{1,0:T(8,128)(2,1)S(1)}, u32[]{:S(2)}, u32[]{:S(2)}) collective-permute-start(bf16[128,512]{1,0:T(8,128)(2,1)S(1)} %get-tuple-element.11), channel_id=1, source_target_pairs={{0,8},{4,12},{8,0},{12,4},{1,9},{5,13},{9,1},{13,5},{2,10},{6,14},... | collective-permute-start | bytes 393224 | tf_op jit(solution)/shard_map/ppermute | solution.py:131
  18.9 1.4 %collective-permute-start.6 = (bf16[128,512]{1,0:T(8,128)(2,1)S(1)}, bf16[128,512]{1,0:T(8,128)(2,1)S(1)}, u32[]{:S(2)}, u32[]{:S(2)}) collective-permute-start(bf16[128,512]{1,0:T(8,128)(2,1)S(1)} %get-tuple-element.12), channel_id=1, source_target_pairs={{0,12},{4,0},{8,4},{12,8},{1,13},{5,1},{9,5},{13,9},{2,14},{6,2},{... | collective-permute-start | bytes 393224 | tf_op jit(solution)/shard_map/ppermute | solution.py:131
  20.3 0.0 collective-permute-done.4.refs_0_
  20.3 7.8 %collective-permute-done.5.refs_1_ = bf16[128,512]{1,0:T(8,128)(2,1)S(1)} collective-permute-done((bf16[128,512]{1,0:T(8,128)(2,1)S(1)}, bf16[128,512]{1,0:T(8,128)(2,1)S(1)}, u32[]{:S(2)}, u32[]{:S(2)}) %collective-permute-start.5) | collective-permute-done | bytes 131104 | tf_op jit(solution)/shard_map/ppermute | solution.py:131
  28.1 3.2 %collective-permute-done.6.refs_2_ = bf16[128,512]{1,0:T(8,128)(2,1)S(1)} collective-permute-done((bf16[128,512]{1,0:T(8,128)(2,1)S(1)}, bf16[128,512]{1,0:T(8,128)(2,1)S(1)}, u32[]{:S(2)}, u32[]{:S(2)}) %collective-permute-start.6) | collective-permute-done | bytes 131104 | tf_op jit(solution)/shard_map/ppermute | solution.py:131
  31.3 0.7 %sum_parts.1 = bf16[1,128,512]{2,1,0:T(8,128)(2,1)} custom-call(s32[1]{0:T(128)S(6)} %copy.6.refs_0_.rows_ref, f32[128,512]{1,0:T(8,128)S(1)} %get-tuple-element.9.kept, bf16[128,512]{1,0:T(8,128)(2,1)S(1)} %collective-permute-done.4.refs_0_, bf16[128,512]{1,0:T(8,128)(2,1)S(1)} %collective-permute-done.5.refs_1_, ...), custom_call_target="tpu_custom_call" | custom-call | tf_op jit(solution)/shard_map/sum_parts/pallas_call | solution.py:134
Async XLA Ops:
  0.0 3.7 %collective-permute-start.3 = (bf16[1,512,512]{2,1,0:T(8,128)(2,1)}, bf16[1,512,512]{2,1,0:T(8,128)(2,1)S(1)}, u32[]{:S(2)}, u32[]{:S(2)}) collective-permute-start(bf16[1,512,512]{2,1,0:T(8,128)(2,1)} %refs_2_.2), channel_id=1, source_target_pairs={{0,1},{2,3},{1,0},{3,2},{4,5},{6,7},{5,4},{7,6},{8,9},{10,11},{9,8... | collective-permute-start | bytes 1572872 | tf_op jit(solution)/shard_map/ppermute | solution.py:99
  0.7 13.8 %collective-permute-start.1 = (bf16[1,512,512]{2,1,0:T(8,128)(2,1)}, bf16[1,512,512]{2,1,0:T(8,128)(2,1)S(1)}, u32[]{:S(2)}, u32[]{:S(2)}) collective-permute-start(bf16[1,512,512]{2,1,0:T(8,128)(2,1)} %refs_2_.2), channel_id=1, source_target_pairs={{0,2},{1,3},{2,0},{3,1},{4,6},{5,7},{6,4},{7,5},{8,10},{9,11},{10,... | collective-permute-start | bytes 1572872 | tf_op jit(solution)/shard_map/ppermute | solution.py:99
  0.9 13.5 %collective-permute-start = (s32[1]{0:T(128)}, s32[1]{0:T(128)}, u32[]{:S(2)}, u32[]{:S(2)}) collective-permute-start(s32[1]{0:T(128)} %param.6), channel_id=1, source_target_pairs={{0,2},{1,3},{2,0},{3,1},{4,6},{5,7},{6,4},{7,5},{8,10},{9,11},{10,... | collective-permute-start | bytes 20 | tf_op jit(solution)/shard_map/ppermute | solution.py:99
  2.1 1.5 %collective-permute-start.2 = (s32[1]{0:T(128)}, s32[1]{0:T(128)}, u32[]{:S(2)}, u32[]{:S(2)}) collective-permute-start(s32[1]{0:T(128)} %param.6), channel_id=1, source_target_pairs={{0,1},{2,3},{1,0},{3,2},{4,5},{6,7},{5,4},{7,6},{8,9},{10,11},{9,8... | collective-permute-start | bytes 20 | tf_op jit(solution)/shard_map/ppermute | solution.py:99
  3.7 1.6 %copy-start = (bf16[4,1,512,512]{3,2,1,0:T(8,128)(2,1)S(1)}, bf16[4,1,512,512]{3,2,1,0:T(8,128)(2,1)}, u32[]{:S(2)}) copy-start(bf16[4,1,512,512]{3,2,1,0:T(8,128)(2,1)} %refs_2_.3) | copy-start | bytes 6291460
  5.3 1.6 %copy-start.2 = (bf16[4,1,512,512]{3,2,1,0:T(8,128)(2,1)S(1)}, bf16[4,1,512,512]{3,2,1,0:T(8,128)(2,1)}, u32[]{:S(2)}) copy-start(bf16[4,1,512,512]{3,2,1,0:T(8,128)(2,1)} %refs_3_.1) | copy-start | bytes 6291460
  6.8 1.0 %copy-start.4 = (bf16[1,512,512]{2,1,0:T(8,128)(2,1)S(1)}, bf16[1,512,512]{2,1,0:T(8,128)(2,1)}, u32[]{:S(2)}) copy-start(bf16[1,512,512]{2,1,0:T(8,128)(2,1)} %refs_2_.2) | copy-start | bytes 1572868
  7.9 0.7 %copy-start.5 = (s32[4]{0:T(128)S(1)}, s32[4]{0:T(128)}, u32[]{:S(2)}) copy-start(s32[4]{0:T(128)} %classes.3) | copy-start | bytes 52
  8.5 5.9 %copy-start.1 = (bf16[4,1,512,512]{3,2,1,0:T(8,128)(2,1)S(1)}, bf16[4,1,512,512]{3,2,1,0:T(8,128)(2,1)}, u32[]{:S(2)}) copy-start(bf16[4,1,512,512]{3,2,1,0:T(8,128)(2,1)} %refs_2_.3) | copy-start | bytes 6291460
  8.5 5.9 %copy-start.3 = (bf16[4,1,512,512]{3,2,1,0:T(8,128)(2,1)S(1)}, bf16[4,1,512,512]{3,2,1,0:T(8,128)(2,1)}, u32[]{:S(2)}) copy-start(bf16[4,1,512,512]{3,2,1,0:T(8,128)(2,1)} %refs_3_.1) | copy-start | bytes 6291460
  15.8 4.5 %collective-permute-start.4 = (bf16[128,512]{1,0:T(8,128)(2,1)S(1)}, bf16[128,512]{1,0:T(8,128)(2,1)S(1)}, u32[]{:S(2)}, u32[]{:S(2)}) collective-permute-start(bf16[128,512]{1,0:T(8,128)(2,1)S(1)} %get-tuple-element.10), channel_id=1, source_target_pairs={{0,4},{4,8},{8,12},{12,0},{1,5},{5,9},{9,13},{13,1},{2,6},{6,10},{... | collective-permute-start | bytes 393224 | tf_op jit(solution)/shard_map/ppermute | solution.py:131
  17.8 10.3 %collective-permute-start.5 = (bf16[128,512]{1,0:T(8,128)(2,1)S(1)}, bf16[128,512]{1,0:T(8,128)(2,1)S(1)}, u32[]{:S(2)}, u32[]{:S(2)}) collective-permute-start(bf16[128,512]{1,0:T(8,128)(2,1)S(1)} %get-tuple-element.11), channel_id=1, source_target_pairs={{0,8},{4,12},{8,0},{12,4},{1,9},{5,13},{9,1},{13,5},{2,10},{6,14},... | collective-permute-start | bytes 393224 | tf_op jit(solution)/shard_map/ppermute | solution.py:131
  18.9 12.3 %collective-permute-start.6 = (bf16[128,512]{1,0:T(8,128)(2,1)S(1)}, bf16[128,512]{1,0:T(8,128)(2,1)S(1)}, u32[]{:S(2)}, u32[]{:S(2)}) collective-permute-start(bf16[128,512]{1,0:T(8,128)(2,1)S(1)} %get-tuple-element.12), channel_id=1, source_target_pairs={{0,12},{4,0},{8,4},{12,8},{1,13},{5,1},{9,5},{13,9},{2,14},{6,2},{... | collective-permute-start | bytes 393224 | tf_op jit(solution)/shard_map/ppermute | solution.py:131

commit v2 on v1

--- a/solution.py
+++ b/solution.py
@@ -9,6 +9,7 @@
 
 SMEM = pl.BlockSpec(memory_space=pltpu.SMEM)
 VMEM = pl.BlockSpec(memory_space=pltpu.VMEM)
+HBM = pl.BlockSpec(memory_space=pltpu.HBM)
 
 
 def neighbour_moves(sectors, grid):
@@ -35,42 +36,86 @@
     return usable | ((kind == 4) & (own < sectors - grid))
 
 
-def add_terms(classes, rows_refs, block_refs, slots, left, right, masked, total, sectors, grid):
+def slot_of(kind, slots):
+    member = functools.reduce(jnp.logical_or, [kind == k for k in slots])
+    return member, sum(jnp.where(kind == k, place, 0) for k, place in slots.items())
+
+
+def mask_rows(block, rows):
+    row = lax.broadcasted_iota(jnp.int32, block.shape, 0)
+    return jnp.where(row < rows, block, jnp.zeros((), block.dtype))
+
+
+def add_term(left, block, right, total):
+    half = jnp.dot(left, block, preferred_element_type=jnp.float32)
+    total[...] += lax.dot_general(
+        half.astype(jnp.bfloat16), right, (((1,), (1,)), ((), ())), preferred_element_type=jnp.float32
+    )
+
+
+def near_kernel(slots, count, sectors, grid, classes_hbm, wave_hbm, left_hbm, right_hbm, *refs):
+    rows_refs, block_refs, far_rows = refs[:count], refs[count : 2 * count - 1], refs[2 * count - 1 : -8]
+    info, total, own_masked, lefts, rights, masked, classes, sems = refs[-8:]
     own = lax.axis_index("sector")
-    pad = total.shape[0]
-    row = lax.broadcasted_iota(jnp.int32, (pad, pad), 0)
-    for place, (rows_ref, block_ref) in enumerate(zip(rows_refs, block_refs)):
-        masked[place] = jnp.where(row < rows_ref[0], block_ref[0], jnp.zeros((), jnp.bfloat16))
-    for term in range(left.shape[0]):
-        kind = classes[term]
-        member = functools.reduce(jnp.logical_or, [kind == k for k in slots])
-        slot = sum(jnp.where(kind == k, place, 0) for k, place in slots.items())
-
-        @pl.when(member & usable_of(kind, own, sectors, grid))
-        def _():
-            half = jnp.dot(left[term, 0], masked[slot], preferred_element_type=jnp.float32)
-            total[...] += lax.dot_general(
-                half.astype(jnp.bfloat16),
-                right[term, 0],
-                (((1,), (1,)), ((), ())),
-                preferred_element_type=jnp.float32,
-            )
-
-
-def first_kernel(slots, count, sectors, grid, classes, *refs):
-    rows_refs, block_refs = refs[:count], refs[count : 2 * count]
-    left, right, total, masked = refs[2 * count :]
+    terms = lefts.shape[0]
+    get_classes = pltpu.make_async_copy(classes_hbm, classes, sems.at[0, terms])
+    get_wave = pltpu.make_async_copy(wave_hbm, own_masked, sems.at[1, terms])
+    get_classes.start()
+    get_wave.start()
+    copies = []
+    for term in range(terms):
+        get_left = pltpu.make_async_copy(left_hbm.at[term, 0], lefts.at[term], sems.at[0, term])
+        get_right = pltpu.make_async_copy(right_hbm.at[term, 0], rights.at[term], sems.at[1, term])
+        get_left.start()
+        get_right.start()
+        copies.append((get_left, get_right))
+    for place, block_ref in enumerate(block_refs, 1):
+        masked[place] = mask_rows(block_ref[0], rows_refs[place][0])
     total[...] = jnp.zeros_like(total)
-    add_terms(classes, rows_refs, block_refs, slots, left, right, masked, total, sectors, grid)
-
-
-def second_kernel(slots, count, sectors, grid, classes, *refs):
-    rows_refs, block_refs = refs[:count], refs[count : 2 * count]
+    for place, rows_ref in enumerate(far_rows):
+        info[terms + place] = rows_ref[0]
+    get_classes.wait()
+    for term in range(terms):
+        info[term] = classes[term]
+    get_wave.wait()
+    masked[0] = mask_rows(own_masked[0], rows_refs[0][0])
+    own_masked[0] = masked[0]
+    for term in range(terms):
+        for copy in copies[term]:
+            copy.wait()
+        member, slot = slot_of(classes[term], slots)
+
+        @pl.when(member & usable_of(classes[term], own, sectors, grid))
+        def _():
+            add_term(lefts[term], masked[slot], rights[term], total)
+
+
+def far_kernel(slots, count, sectors, grid, info, *refs):
+    even_refs, odd_refs = refs[:count], refs[count : 2 * count]
     left, right, before, kept = refs[2 * count : 2 * count + 4]
     sent = refs[2 * count + 4 : -2]
+    terms = left.shape[0]
     masked, total = refs[-2:]
+    own = lax.axis_index("sector")
+    even = lax.rem(own, 2) == 0
+    for place in range(count):
+
+        @pl.when(even)
+        def _():
+            masked[place] = mask_rows(even_refs[place][0], info[terms + place])
+
+        @pl.when(jnp.logical_not(even))
+        def _():
+            masked[place] = mask_rows(odd_refs[place][0], info[terms + place])
+
     total[...] = before[...]
-    add_terms(classes, rows_refs, block_refs, slots, left, right, masked, total, sectors, grid)
+    for term in range(terms):
+        member, slot = slot_of(info[term], slots)
+
+        @pl.when(member & usable_of(info[term], own, sectors, grid))
+        def _():
+            add_term(left[term], masked[slot], right[term], total)
+
     share = kept.shape[0]
     parts = len(sent) + 1
     me = lax.axis_index("term")
@@ -97,35 +142,48 @@
     share = pad // parts
     down, up = neighbour_moves(sectors, grid)
     send = lambda array, pairs: lax.ppermute(array, "sector", pairs)
+    parity = lambda pairs, odd: [(s, t) for s, t in pairs if s % 2 == odd]
+    even_blocks = [send(wave_blocks, parity(pairs, 0)) for pairs in up]
     down_blocks = [send(wave_blocks, pairs) for pairs in down]
-    up_blocks = [send(wave_blocks, pairs) for pairs in up]
     down_rows = [send(sector_rows, pairs) for pairs in down]
     up_rows = [send(sector_rows, pairs) for pairs in up]
     limit = pltpu.CompilerParams(vmem_limit_bytes=24 * 2**20)
 
-    first = [wave_blocks] + down_blocks
-    count = len(first)
-    total = pl.pallas_call(
-        functools.partial(first_kernel, {0: 0, 1: 1, 2: len(down)}, count, sectors, grid),
-        out_shape=jax.ShapeDtypeStruct((pad, pad), jnp.float32),
-        in_specs=[SMEM] * (1 + count) + [VMEM] * (count + 2),
-        out_specs=VMEM,
-        scratch_shapes=[pltpu.VMEM((count, pad, pad), jnp.bfloat16)],
+    in_hbm = lambda array: pltpu.with_memory_space_constraint(array, pltpu.HBM)
+    count = 1 + len(down_blocks)
+    terms = left_env.shape[0]
+    info, total, own_masked, lefts, rights = pl.pallas_call(
+        functools.partial(near_kernel, {0: 0, 1: 1, 2: len(down)}, count, sectors, grid),
+        out_shape=[
+            jax.ShapeDtypeStruct((terms + len(up),), jnp.int32),
+            jax.ShapeDtypeStruct((pad, pad), jnp.float32),
+            jax.ShapeDtypeStruct((1, pad, pad), jnp.bfloat16),
+            jax.ShapeDtypeStruct((terms, pad, pad), jnp.bfloat16),
+            jax.ShapeDtypeStruct((terms, pad, pad), jnp.bfloat16),
+        ],
+        in_specs=[HBM] * 4 + [SMEM] * count + [VMEM] * (count - 1) + [SMEM] * len(up),
+        out_specs=[SMEM] + [VMEM] * 4,
+        scratch_shapes=[
+            pltpu.VMEM((count, pad, pad), jnp.bfloat16),
+            pltpu.SMEM((terms,), jnp.int32),
+            pltpu.SemaphoreType.DMA((2, terms + 1)),
+        ],
         compiler_params=limit,
         name="near_terms",
-    )(term_class, sector_rows, *down_rows, *first, left_env, right_env)
-
-    count = len(up_blocks)
+    )(*(in_hbm(a) for a in (term_class, wave_blocks, left_env, right_env)), sector_rows, *down_rows, *down_blocks, *up_rows)
+    odd_blocks = [send(own_masked, parity(pairs, 1)) for pairs in up]
+
+    count = len(up)
     kept, *sent = pl.pallas_call(
-        functools.partial(second_kernel, {3: 0, 4: len(up) - 1}, count, sectors, grid),
+        functools.partial(far_kernel, {3: 0, 4: count - 1}, count, sectors, grid),
         out_shape=[jax.ShapeDtypeStruct((share, pad), jnp.float32)]
         + [jax.ShapeDtypeStruct((share, pad), jnp.bfloat16)] * (parts - 1),
-        in_specs=[SMEM] * (1 + count) + [VMEM] * (count + 3),
+        in_specs=[SMEM] + [VMEM] * (2 * count + 3),
         out_specs=[VMEM] * parts,
         scratch_shapes=[pltpu.VMEM((count, pad, pad), jnp.bfloat16), pltpu.VMEM((pad, pad), jnp.float32)],
         compiler_params=limit,
         name="far_terms",
-    )(term_class, *up_rows, *up_blocks, left_env, right_env, total)
+    )(info, *even_blocks, *odd_blocks, lefts, rights, total)
 
     got = [
         lax.ppermute(part, "term", [(i, (i + step) % parts) for i in range(parts)])

time: 32.4 us -> 32.6 us (level)
  the two profiles are of different devices: /device:TPU:11 before, /device:TPU:1 now
where the time goes in v2:
time: 32.6 us; the launch traced here: 32.1 us
  waiting for transfers between devices  13.1 us (40%)
  starting transfers between devices  10.7 us (33%)
  Pallas kernels  7.59 us (23%)
  between operations  0.71 us (2%)
    ppermute x5, waiting for transfers between devices, per_device(): send = lambda array, pairs: lax.ppermute(array, 'sector', pairs)  7.22 us
    ppermute x5, starting transfers between devices, per_device(): send = lambda array, pairs: lax.ppermute(array, 'sector', pairs)  6.42 us
    ppermute x3, waiting for transfers between devices, per_device(): lax.ppermute(part, 'term', [(i, (i + step) % parts) for i in range(parts)])  5.86 us
    pallas_call x1, Pallas kernels, per_device(): pl.pallas_call(functools.partial(near_kernel, {0: 0, 1: 1, 2: len(down)},...  5.36 us
    ppermute x3, starting transfers between devices, per_device(): lax.ppermute(part, 'term', [(i, (i + step) % parts) for i in range(parts)])  4.31 us
    pallas_call x1, Pallas kernels, per_device(): pl.pallas_call(functools.partial(far_kernel, {3: 0, 4: count - 1}, count,...  1.49 us
    pallas_call x1, Pallas kernels, per_device(): pl.pallas_call(last_kernel, out_shape=jax.ShapeDtypeStruct((1, share, pad...  0.74 us
  transfers between devices with their start and end apart: 8, of which 3 were waited for; matrix products, arithmetic and copies ran while one was open for 0% of the time, Pallas kernels for 17%

profile of v2, /device:TPU:1, one launch (start us, length us, event | category | flops | bytes accessed | tf_op | source)
XLA Modules:
  0.0 32.1 jit_solution(9295183190138172598)
XLA Ops:
  0.0 0.1 collective-permute-start.1
  0.1 0.5 %collective-permute-start = (s32[1]{0:T(128)}, s32[1]{0:T(128)}, u32[]{:S(2)}, u32[]{:S(2)}) collective-permute-start(s32[1]{0:T(128)} %param.6), channel_id=1, source_target_pairs={{0,1},{2,3},{1,0},{3,2},{4,5},{6,7},{5,4},{7,6},{8,9},{10,11},{9,8... | collective-permute-start | bytes 20 | tf_op jit(solution)/shard_map/ppermute | solution.py:144
  0.5 2.2 %collective-permute-start.2 = (s32[1]{0:T(128)}, s32[1]{0:T(128)}, u32[]{:S(2)}, u32[]{:S(2)}) collective-permute-start(s32[1]{0:T(128)} %param.6), channel_id=1, source_target_pairs={{0,2},{1,3},{2,0},{3,1},{4,6},{5,7},{6,4},{7,5},{8,10},{9,11},{10,... | collective-permute-start | bytes 20 | tf_op jit(solution)/shard_map/ppermute | solution.py:144
  2.7 0.7 %collective-permute-start.3 = (bf16[1,512,512]{2,1,0:T(8,128)(2,1)}, bf16[1,512,512]{2,1,0:T(8,128)(2,1)S(1)}, u32[]{:S(2)}, u32[]{:S(2)}) collective-permute-start(bf16[1,512,512]{2,1,0:T(8,128)(2,1)} %wave_hbm.1), channel_id=1, source_target_pairs={{0,2},{2,0},{4,6},{6,4},{8,10},{10,8},{12,14},{14,12},{16,18},{18,... | collective-permute-start | bytes 1572872 | tf_op jit(solution)/shard_map/ppermute | solution.py:144
  4.1 0.0 collective-permute-done.refs_1_
  4.1 0.0 collective-permute-done.2.refs_3_
  4.1 0.0 collective-permute-done.1.refs_2_
  4.1 5.4 %near_terms.1 = (s32[5]{0:T(128)S(1)}, f32[512,512]{1,0:T(8,128)S(1)}, bf16[1,512,512]{2,1,0:T(8,128)(2,1)S(1)}, bf16[4,512,512]{2,1,0:T(8,128)(2,1)S(1)}, bf16[4,512,512]{2,1,0:T(8,128)(2,1)S(1)}) custom-call(s32[4]{0:T(128)} %classes_hbm.1, bf16[1,512,512]{2,1,0:T(8,128)(2,1)} %wave_hbm.1, bf16[4,1,512,512]{3,2,1,0:T(8,128)(2,1)} %left_hbm.1, ...), custom_call_target="tpu_custom_call" | custom-call | tf_op jit(solution)/shard_map/near_terms/pallas_call | solution.py:155
  9.5 3.0 %collective-permute-start.4 = (bf16[1,512,512]{2,1,0:T(8,128)(2,1)S(1)}, bf16[1,512,512]{2,1,0:T(8,128)(2,1)S(1)}, u32[]{:S(2)}, u32[]{:S(2)}) collective-permute-start(bf16[1,512,512]{2,1,0:T(8,128)(2,1)S(1)} %get-tuple-element.15), channel_id=1, source_target_pairs={{1,3},{3,1},{5,7},{7,5},{9,11},{11,9},{13,15},{15,13},{17,19},{19,... | collective-permute-start | bytes 1572872 | tf_op jit(solution)/shard_map/ppermute | solution.py:144
  12.5 0.0 collective-permute-done.3.refs_0_
  12.5 7.2 %collective-permute-done.4.refs_1_ = bf16[1,512,512]{2,1,0:T(8,128)(2,1)S(1)} collective-permute-done((bf16[1,512,512]{2,1,0:T(8,128)(2,1)S(1)}, bf16[1,512,512]{2,1,0:T(8,128)(2,1)S(1)}, u32[]{:S(2)}, u32[]{:S(2)}) %collective-permute-start.4) | collective-permute-done | bytes 524320 | tf_op jit(solution)/shard_map/ppermute | solution.py:144
  19.7 1.5 %far_terms.1 = (f32[128,512]{1,0:T(8,128)S(1)}, bf16[128,512]{1,0:T(8,128)(2,1)S(1)}, bf16[128,512]{1,0:T(8,128)(2,1)S(1)}, bf16[128,512]{1,0:T(8,128)(2,1)S(1)}) custom-call(s32[5]{0:T(128)S(1)} %get-tuple-element.14.info, bf16[1,512,512]{2,1,0:T(8,128)(2,1)S(1)} %collective-permute-done.3.refs_0_, bf16[1,512,512]{2,1,0:T(8,128)(2,1)S(1)} %collective-permute-done.4.refs_1_, ...), custom_call_target="tpu_custom_call" | custom-call | tf_op jit(solution)/shard_map/far_terms/pallas_call | solution.py:177
  21.2 1.3 %collective-permute-start.5 = (bf16[128,512]{1,0:T(8,128)(2,1)S(1)}, bf16[128,512]{1,0:T(8,128)(2,1)S(1)}, u32[]{:S(2)}, u32[]{:S(2)}) collective-permute-start(bf16[128,512]{1,0:T(8,128)(2,1)S(1)} %get-tuple-element.20), channel_id=1, source_target_pairs={{0,4},{4,8},{8,12},{12,0},{1,5},{5,9},{9,13},{13,1},{2,6},{6,10},{... | collective-permute-start | bytes 393224 | tf_op jit(solution)/shard_map/ppermute | solution.py:189
  22.6 2.3 %collective-permute-start.6 = (bf16[128,512]{1,0:T(8,128)(2,1)S(1)}, bf16[128,512]{1,0:T(8,128)(2,1)S(1)}, u32[]{:S(2)}, u32[]{:S(2)}) collective-permute-start(bf16[128,512]{1,0:T(8,128)(2,1)S(1)} %get-tuple-element.21), channel_id=1, source_target_pairs={{0,8},{4,12},{8,0},{12,4},{1,9},{5,13},{9,1},{13,5},{2,10},{6,14},... | collective-permute-start | bytes 393224 | tf_op jit(solution)/shard_map/ppermute | solution.py:189
  24.9 0.7 %collective-permute-start.7 = (bf16[128,512]{1,0:T(8,128)(2,1)S(1)}, bf16[128,512]{1,0:T(8,128)(2,1)S(1)}, u32[]{:S(2)}, u32[]{:S(2)}) collective-permute-start(bf16[128,512]{1,0:T(8,128)(2,1)S(1)} %get-tuple-element.22), channel_id=1, source_target_pairs={{0,12},{4,0},{8,4},{12,8},{1,13},{5,1},{9,5},{13,9},{2,14},{6,2},{... | collective-permute-start | bytes 393224 | tf_op jit(solution)/shard_map/ppermute | solution.py:189
  25.5 1.9 %collective-permute-done.5.refs_0_ = bf16[128,512]{1,0:T(8,128)(2,1)S(1)} collective-permute-done((bf16[128,512]{1,0:T(8,128)(2,1)S(1)}, bf16[128,512]{1,0:T(8,128)(2,1)S(1)}, u32[]{:S(2)}, u32[]{:S(2)}) %collective-permute-start.5) | collective-permute-done | bytes 131104 | tf_op jit(solution)/shard_map/ppermute | solution.py:189
  27.4 4.0 %collective-permute-done.6.refs_1_ = bf16[128,512]{1,0:T(8,128)(2,1)S(1)} collective-permute-done((bf16[128,512]{1,0:T(8,128)(2,1)S(1)}, bf16[128,512]{1,0:T(8,128)(2,1)S(1)}, u32[]{:S(2)}, u32[]{:S(2)}) %collective-permute-start.6) | collective-permute-done | bytes 131104 | tf_op jit(solution)/shard_map/ppermute | solution.py:189
  31.4 0.0 collective-permute-done.7.refs_2_
  31.4 0.7 %sum_parts.1 = bf16[1,128,512]{2,1,0:T(8,128)(2,1)} custom-call(s32[1]{0:T(128)S(6)} %copy.6.refs_0_.rows_ref, f32[128,512]{1,0:T(8,128)S(1)} %get-tuple-element.19.kept, bf16[128,512]{1,0:T(8,128)(2,1)S(1)} %collective-permute-done.5.refs_0_, bf16[128,512]{1,0:T(8,128)(2,1)S(1)} %collective-permute-done.6.refs_1_, ...), custom_call_target="tpu_custom_call" | custom-call | tf_op jit(solution)/shard_map/sum_parts/pallas_call | solution.py:192
Async XLA Ops:
  0.0 4.1 %collective-permute-start.1 = (bf16[1,512,512]{2,1,0:T(8,128)(2,1)}, bf16[1,512,512]{2,1,0:T(8,128)(2,1)S(1)}, u32[]{:S(2)}, u32[]{:S(2)}) collective-permute-start(bf16[1,512,512]{2,1,0:T(8,128)(2,1)} %wave_hbm.1), channel_id=1, source_target_pairs={{0,1},{2,3},{1,0},{3,2},{4,5},{6,7},{5,4},{7,6},{8,9},{10,11},{9,8... | collective-permute-start | bytes 1572872 | tf_op jit(solution)/shard_map/ppermute | solution.py:144
  0.1 4.0 %collective-permute-start = (s32[1]{0:T(128)}, s32[1]{0:T(128)}, u32[]{:S(2)}, u32[]{:S(2)}) collective-permute-start(s32[1]{0:T(128)} %param.6), channel_id=1, source_target_pairs={{0,1},{2,3},{1,0},{3,2},{4,5},{6,7},{5,4},{7,6},{8,9},{10,11},{9,8... | collective-permute-start | bytes 20 | tf_op jit(solution)/shard_map/ppermute | solution.py:144
  0.5 3.6 %collective-permute-start.2 = (s32[1]{0:T(128)}, s32[1]{0:T(128)}, u32[]{:S(2)}, u32[]{:S(2)}) collective-permute-start(s32[1]{0:T(128)} %param.6), channel_id=1, source_target_pairs={{0,2},{1,3},{2,0},{3,1},{4,6},{5,7},{6,4},{7,5},{8,10},{9,11},{10,... | collective-permute-start | bytes 20 | tf_op jit(solution)/shard_map/ppermute | solution.py:144
  2.7 9.8 %collective-permute-start.3 = (bf16[1,512,512]{2,1,0:T(8,128)(2,1)}, bf16[1,512,512]{2,1,0:T(8,128)(2,1)S(1)}, u32[]{:S(2)}, u32[]{:S(2)}) collective-permute-start(bf16[1,512,512]{2,1,0:T(8,128)(2,1)} %wave_hbm.1), channel_id=1, source_target_pairs={{0,2},{2,0},{4,6},{6,4},{8,10},{10,8},{12,14},{14,12},{16,18},{18,... | collective-permute-start | bytes 1572872 | tf_op jit(solution)/shard_map/ppermute | solution.py:144
  9.5 10.2 %collective-permute-start.4 = (bf16[1,512,512]{2,1,0:T(8,128)(2,1)S(1)}, bf16[1,512,512]{2,1,0:T(8,128)(2,1)S(1)}, u32[]{:S(2)}, u32[]{:S(2)}) collective-permute-start(bf16[1,512,512]{2,1,0:T(8,128)(2,1)S(1)} %get-tuple-element.15), channel_id=1, source_target_pairs={{1,3},{3,1},{5,7},{7,5},{9,11},{11,9},{13,15},{15,13},{17,19},{19,... | collective-permute-start | bytes 1572872 | tf_op jit(solution)/shard_map/ppermute | solution.py:144
  21.2 6.2 %collective-permute-start.5 = (bf16[128,512]{1,0:T(8,128)(2,1)S(1)}, bf16[128,512]{1,0:T(8,128)(2,1)S(1)}, u32[]{:S(2)}, u32[]{:S(2)}) collective-permute-start(bf16[128,512]{1,0:T(8,128)(2,1)S(1)} %get-tuple-element.20), channel_id=1, source_target_pairs={{0,4},{4,8},{8,12},{12,0},{1,5},{5,9},{9,13},{13,1},{2,6},{6,10},{... | collective-permute-start | bytes 393224 | tf_op jit(solution)/shard_map/ppermute | solution.py:189
  22.6 8.8 %collective-permute-start.6 = (bf16[128,512]{1,0:T(8,128)(2,1)S(1)}, bf16[128,512]{1,0:T(8,128)(2,1)S(1)}, u32[]{:S(2)}, u32[]{:S(2)}) collective-permute-start(bf16[128,512]{1,0:T(8,128)(2,1)S(1)} %get-tuple-element.21), channel_id=1, source_target_pairs={{0,8},{4,12},{8,0},{12,4},{1,9},{5,13},{9,1},{13,5},{2,10},{6,14},... | collective-permute-start | bytes 393224 | tf_op jit(solution)/shard_map/ppermute | solution.py:189
  24.9 6.5 %collective-permute-start.7 = (bf16[128,512]{1,0:T(8,128)(2,1)S(1)}, bf16[128,512]{1,0:T(8,128)(2,1)S(1)}, u32[]{:S(2)}, u32[]{:S(2)}) collective-permute-start(bf16[128,512]{1,0:T(8,128)(2,1)S(1)} %get-tuple-element.22), channel_id=1, source_target_pairs={{0,12},{4,0},{8,4},{12,8},{1,13},{5,1},{9,5},{13,9},{2,14},{6,2},{... | collective-permute-start | bytes 393224 | tf_op jit(solution)/shard_map/ppermute | solution.py:189

commit v3 on v0

v3 whole, which is shorter than its diff:
```python
import functools

import jax
import jax.numpy as jnp
from jax import lax
from jax.experimental import pallas as pl
from jax.experimental.pallas import tpu as pltpu
from jax.sharding import PartitionSpec as P

SMEM = pl.BlockSpec(memory_space=pltpu.SMEM)
VMEM = pl.BlockSpec(memory_space=pltpu.VMEM)
HBM = pl.BlockSpec(memory_space=pltpu.HBM)
LIMIT = pltpu.CompilerParams(vmem_limit_bytes=24 * 2**20)


def neighbour_moves(sectors, grid):
    down_in = [(s, s + 1) for s in range(sectors - 1) if (s + 1) % grid != 0]
    down_out = [(s, s - 1) for s in range(1, sectors) if s % grid != 0]
    up_in = [(s, s + grid) for s in range(sectors - grid)]
    up_out = [(s, s - grid) for s in range(grid, sectors)]
    moves = []
    for first, second in ((down_in, down_out), (up_in, up_out)):
        targets = [t for _, t in first + second]
        if len(set(targets)) == len(targets):
            moves.append([first + second])
        else:
            moves.append([first, second])
    return moves


def usable_of(kind, own, sectors, grid):
    column = lax.rem(own, grid)
    usable = kind == 0
    usable = usable | ((kind == 1) & (column != 0))
    usable = usable | ((kind == 2) & (column != grid - 1))
    usable = usable | ((kind == 3) & (own >= grid))
    return usable | ((kind == 4) & (own < sectors - grid))


def slot_of(kind, slots):
    member = functools.reduce(jnp.logical_or, [kind == k for k in slots])
    return member, sum(jnp.where(kind == k, place, 0) for k, place in slots.items())


def shard_rows(shard, share):
    return pl.ds(pl.multiple_of(shard * share, share), share)


def add_terms(info, slots, sectors, grid, blocks, left, right, add):
    own = lax.axis_index("sector")
    for term in range(left.shape[0]):
        member, slot = slot_of(info[term], slots)
        usable = member & usable_of(info[term], own, sectors, grid)
        for place, block in enumerate(blocks):

            @pl.when(usable & (slot == place))
            def _():
                add(term, block)


def product(left, block, right):
    half = jnp.dot(left, block, preferred_element_type=jnp.float32)
    return lax.dot_general(
        half.astype(jnp.bfloat16), right, (((1,), (1,)), ((), ())), preferred_element_type=jnp.float32
    )


def mask_kernel(shared, classes_hbm, rows, wave_hbm, info, masked, first, rest, classes, sems):
    terms = classes.shape[0]
    copies = [
        pltpu.make_async_copy(wave_hbm, masked, sems.at[0]),
        pltpu.make_async_copy(classes_hbm, classes, sems.at[1]),
    ]
    for copy in copies:
        copy.start()
    for copy in copies:
        copy.wait()
    for term in range(terms):
        info[term] = classes[term]
    info[terms] = rows[0]
    row = lax.broadcasted_iota(jnp.int32, masked.shape[1:], 0)
    masked[0] = jnp.where(row < rows[0], masked[0], jnp.zeros((), jnp.bfloat16))
    odd = lax.rem(lax.axis_index("term"), 2)
    first[...] = masked[0, shard_rows(odd, shared), :]
    rest[...] = masked[0, pl.ds(2 * shared, rest.shape[0]), :]


def own_kernel(info, block, left_hbm, right_hbm, total, left, right, sems):
    copies = []
    for term in range(left.shape[0]):
        pair = (
            pltpu.make_async_copy(left_hbm.at[term, 0], left.at[term], sems.at[0, term]),
            pltpu.make_async_copy(right_hbm.at[term, 0], right.at[term], sems.at[1, term]),
        )
        for copy in pair:
            copy.start()
        copies.append(pair)
    total[...] = jnp.zeros_like(total)
    for term, pair in enumerate(copies):
        for copy in pair:
            copy.wait()

        @pl.when(info[term] == 0)
        def _():
            total[...] += product(left[term], block[0], right[term])


def near_kernel(slots, sectors, grid, info, *refs):
    blocks, (left, right, before, total) = refs[:-4], refs[-4:]
    total[...] = before[...]

    def add(term, block):
        total[...] += product(left[term], block[0], right[term])

    add_terms(info, slots, sectors, grid, blocks, left, right, add)


def far_first_kernel(slots, sectors, grid, count, info, *refs):
    firsts, swapped, rests = refs[:count], refs[count : 2 * count], refs[2 * count : 3 * count]
    left, right, before, sent, blocks, total = refs[3 * count :]
    me = lax.axis_index("term")
    odd = lax.rem(me, 2)
    partner = me + 1 - 2 * odd
    shared = firsts[0].shape[0]
    for place in range(count):
        blocks[place, shard_rows(odd, shared), :] = firsts[place][...]
        blocks[place, shard_rows(1 - odd, shared), :] = swapped[place][...]
        blocks[place, pl.ds(2 * shared, rests[place].shape[0]), :] = rests[place][...]
    passed, share = total.shape[0], total.shape[1]
    shards = [shard_rows(lax.rem(partner + 2 * (k + 1), 2 * (passed + 1)), share) for k in range(passed)]
    for k in range(passed):
        total[k] = before[shards[k], :]

    def add(term, block):
        for k in range(passed):
            total[k] += product(left[term, shards[k], :], block[...], right[term])

    add_terms(info, slots, sectors, grid, [blocks.at[place] for place in range(count)], left, right, add)
    sent[...] = total[...].astype(jnp.bfloat16)


def far_rest_kernel(slots, sectors, grid, count, info, blocks, left, right, before, sent, kept, total):
    me = lax.axis_index("term")
    partner = me + 1 - 2 * lax.rem(me, 2)
    own_shards, share = kept.shape[0], kept.shape[1]
    total[...] = before[...]

    def add(term, block):
        total[...] += product(left[term], block[...], right[term])

    add_terms(info, slots, sectors, grid, [blocks.at[place] for place in range(count)], left, right, add)
    sent[...] = total[shard_rows(partner, share), :].astype(jnp.bfloat16)
    for k in range(own_shards):
        kept[k] = total[shard_rows(lax.rem(me + 2 * k, 2 * own_shards), share), :]


def pass_kernel(kept, got, *sent):
    for k, part in enumerate(sent):
        part[...] = (kept[k + 1] + got[k].astype(jnp.float32)).astype(jnp.bfloat16)


def last_kernel(info, kept, *refs):
    got, out = refs[:-1], refs[-1]
    total = kept[0]
    for part in got:
        total = total + part[...].astype(jnp.float32)
    share = total.shape[0]
    row = lax.axis_index("term") * share + lax.broadcasted_iota(jnp.int32, total.shape, 0)
    out[0] = jnp.where(row < info[info.shape[0] - 1], total, 0.0).astype(jnp.bfloat16)


def call(kernel, name, shapes, in_specs, scratch, *args, out_specs=None):
    return pl.pallas_call(
        kernel,
        out_shape=[jax.ShapeDtypeStruct(shape, dtype) for shape, dtype in shapes],
        in_specs=in_specs,
        out_specs=out_specs or [VMEM] * len(shapes),
        scratch_shapes=scratch,
        compiler_params=LIMIT,
        name=name,
    )(*args)


def per_device(wave_blocks, sector_rows, term_class, left_env, right_env):
    pad, columns = wave_blocks.shape[1:]
    terms = term_class.shape[0]
    sectors, parts = lax.axis_size("sector"), lax.axis_size("term")
    grid = max(2, sectors // 4)
    share = pad // parts
    shared = 9 * pad // 512 * 16
    passed = parts // 2 - 1
    down, up = neighbour_moves(sectors, grid)
    near_slots, far_slots = {1: 0, 2: len(down) - 1}, {3: 0, 4: len(up) - 1}
    count = len(up)
    send = lambda array, pairs: lax.ppermute(array, "sector", pairs)
    swap = [(i, i ^ 1) for i in range(parts)]
    in_hbm = lambda array: pltpu.with_memory_space_constraint(array, pltpu.HBM)
    bf16, f32 = jnp.bfloat16, jnp.float32

    info, masked, first, rest = call(
        functools.partial(mask_kernel, shared),
        "mask",
        [((terms + 1,), jnp.int32), ((1, pad, columns), bf16), ((shared, columns), bf16), ((pad - 2 * shared, columns), bf16)],
        [HBM, SMEM, HBM],
        [pltpu.SMEM((terms,), jnp.int32), pltpu.SemaphoreType.DMA((2,))],
        in_hbm(term_class), sector_rows, in_hbm(wave_blocks),
        out_specs=[SMEM] + [VMEM] * 3,
    )
    firsts = [send(first, pairs) for pairs in up]
    near_blocks = [send(masked, pairs) for pairs in down]
    rests = [send(rest, pairs) for pairs in up]
    total, *env = call(
        own_kernel,
        "own_terms",
        [((pad, pad), f32), ((terms, pad, pad), bf16), ((terms, pad, pad), bf16)],
        [SMEM, VMEM, HBM, HBM],
        [pltpu.SemaphoreType.DMA((2, terms))],
        info, masked, in_hbm(left_env), in_hbm(right_env),
    )
    firsts, total = lax.optimization_barrier((firsts, total))
    swapped = [lax.ppermute(array, "term", swap) for array in firsts]
    (total,) = call(
        functools.partial(near_kernel, near_slots, sectors, grid),
        "near_terms",
        [((pad, pad), f32)],
        [SMEM] + [VMEM] * (len(down) + 3),
        [],
        info, *near_blocks, *env, total,
    )
    sent, blocks = call(
        functools.partial(far_first_kernel, far_slots, sectors, grid, count),
        "far_first",
        [((passed, share, pad), bf16), ((count, pad, columns), bf16)],
        [SMEM] + [VMEM] * (3 * count + 3),
        [pltpu.VMEM((passed, share, pad), f32)],
        info, *firsts, *swapped, *rests, *env, total,
    )
    got = lax.ppermute(sent, "term", swap)
    sent, kept = call(
        functools.partial(far_rest_kernel, far_slots, sectors, grid, count),
        "far_rest",
        [((share, pad), bf16), ((passed + 1, share, pad), f32)],
        [SMEM] + [VMEM] * 4,
        [pltpu.VMEM((pad, pad), f32)],
        info, blocks, *env, total,
    )
    last = [lax.ppermute(sent, "term", swap)]
    sums = call(
        pass_kernel,
        "pass_on",
        [((share, pad), bf16)] * passed,
        [VMEM] * 2,
        [],
        kept, got,
    )
    for k, part in enumerate(sums, 1):
        last.append(lax.ppermute(part, "term", [(i, (i + 2 * k) % parts) for i in range(parts)]))
    (out,) = call(
        last_kernel,
        "sum_parts",
        [((1, share, pad), bf16)],
        [SMEM] + [VMEM] * (1 + len(last)),
        [],
        info, kept, *last,
    )
    return out


def solution(mesh):
    placed = (
        P(("groups", "sector"), None, None),
        P(("groups", "sector")),
        P(("groups", "term")),
        P(("groups", "term"), "sector", None, None),
        P(("groups", "term"), "sector", None, None),
    )
    return jax.shard_map(
        per_device,
        mesh=mesh,
        in_specs=placed,
        out_specs=P(("groups", "sector"), "term", None),
        check_vma=False,
    )
```

time: 79 us -> 31.8 us (0.40)
  waiting for transfers between devices: 39.9 us -> 10.7 us
  between operations: 22 us -> 0.7 us
  starting transfers between devices: 0.04 us -> 12.3 us
  other arithmetic: 10.2 us -> 0 us
  Pallas kernels: 0 us -> 8.12 us
  matrix products: 5.16 us -> 0 us
  local copies, waits for them, and re-layouts: 1.46 us -> 0 us
    reduce_scatter x1 -> x0, waiting for transfers between devices: 27.6 us -> none  [per_device(): lax.psum_scatter(jnp.einsum('kic,kdc->id', halfway, rights, preferred_ele...]
    ppermute x0 -> x7, starting transfers between devices: none -> 12.3 us  [the longest x3 3.17 us: per_device(): send = lambda array, pairs: lax.ppermute(array, 'sector', pairs)]
    all_gather x1 -> x0, waiting for transfers between devices: 12.2 us -> none  [per_device(): whole = lax.all_gather(masked, 'sector', axis=0, tiled=True)]
    ppermute x0 -> x7, waiting for transfers between devices: none -> 10.7 us  [the longest x1 4.53 us: per_device(): lax.ppermute(part, 'term', [(i, (i + 2 * k) % parts) for i in range(parts)])]
    pallas_call x0 -> x7, Pallas kernels: none -> 8.12 us  [call(): pl.pallas_call(kernel, out_shape=[jax.ShapeDtypeStruct(shape, dtype) for...]
    dot_general x1 -> x0, matrix products: 5.16 us -> none  [per_device(): jnp.einsum('kic,kdc->id', halfway, rights, preferred_element_type=jnp.flo...]
    select_n x2 -> x0, other arithmetic: 4.62 us -> none  [the longest x1 2.64 us: per_device(): picked_list.append(jnp.where(usable, block_now, zero_block))]
    reduce_sum x1 -> x0, other arithmetic: 3.89 us -> none  [per_device(): offset_now = jnp.sum(jnp.where(class_ids == current, offset_table, 0))]
  transfers between devices with their start and end apart: 2 -> 7, of which waited for: 2 -> 6; matrix products, arithmetic and copies ran while one was open for 7% -> 0% of each run, Pallas kernels for 0% -> 14%
where the time goes in v3:
time: 31.8 us
  starting transfers between devices  12.3 us (39%)
  waiting for transfers between devices  10.7 us (34%)
  Pallas kernels  8.12 us (26%)
  between operations  0.7 us (2%)
    pallas_call x7, Pallas kernels, call(): pl.pallas_call(kernel, out_shape=[jax.ShapeDtypeStruct(shape, dtype) for...  8.12 us
    ppermute x1, waiting for transfers between devices, per_device(): lax.ppermute(part, 'term', [(i, (i + 2 * k) % parts) for i in range(parts)])  4.53 us
    ppermute x3, waiting for transfers between devices, per_device(): send = lambda array, pairs: lax.ppermute(array, 'sector', pairs)  3.41 us
    ppermute x3, starting transfers between devices, per_device(): send = lambda array, pairs: lax.ppermute(array, 'sector', pairs)  3.17 us
    ppermute x1, starting transfers between devices, per_device(): lax.ppermute(part, 'term', [(i, (i + 2 * k) % parts) for i in range(parts)])  2.88 us
    ppermute x1, starting transfers between devices, per_device(): got = lax.ppermute(sent, 'term', swap)  2.75 us
    ppermute x1, starting transfers between devices, per_device(): swapped = [lax.ppermute(array, 'term', swap) for array in firsts]  2.03 us
    ppermute x1, waiting for transfers between devices, per_device(): got = lax.ppermute(sent, 'term', swap)  1.69 us
  transfers between devices with their start and end apart: 7, of which 6 were waited for; matrix products, arithmetic and copies ran while one was open for 0% of the time, Pallas kernels for 14%

profile of v3, /device:TPU:0, one launch (start us, length us, event | category | flops | bytes accessed | tf_op | source)
XLA Modules:
  0.0 31.8 jit_solution(12698478674406076656)
XLA Ops:
  0.7 1.7 %mask.1 = (s32[5]{0:T(128)S(1)}, bf16[1,512,512]{2,1,0:T(8,128)(2,1)S(1)}, bf16[144,512]{1,0:T(8,128)(2,1)S(1)}, bf16[224,512]{1,0:T(8,128)(2,1)S(1)}) custom-call(s32[4]{0:T(128)} %classes_hbm.1, s32[1]{0:T(128)S(6)} %copy.6.rows, bf16[1,512,512]{2,1,0:T(8,128)(2,1)} %wave_hbm.1), custom_call_target="tpu_custom_call" | custom-call | tf_op jit(solution)/shard_map/mask/pallas_call | solution.py:173
  2.3 0.5 %collective-permute-start.3 = (bf16[1,512,512]{2,1,0:T(8,128)(2,1)S(1)}, bf16[1,512,512]{2,1,0:T(8,128)(2,1)S(1)}, u32[]{:S(2)}, u32[]{:S(2)}) collective-permute-start(bf16[1,512,512]{2,1,0:T(8,128)(2,1)S(1)} %get-tuple-element.20.block), channel_id=1, source_target_pairs={{0,1},{2,3},{1,0},{3,2},{4,5},{6,7},{5,4},{7,6},{8,9},{10,11},{9,8... | collective-permute-start | bytes 1572872 | tf_op jit(solution)/shard_map/ppermute | solution.py:195
  2.8 2.6 %collective-permute-start = (bf16[144,512]{1,0:T(8,128)(2,1)S(1)}, bf16[144,512]{1,0:T(8,128)(2,1)S(1)}, u32[]{:S(2)}, u32[]{:S(2)}) collective-permute-start(bf16[144,512]{1,0:T(8,128)(2,1)S(1)} %get-tuple-element.19), channel_id=1, source_target_pairs={{0,2},{1,3},{2,0},{3,1},{4,6},{5,7},{6,4},{7,5},{8,10},{9,11},{10,... | collective-permute-start | bytes 442376 | tf_op jit(solution)/shard_map/ppermute | solution.py:195
  5.4 0.1 collective-permute-start.2
  5.5 3.2 %own_terms.1 = (f32[512,512]{1,0:T(8,128)S(1)}, bf16[4,512,512]{2,1,0:T(8,128)(2,1)S(1)}, bf16[4,512,512]{2,1,0:T(8,128)(2,1)S(1)}) custom-call(s32[5]{0:T(128)S(1)} %get-tuple-element.18.info, bf16[1,512,512]{2,1,0:T(8,128)(2,1)S(1)} %get-tuple-element.20.block, bf16[4,1,512,512]{3,2,1,0:T(8,128)(2,1)} %left_hbm.1, bf16[4,1,512,512]{3,2,1,0:T(8,128)(2,1)} %right_hbm.1), custom_call_target="tpu_custom_call" | custom-call | tf_op jit(solution)/shard_map/own_terms/pallas_call | solution.py:173
  8.7 1.4 %collective-permute-done.refs_0_ = bf16[144,512]{1,0:T(8,128)(2,1)S(1)} collective-permute-done((bf16[144,512]{1,0:T(8,128)(2,1)S(1)}, bf16[144,512]{1,0:T(8,128)(2,1)S(1)}, u32[]{:S(2)}, u32[]{:S(2)}) %collective-permute-start) | collective-permute-done | bytes 147488 | tf_op jit(solution)/shard_map/ppermute | solution.py:195
  10.1 2.0 %collective-permute-start.1 = (bf16[144,512]{1,0:T(8,128)(2,1)S(1)}, bf16[144,512]{1,0:T(8,128)(2,1)S(1)}, u32[]{:S(2)}, u32[]{:S(2)}) collective-permute-start(bf16[144,512]{1,0:T(8,128)(2,1)S(1)} %collective-permute-done.refs_0_), channel_id=1, source_target_pairs={{0,4},{4,0},{8,12},{12,8},{1,5},{5,1},{9,13},{13,9},{2,6},{6,2},{1... | collective-permute-start | bytes 442376 | tf_op jit(solution)/shard_map/ppermute | solution.py:221
  12.1 0.0 collective-permute-done.3.refs_0_
  12.1 0.7 %near_terms.1.refs_5_.before = f32[512,512]{1,0:T(8,128)S(1)} custom-call(s32[5]{0:T(128)S(1)} %get-tuple-element.18.info, bf16[1,512,512]{2,1,0:T(8,128)(2,1)S(1)} %collective-permute-done.3.refs_0_, bf16[4,512,512]{2,1,0:T(8,128)(2,1)S(1)} %get-tuple-element.24.refs_1_.refs_3_.left, bf16[4,512,512]{2,1,0:T(8,128)(2,1)S(1)} %get-tuple-element.25.refs_2_.refs_4_.right, ...), custom_call_target="tpu_custom_call" | custom-call | tf_op jit(solution)/shard_map/near_terms/pallas_call | solution.py:173
  12.8 2.0 %collective-permute-done.2.refs_2_ = bf16[224,512]{1,0:T(8,128)(2,1)S(1)} collective-permute-done((bf16[224,512]{1,0:T(8,128)(2,1)S(1)}, bf16[224,512]{1,0:T(8,128)(2,1)S(1)}, u32[]{:S(2)}, u32[]{:S(2)}) %collective-permute-start.2) | collective-permute-done | bytes 229408 | tf_op jit(solution)/shard_map/ppermute | solution.py:195
  14.8 0.7 %collective-permute-done.1.refs_1_ = bf16[144,512]{1,0:T(8,128)(2,1)S(1)} collective-permute-done((bf16[144,512]{1,0:T(8,128)(2,1)S(1)}, bf16[144,512]{1,0:T(8,128)(2,1)S(1)}, u32[]{:S(2)}, u32[]{:S(2)}) %collective-permute-start.1) | collective-permute-done | bytes 147488 | tf_op jit(solution)/shard_map/ppermute | solution.py:221
  15.5 0.7 %far_first.1 = (bf16[1,128,512]{2,1,0:T(8,128)(2,1)S(1)}, bf16[1,512,512]{2,1,0:T(8,128)(2,1)S(1)}) custom-call(s32[5]{0:T(128)S(1)} %get-tuple-element.18.info, bf16[144,512]{1,0:T(8,128)(2,1)S(1)} %collective-permute-done.refs_0_, bf16[144,512]{1,0:T(8,128)(2,1)S(1)} %collective-permute-done.1.refs_1_, ...), custom_call_target="tpu_custom_call" | custom-call | tf_op jit(solution)/shard_map/far_first/pallas_call | solution.py:173
  16.1 2.8 %collective-permute-start.5 = (bf16[1,128,512]{2,1,0:T(8,128)(2,1)S(1)}, bf16[1,128,512]{2,1,0:T(8,128)(2,1)S(1)}, u32[]{:S(2)}, u32[]{:S(2)}) collective-permute-start(bf16[1,128,512]{2,1,0:T(8,128)(2,1)S(1)} %get-tuple-element.30), channel_id=1, source_target_pairs={{0,4},{4,0},{8,12},{12,8},{1,5},{5,1},{9,13},{13,9},{2,6},{6,2},{1... | collective-permute-start | bytes 393224 | tf_op jit(solution)/shard_map/ppermute | solution.py:238
  18.9 0.7 %far_rest.1 = (bf16[128,512]{1,0:T(8,128)(2,1)S(1)}, f32[2,128,512]{2,1,0:T(8,128)S(1)}) custom-call(s32[5]{0:T(128)S(1)} %get-tuple-element.18.info, bf16[1,512,512]{2,1,0:T(8,128)(2,1)S(1)} %get-tuple-element.27.blocks, bf16[4,512,512]{2,1,0:T(8,128)(2,1)S(1)} %get-tuple-element.24.refs_1_.refs_3_.left, ...), custom_call_target="tpu_custom_call" | custom-call | tf_op jit(solution)/shard_map/far_rest/pallas_call | solution.py:173
  19.6 1.5 %collective-permute-start.4 = (bf16[128,512]{1,0:T(8,128)(2,1)S(1)}, bf16[128,512]{1,0:T(8,128)(2,1)S(1)}, u32[]{:S(2)}, u32[]{:S(2)}) collective-permute-start(bf16[128,512]{1,0:T(8,128)(2,1)S(1)} %get-tuple-element.29), channel_id=1, source_target_pairs={{0,4},{4,0},{8,12},{12,8},{1,5},{5,1},{9,13},{13,9},{2,6},{6,2},{1... | collective-permute-start | bytes 393224 | tf_op jit(solution)/shard_map/ppermute | solution.py:247
  21.1 1.7 %collective-permute-done.5.got = bf16[1,128,512]{2,1,0:T(8,128)(2,1)S(1)} collective-permute-done((bf16[1,128,512]{2,1,0:T(8,128)(2,1)S(1)}, bf16[1,128,512]{2,1,0:T(8,128)(2,1)S(1)}, u32[]{:S(2)}, u32[]{:S(2)}) %collective-permute-start.5) | collective-permute-done | bytes 131104 | tf_op jit(solution)/shard_map/ppermute | solution.py:238
  22.8 2.9 %collective-permute-start.6 = (bf16[128,512]{1,0:T(8,128)(2,1)S(1)}, bf16[128,512]{1,0:T(8,128)(2,1)S(1)}, u32[]{:S(2)}, u32[]{:S(2)}) collective-permute-start(bf16[128,512]{1,0:T(8,128)(2,1)S(1)} %pass_on.1), channel_id=1, source_target_pairs={{0,8},{4,12},{8,0},{12,4},{1,9},{5,13},{9,1},{13,5},{2,10},{6,14},... | collective-permute-start | bytes 393224 | tf_op jit(solution)/shard_map/ppermute | solution.py:257
  25.7 0.4 %collective-permute-done.4.refs_0_ = bf16[128,512]{1,0:T(8,128)(2,1)S(1)} collective-permute-done((bf16[128,512]{1,0:T(8,128)(2,1)S(1)}, bf16[128,512]{1,0:T(8,128)(2,1)S(1)}, u32[]{:S(2)}, u32[]{:S(2)}) %collective-permute-start.4) | collective-permute-done | bytes 131104 | tf_op jit(solution)/shard_map/ppermute | solution.py:247
  26.0 4.5 %collective-permute-done.6.refs_1_ = bf16[128,512]{1,0:T(8,128)(2,1)S(1)} collective-permute-done((bf16[128,512]{1,0:T(8,128)(2,1)S(1)}, bf16[128,512]{1,0:T(8,128)(2,1)S(1)}, u32[]{:S(2)}, u32[]{:S(2)}) %collective-permute-start.6) | collective-permute-done | bytes 131104 | tf_op jit(solution)/shard_map/ppermute | solution.py:257
  30.6 1.3 %sum_parts.1 = bf16[1,128,512]{2,1,0:T(8,128)(2,1)} custom-call(s32[5]{0:T(128)S(1)} %get-tuple-element.18.info, f32[2,128,512]{2,1,0:T(8,128)S(1)} %get-tuple-element.28.kept, bf16[128,512]{1,0:T(8,128)(2,1)S(1)} %collective-permute-done.4.refs_0_, bf16[128,512]{1,0:T(8,128)(2,1)S(1)} %collective-permute-done.6.refs_1_), custom_call_target="tpu_custom_call" | custom-call | tf_op jit(solution)/shard_map/sum_parts/pallas_call | solution.py:173
  (1 shorter events, 0.0 us)
Async XLA Ops:
  2.3 9.8 %collective-permute-start.3 = (bf16[1,512,512]{2,1,0:T(8,128)(2,1)S(1)}, bf16[1,512,512]{2,1,0:T(8,128)(2,1)S(1)}, u32[]{:S(2)}, u32[]{:S(2)}) collective-permute-start(bf16[1,512,512]{2,1,0:T(8,128)(2,1)S(1)} %get-tuple-element.20.block), channel_id=1, source_target_pairs={{0,1},{2,3},{1,0},{3,2},{4,5},{6,7},{5,4},{7,6},{8,9},{10,11},{9,8... | collective-permute-start | bytes 1572872 | tf_op jit(solution)/shard_map/ppermute | solution.py:195
  2.8 7.3 %collective-permute-start = (bf16[144,512]{1,0:T(8,128)(2,1)S(1)}, bf16[144,512]{1,0:T(8,128)(2,1)S(1)}, u32[]{:S(2)}, u32[]{:S(2)}) collective-permute-start(bf16[144,512]{1,0:T(8,128)(2,1)S(1)} %get-tuple-element.19), channel_id=1, source_target_pairs={{0,2},{1,3},{2,0},{3,1},{4,6},{5,7},{6,4},{7,5},{8,10},{9,11},{10,... | collective-permute-start | bytes 442376 | tf_op jit(solution)/shard_map/ppermute | solution.py:195
  5.4 9.4 %collective-permute-start.2 = (bf16[224,512]{1,0:T(8,128)(2,1)S(1)}, bf16[224,512]{1,0:T(8,128)(2,1)S(1)}, u32[]{:S(2)}, u32[]{:S(2)}) collective-permute-start(bf16[224,512]{1,0:T(8,128)(2,1)S(1)} %get-tuple-element.23), channel_id=1, source_target_pairs={{0,2},{1,3},{2,0},{3,1},{4,6},{5,7},{6,4},{7,5},{8,10},{9,11},{10,... | collective-permute-start | bytes 688136 | tf_op jit(solution)/shard_map/ppermute | solution.py:195
  10.1 5.3 %collective-permute-start.1 = (bf16[144,512]{1,0:T(8,128)(2,1)S(1)}, bf16[144,512]{1,0:T(8,128)(2,1)S(1)}, u32[]{:S(2)}, u32[]{:S(2)}) collective-permute-start(bf16[144,512]{1,0:T(8,128)(2,1)S(1)} %collective-permute-done.refs_0_), channel_id=1, source_target_pairs={{0,4},{4,0},{8,12},{12,8},{1,5},{5,1},{9,13},{13,9},{2,6},{6,2},{1... | collective-permute-start | bytes 442376 | tf_op jit(solution)/shard_map/ppermute | solution.py:221
  16.1 6.6 %collective-permute-start.5 = (bf16[1,128,512]{2,1,0:T(8,128)(2,1)S(1)}, bf16[1,128,512]{2,1,0:T(8,128)(2,1)S(1)}, u32[]{:S(2)}, u32[]{:S(2)}) collective-permute-start(bf16[1,128,512]{2,1,0:T(8,128)(2,1)S(1)} %get-tuple-element.30), channel_id=1, source_target_pairs={{0,4},{4,0},{8,12},{12,8},{1,5},{5,1},{9,13},{13,9},{2,6},{6,2},{1... | collective-permute-start | bytes 393224 | tf_op jit(solution)/shard_map/ppermute | solution.py:238
  19.6 6.5 %collective-permute-start.4 = (bf16[128,512]{1,0:T(8,128)(2,1)S(1)}, bf16[128,512]{1,0:T(8,128)(2,1)S(1)}, u32[]{:S(2)}, u32[]{:S(2)}) collective-permute-start(bf16[128,512]{1,0:T(8,128)(2,1)S(1)} %get-tuple-element.29), channel_id=1, source_target_pairs={{0,4},{4,0},{8,12},{12,8},{1,5},{5,1},{9,13},{13,9},{2,6},{6,2},{1... | collective-permute-start | bytes 393224 | tf_op jit(solution)/shard_map/ppermute | solution.py:247
  22.8 7.8 %collective-permute-start.6 = (bf16[128,512]{1,0:T(8,128)(2,1)S(1)}, bf16[128,512]{1,0:T(8,128)(2,1)S(1)}, u32[]{:S(2)}, u32[]{:S(2)}) collective-permute-start(bf16[128,512]{1,0:T(8,128)(2,1)S(1)} %pass_on.1), channel_id=1, source_target_pairs={{0,8},{4,12},{8,0},{12,4},{1,9},{5,13},{9,1},{13,5},{2,10},{6,14},... | collective-permute-start | bytes 393224 | tf_op jit(solution)/shard_map/ppermute | solution.py:257

commit v4 on v3

--- a/solution.py
+++ b/solution.py
@@ -65,29 +65,31 @@
     )
 
 
-def mask_kernel(shared, classes_hbm, rows, wave_hbm, info, masked, first, rest, classes, sems):
-    terms = classes.shape[0]
+def mask_rows(block, rows, start=0):
+    row = start + lax.broadcasted_iota(jnp.int32, block.shape, 0)
+    return jnp.where(row < rows, block, jnp.zeros((), block.dtype))
+
+
+def cut_kernel(shared, wave_hbm, first, rest, sems):
+    odd = lax.rem(lax.axis_index("term"), 2)
     copies = [
-        pltpu.make_async_copy(wave_hbm, masked, sems.at[0]),
-        pltpu.make_async_copy(classes_hbm, classes, sems.at[1]),
+        pltpu.make_async_copy(wave_hbm.at[0, shard_rows(odd, shared)], first, sems.at[0]),
+        pltpu.make_async_copy(wave_hbm.at[0, pl.ds(2 * shared, rest.shape[0])], rest, sems.at[1]),
     ]
     for copy in copies:
         copy.start()
     for copy in copies:
         copy.wait()
+
+
+def own_kernel(classes_hbm, rows, wave_hbm, left_hbm, right_hbm, info, total, left, right, block, classes, sems):
+    terms = left.shape[0]
+    get_classes = pltpu.make_async_copy(classes_hbm, classes, sems.at[0, terms])
+    get_block = pltpu.make_async_copy(wave_hbm.at[0], block, sems.at[1, terms])
+    get_classes.start()
+    get_block.start()
+    copies = []
     for term in range(terms):
-        info[term] = classes[term]
-    info[terms] = rows[0]
-    row = lax.broadcasted_iota(jnp.int32, masked.shape[1:], 0)
-    masked[0] = jnp.where(row < rows[0], masked[0], jnp.zeros((), jnp.bfloat16))
-    odd = lax.rem(lax.axis_index("term"), 2)
-    first[...] = masked[0, shard_rows(odd, shared), :]
-    rest[...] = masked[0, pl.ds(2 * shared, rest.shape[0]), :]
-
-
-def own_kernel(info, block, left_hbm, right_hbm, total, left, right, sems):
-    copies = []
-    for term in range(left.shape[0]):
         pair = (
             pltpu.make_async_copy(left_hbm.at[term, 0], left.at[term], sems.at[0, term]),
             pltpu.make_async_copy(right_hbm.at[term, 0], right.at[term], sems.at[1, term]),
@@ -96,36 +98,46 @@
             copy.start()
         copies.append(pair)
     total[...] = jnp.zeros_like(total)
+    get_classes.wait()
+    for term in range(terms):
+        info[term] = classes[term]
+    get_block.wait()
+    block[...] = mask_rows(block[...], rows[0])
     for term, pair in enumerate(copies):
         for copy in pair:
             copy.wait()
 
-        @pl.when(info[term] == 0)
+        @pl.when(classes[term] == 0)
         def _():
-            total[...] += product(left[term], block[0], right[term])
-
-
-def near_kernel(slots, sectors, grid, info, *refs):
-    blocks, (left, right, before, total) = refs[:-4], refs[-4:]
+            total[...] += product(left[term], block[...], right[term])
+
+
+def near_kernel(slots, sectors, grid, count, info, *refs):
+    rows, got = refs[:count], refs[count : 2 * count]
+    left, right, before, total, blocks = refs[2 * count :]
+    for place in range(count):
+        blocks[place] = mask_rows(got[place][0], rows[place][0])
     total[...] = before[...]
 
     def add(term, block):
-        total[...] += product(left[term], block[0], right[term])
-
-    add_terms(info, slots, sectors, grid, blocks, left, right, add)
+        total[...] += product(left[term], block[...], right[term])
+
+    add_terms(info, slots, sectors, grid, [blocks.at[place] for place in range(count)], left, right, add)
 
 
 def far_first_kernel(slots, sectors, grid, count, info, *refs):
-    firsts, swapped, rests = refs[:count], refs[count : 2 * count], refs[2 * count : 3 * count]
-    left, right, before, sent, blocks, total = refs[3 * count :]
+    rows, firsts, swapped, rests = (refs[i * count : (i + 1) * count] for i in range(4))
+    left, right, before, sent, blocks, total = refs[4 * count :]
     me = lax.axis_index("term")
     odd = lax.rem(me, 2)
     partner = me + 1 - 2 * odd
     shared = firsts[0].shape[0]
     for place in range(count):
-        blocks[place, shard_rows(odd, shared), :] = firsts[place][...]
-        blocks[place, shard_rows(1 - odd, shared), :] = swapped[place][...]
-        blocks[place, pl.ds(2 * shared, rests[place].shape[0]), :] = rests[place][...]
+        pieces = ((odd * shared, firsts), ((1 - odd) * shared, swapped), (2 * shared, rests))
+        for start, refs_of in pieces:
+            piece = refs_of[place]
+            rows_at = pl.ds(pl.multiple_of(start, 16), piece.shape[0])
+            blocks[place, rows_at, :] = mask_rows(piece[...], rows[place][0], start)
     passed, share = total.shape[0], total.shape[1]
     shards = [shard_rows(lax.rem(partner + 2 * (k + 1), 2 * (passed + 1)), share) for k in range(passed)]
     for k in range(passed):
@@ -159,14 +171,14 @@
         part[...] = (kept[k + 1] + got[k].astype(jnp.float32)).astype(jnp.bfloat16)
 
 
-def last_kernel(info, kept, *refs):
+def last_kernel(rows, kept, *refs):
     got, out = refs[:-1], refs[-1]
     total = kept[0]
     for part in got:
         total = total + part[...].astype(jnp.float32)
     share = total.shape[0]
     row = lax.axis_index("term") * share + lax.broadcasted_iota(jnp.int32, total.shape, 0)
-    out[0] = jnp.where(row < info[info.shape[0] - 1], total, 0.0).astype(jnp.bfloat16)
+    out[0] = jnp.where(row < rows[0], total, 0.0).astype(jnp.bfloat16)
 
 
 def call(kernel, name, shapes, in_specs, scratch, *args, out_specs=None):
@@ -187,7 +199,7 @@
     sectors, parts = lax.axis_size("sector"), lax.axis_size("term")
     grid = max(2, sectors // 4)
     share = pad // parts
-    shared = 9 * pad // 512 * 16
+    shared = 11 * pad // 512 * 16
     passed = parts // 2 - 1
     down, up = neighbour_moves(sectors, grid)
     near_slots, far_slots = {1: 0, 2: len(down) - 1}, {3: 0, 4: len(up) - 1}
@@ -197,43 +209,46 @@
     in_hbm = lambda array: pltpu.with_memory_space_constraint(array, pltpu.HBM)
     bf16, f32 = jnp.bfloat16, jnp.float32
 
-    info, masked, first, rest = call(
-        functools.partial(mask_kernel, shared),
-        "mask",
-        [((terms + 1,), jnp.int32), ((1, pad, columns), bf16), ((shared, columns), bf16), ((pad - 2 * shared, columns), bf16)],
-        [HBM, SMEM, HBM],
-        [pltpu.SMEM((terms,), jnp.int32), pltpu.SemaphoreType.DMA((2,))],
-        in_hbm(term_class), sector_rows, in_hbm(wave_blocks),
-        out_specs=[SMEM] + [VMEM] * 3,
+    first, rest = call(
+        functools.partial(cut_kernel, shared),
+        "cut",
+        [((shared, columns), bf16), ((pad - 2 * shared, columns), bf16)],
+        [HBM],
+        [pltpu.SemaphoreType.DMA((2,))],
+        in_hbm(wave_blocks),
     )
     firsts = [send(first, pairs) for pairs in up]
-    near_blocks = [send(masked, pairs) for pairs in down]
-    rests = [send(rest, pairs) for pairs in up]
-    total, *env = call(
+    near_blocks = [send(wave_blocks, pairs) for pairs in down]
+    near_rows = [send(sector_rows, pairs) for pairs in down]
+    far_rows = [send(sector_rows, pairs) for pairs in up]
+    info, total, *env = call(
         own_kernel,
         "own_terms",
-        [((pad, pad), f32), ((terms, pad, pad), bf16), ((terms, pad, pad), bf16)],
-        [SMEM, VMEM, HBM, HBM],
-        [pltpu.SemaphoreType.DMA((2, terms))],
-        info, masked, in_hbm(left_env), in_hbm(right_env),
-    )
-    firsts, total = lax.optimization_barrier((firsts, total))
+        [((terms,), jnp.int32), ((pad, pad), f32), ((terms, pad, pad), bf16), ((terms, pad, pad), bf16)],
+        [HBM, SMEM] + [HBM] * 3,
+        [pltpu.VMEM((pad, columns), bf16), pltpu.SMEM((terms,), jnp.int32), pltpu.SemaphoreType.DMA((2, terms + 1))],
+        in_hbm(term_class), sector_rows, *(in_hbm(array) for array in (wave_blocks, left_env, right_env)),
+        out_specs=[SMEM] + [VMEM] * 3,
+    )
+    firsts, rest, total = lax.optimization_barrier((firsts, rest, total))
     swapped = [lax.ppermute(array, "term", swap) for array in firsts]
+    rests = [send(rest, pairs) for pairs in up]
+
     (total,) = call(
-        functools.partial(near_kernel, near_slots, sectors, grid),
+        functools.partial(near_kernel, near_slots, sectors, grid, len(down)),
         "near_terms",
         [((pad, pad), f32)],
-        [SMEM] + [VMEM] * (len(down) + 3),
-        [],
-        info, *near_blocks, *env, total,
+        [SMEM] * (1 + len(down)) + [VMEM] * (len(down) + 3),
+        [pltpu.VMEM((len(down), pad, columns), bf16)],
+        info, *near_rows, *near_blocks, *env, total,
     )
     sent, blocks = call(
         functools.partial(far_first_kernel, far_slots, sectors, grid, count),
         "far_first",
         [((passed, share, pad), bf16), ((count, pad, columns), bf16)],
-        [SMEM] + [VMEM] * (3 * count + 3),
+        [SMEM] * (1 + count) + [VMEM] * (3 * count + 3),
         [pltpu.VMEM((passed, share, pad), f32)],
-        info, *firsts, *swapped, *rests, *env, total,
+        info, *far_rows, *firsts, *swapped, *rests, *env, total,
     )
     got = lax.ppermute(sent, "term", swap)
     sent, kept = call(
@@ -244,7 +259,6 @@
         [pltpu.VMEM((pad, pad), f32)],
         info, blocks, *env, total,
     )
-    last = [lax.ppermute(sent, "term", swap)]
     sums = call(
         pass_kernel,
         "pass_on",
@@ -253,15 +267,19 @@
         [],
         kept, got,
     )
-    for k, part in enumerate(sums, 1):
-        last.append(lax.ppermute(part, "term", [(i, (i + 2 * k) % parts) for i in range(parts)]))
+    last = [
+        lax.ppermute(part, "term", [(i, (i + 2 * k) % parts) for i in range(parts)])
+        for k, part in enumerate(sums, 1)
+    ]
+    sent, *sums = lax.optimization_barrier((sent, *sums))
+    last.append(lax.ppermute(sent, "term", swap))
     (out,) = call(
         last_kernel,
         "sum_parts",
         [((1, share, pad), bf16)],
         [SMEM] + [VMEM] * (1 + len(last)),
         [],
-        info, kept, *last,
+        sector_rows, kept, *last,
     )
     return out
 

time: 31.8 us -> 31.9 us (level); the launches traced: 31.8 us -> 31.5 us
  Pallas kernels: 8.12 us -> 9.55 us
  starting transfers between devices: 12.3 us -> 11.4 us
  waiting for transfers between devices: 10.7 us -> 9.87 us
    ppermute x1, waiting for transfers between devices: 4.53 us -> 2.22 us  [per_device(): lax.ppermute(part, 'term', [(i, (i + 2 * k) % parts) for i in range(parts)])]
    ppermute x1, starting transfers between devices: 2.75 us -> 0.52 us  [per_device(): got = lax.ppermute(sent, 'term', swap)]
    ppermute x1, waiting for transfers between devices: 1.69 us -> 3.81 us  [per_device(): got = lax.ppermute(sent, 'term', swap)]
    ppermute x3 -> x5, starting transfers between devices: 3.17 us -> 5.04 us  [per_device(): send = lambda array, pairs: lax.ppermute(array, 'sector', pairs)]
    pallas_call x7, Pallas kernels: 8.12 us -> 9.55 us  [call(): pl.pallas_call(kernel, out_shape=[jax.ShapeDtypeStruct(shape, dtype) for...]
    ppermute x1, waiting for transfers between devices: 0.36 us -> 1.35 us  [per_device(): last.append(lax.ppermute(sent, 'term', swap))]
    ppermute x1, starting transfers between devices: 1.49 us -> 0.52 us  [per_device(): last.append(lax.ppermute(sent, 'term', swap))]
    ppermute x3 -> x5, waiting for transfers between devices: 3.41 us -> 2.49 us  [per_device(): send = lambda array, pairs: lax.ppermute(array, 'sector', pairs)]
  transfers between devices with their start and end apart: 7 -> 9, of which waited for: 6 -> 6; matrix products, arithmetic and copies ran while one was open for 0% -> 0% of each run, Pallas kernels for 14% -> 24%
where the time goes in v4:
time: 31.9 us; the launch traced here: 31.5 us
  starting transfers between devices  11.4 us (36%)
  waiting for transfers between devices  9.87 us (31%)
  Pallas kernels  9.55 us (30%)
  between operations  0.7 us (2%)
    pallas_call x7, Pallas kernels, call(): pl.pallas_call(kernel, out_shape=[jax.ShapeDtypeStruct(shape, dtype) for...  9.55 us
    ppermute x5, starting transfers between devices, per_device(): send = lambda array, pairs: lax.ppermute(array, 'sector', pairs)  5.04 us
    ppermute x1, waiting for transfers between devices, per_device(): got = lax.ppermute(sent, 'term', swap)  3.81 us
    ppermute x1, starting transfers between devices, per_device(): lax.ppermute(part, 'term', [(i, (i + 2 * k) % parts) for i in range(parts)])  3.46 us
    ppermute x5, waiting for transfers between devices, per_device(): send = lambda array, pairs: lax.ppermute(array, 'sector', pairs)  2.49 us
    ppermute x1, waiting for transfers between devices, per_device(): lax.ppermute(part, 'term', [(i, (i + 2 * k) % parts) for i in range(parts)])  2.22 us
    ppermute x1, starting transfers between devices, per_device(): swapped = [lax.ppermute(array, 'term', swap) for array in firsts]  1.83 us
    ppermute x1, waiting for transfers between devices, per_device(): last.append(lax.ppermute(sent, 'term', swap))  1.35 us
  transfers between devices with their start and end apart: 9, of which 6 were waited for; matrix products, arithmetic and copies ran while one was open for 0% of the time, Pallas kernels for 24%

profile of v4, /device:TPU:0, one launch (start us, length us, event | category | flops | bytes accessed | tf_op | source)
XLA Modules:
  0.0 31.5 jit_solution(15464696723260877707)
XLA Ops:
  0.0 0.5 %collective-permute-start.5 = (bf16[1,512,512]{2,1,0:T(8,128)(2,1)}, bf16[1,512,512]{2,1,0:T(8,128)(2,1)S(1)}, u32[]{:S(2)}, u32[]{:S(2)}) collective-permute-start(bf16[1,512,512]{2,1,0:T(8,128)(2,1)} %wave_hbm.3), channel_id=1, source_target_pairs={{0,1},{2,3},{1,0},{3,2},{4,5},{6,7},{5,4},{7,6},{8,9},{10,11},{9,8... | collective-permute-start | bytes 1572872 | tf_op jit(solution)/shard_map/ppermute | solution.py:207
  0.5 1.0 %cut.1 = (bf16[176,512]{1,0:T(8,128)(2,1)S(1)}, bf16[160,512]{1,0:T(8,128)(2,1)S(1)}) custom-call(bf16[1,512,512]{2,1,0:T(8,128)(2,1)} %wave_hbm.3), custom_call_target="tpu_custom_call" | custom-call | tf_op jit(solution)/shard_map/cut/pallas_call | solution.py:185
  1.5 2.6 %collective-permute-start.1 = (bf16[176,512]{1,0:T(8,128)(2,1)S(1)}, bf16[176,512]{1,0:T(8,128)(2,1)S(1)}, u32[]{:S(2)}, u32[]{:S(2)}) collective-permute-start(bf16[176,512]{1,0:T(8,128)(2,1)S(1)} %get-tuple-element.20), channel_id=1, source_target_pairs={{0,2},{1,3},{2,0},{3,1},{4,6},{5,7},{6,4},{7,5},{8,10},{9,11},{10,... | collective-permute-start | bytes 540680 | tf_op jit(solution)/shard_map/ppermute | solution.py:207
  4.7 3.8 %own_terms.1 = (s32[4]{0:T(128)S(1)}, f32[512,512]{1,0:T(8,128)S(1)}, bf16[4,512,512]{2,1,0:T(8,128)(2,1)S(1)}, bf16[4,512,512]{2,1,0:T(8,128)(2,1)S(1)}) custom-call(s32[4]{0:T(128)} %classes_hbm.1, s32[1]{0:T(128)S(6)} %copy.6.rows, bf16[1,512,512]{2,1,0:T(8,128)(2,1)} %wave_hbm.3, bf16[4,1,512,512]{3,2,1,0:T(8,128)(2,1)} %left_hbm.1, ...), custom_call_target="tpu_custom_call" | custom-call | tf_op jit(solution)/shard_map/own_terms/pallas_call | solution.py:185
  8.5 0.8 %collective-permute-done.1.refs_1_ = bf16[176,512]{1,0:T(8,128)(2,1)S(1)} collective-permute-done((bf16[176,512]{1,0:T(8,128)(2,1)S(1)}, bf16[176,512]{1,0:T(8,128)(2,1)S(1)}, u32[]{:S(2)}, u32[]{:S(2)}) %collective-permute-start.1) | collective-permute-done | bytes 180256 | tf_op jit(solution)/shard_map/ppermute | solution.py:207
  9.3 1.8 %collective-permute-start.2 = (bf16[176,512]{1,0:T(8,128)(2,1)S(1)}, bf16[176,512]{1,0:T(8,128)(2,1)S(1)}, u32[]{:S(2)}, u32[]{:S(2)}) collective-permute-start(bf16[176,512]{1,0:T(8,128)(2,1)S(1)} %collective-permute-done.1.refs_1_), channel_id=1, source_target_pairs={{0,4},{4,0},{8,12},{12,8},{1,5},{5,1},{9,13},{13,9},{2,6},{6,2},{1... | collective-permute-start | bytes 540680 | tf_op jit(solution)/shard_map/ppermute | solution.py:234
  11.1 1.5 %collective-permute-start.3 = (bf16[160,512]{1,0:T(8,128)(2,1)S(1)}, bf16[160,512]{1,0:T(8,128)(2,1)S(1)}, u32[]{:S(2)}, u32[]{:S(2)}) collective-permute-start(bf16[160,512]{1,0:T(8,128)(2,1)S(1)} %get-tuple-element.24), channel_id=1, source_target_pairs={{0,2},{1,3},{2,0},{3,1},{4,6},{5,7},{6,4},{7,5},{8,10},{9,11},{10,... | collective-permute-start | bytes 491528 | tf_op jit(solution)/shard_map/ppermute | solution.py:207
  12.6 0.0 collective-permute-start.4
  12.6 0.5 %collective-permute-start = (s32[1]{0:T(128)}, s32[1]{0:T(128)}, u32[]{:S(2)}, u32[]{:S(2)}) collective-permute-start(s32[1]{0:T(128)} %param.6), channel_id=1, source_target_pairs={{0,2},{1,3},{2,0},{3,1},{4,6},{5,7},{6,4},{7,5},{8,10},{9,11},{10,... | collective-permute-start | bytes 20 | tf_op jit(solution)/shard_map/ppermute | solution.py:207
  13.1 0.8 %collective-permute-done.4.refs_0_ = s32[1]{0:T(128)} collective-permute-done((s32[1]{0:T(128)}, s32[1]{0:T(128)}, u32[]{:S(2)}, u32[]{:S(2)}) %collective-permute-start.4) | collective-permute-done | bytes 36 | tf_op jit(solution)/shard_map/ppermute | solution.py:207
  14.0 0.0 collective-permute-done.5.refs_1_
  14.0 2.0 %near_terms.1.refs_6_.before = f32[512,512]{1,0:T(8,128)S(1)} custom-call(s32[4]{0:T(128)S(1)} %get-tuple-element.19.info, s32[1]{0:T(128)} %collective-permute-done.4.refs_0_, bf16[1,512,512]{2,1,0:T(8,128)(2,1)S(1)} %collective-permute-done.5.refs_1_, bf16[4,512,512]{2,1,0:T(8,128)(2,1)S(1)} %get-tuple-element.25.refs_2_.refs_4_.left, ...), custom_call_target="tpu_custom_call" | custom-call | tf_op jit(solution)/shard_map/near_terms/pallas_call | solution.py:185
  15.9 0.9 %collective-permute-done.refs_0_ = s32[1]{0:T(128)} collective-permute-done((s32[1]{0:T(128)}, s32[1]{0:T(128)}, u32[]{:S(2)}, u32[]{:S(2)}) %collective-permute-start) | collective-permute-done | bytes 36 | tf_op jit(solution)/shard_map/ppermute | solution.py:207
  16.8 0.0 collective-permute-done.3.refs_3_
  16.8 0.0 collective-permute-done.2.refs_2_
  16.8 1.3 %far_first.1 = (bf16[1,128,512]{2,1,0:T(8,128)(2,1)S(1)}, bf16[1,512,512]{2,1,0:T(8,128)(2,1)S(1)}) custom-call(s32[4]{0:T(128)S(1)} %get-tuple-element.19.info, s32[1]{0:T(128)} %collective-permute-done.refs_0_, bf16[176,512]{1,0:T(8,128)(2,1)S(1)} %collective-permute-done.1.refs_1_, bf16[176,512]{1,0:T(8,128)(2,1)S(1)} %collective-permute-done.2.refs_2_, ...), custom_call_target="tpu_custom_call" | custom-call | tf_op jit(solution)/shard_map/far_first/pallas_call | solution.py:185
  18.1 0.5 %collective-permute-start.6 = (bf16[1,128,512]{2,1,0:T(8,128)(2,1)S(1)}, bf16[1,128,512]{2,1,0:T(8,128)(2,1)S(1)}, u32[]{:S(2)}, u32[]{:S(2)}) collective-permute-start(bf16[1,128,512]{2,1,0:T(8,128)(2,1)S(1)} %get-tuple-element.30), channel_id=1, source_target_pairs={{0,4},{4,0},{8,12},{12,8},{1,5},{5,1},{9,13},{13,9},{2,6},{6,2},{1... | collective-permute-start | bytes 393224 | tf_op jit(solution)/shard_map/ppermute | solution.py:253
  18.7 0.7 %far_rest.1 = (bf16[128,512]{1,0:T(8,128)(2,1)S(1)}, f32[2,128,512]{2,1,0:T(8,128)S(1)}) custom-call(s32[4]{0:T(128)S(1)} %get-tuple-element.19.info, bf16[1,512,512]{2,1,0:T(8,128)(2,1)S(1)} %get-tuple-element.28.blocks, bf16[4,512,512]{2,1,0:T(8,128)(2,1)S(1)} %get-tuple-element.25.refs_2_.refs_4_.left, ...), custom_call_target="tpu_custom_call" | custom-call | tf_op jit(solution)/shard_map/far_rest/pallas_call | solution.py:185
  19.4 3.8 %collective-permute-done.6.got = bf16[1,128,512]{2,1,0:T(8,128)(2,1)S(1)} collective-permute-done((bf16[1,128,512]{2,1,0:T(8,128)(2,1)S(1)}, bf16[1,128,512]{2,1,0:T(8,128)(2,1)S(1)}, u32[]{:S(2)}, u32[]{:S(2)}) %collective-permute-start.6) | collective-permute-done | bytes 131104 | tf_op jit(solution)/shard_map/ppermute | solution.py:253
  23.2 0.5 %collective-permute-start.8 = (bf16[128,512]{1,0:T(8,128)(2,1)S(1)}, bf16[128,512]{1,0:T(8,128)(2,1)S(1)}, u32[]{:S(2)}, u32[]{:S(2)}) collective-permute-start(bf16[128,512]{1,0:T(8,128)(2,1)S(1)} %get-tuple-element.32), channel_id=1, source_target_pairs={{0,4},{4,0},{8,12},{12,8},{1,5},{5,1},{9,13},{13,9},{2,6},{6,2},{1... | collective-permute-start | bytes 393224 | tf_op jit(solution)/shard_map/ppermute | solution.py:275
  23.7 3.5 %collective-permute-start.7 = (bf16[128,512]{1,0:T(8,128)(2,1)S(1)}, bf16[128,512]{1,0:T(8,128)(2,1)S(1)}, u32[]{:S(2)}, u32[]{:S(2)}) collective-permute-start(bf16[128,512]{1,0:T(8,128)(2,1)S(1)} %pass_on.1), channel_id=1, source_target_pairs={{0,8},{4,12},{8,0},{12,4},{1,9},{5,13},{9,1},{13,5},{2,10},{6,14},... | collective-permute-start | bytes 393224 | tf_op jit(solution)/shard_map/ppermute | solution.py:271
  27.2 1.4 %collective-permute-done.8.refs_1_ = bf16[128,512]{1,0:T(8,128)(2,1)S(1)} collective-permute-done((bf16[128,512]{1,0:T(8,128)(2,1)S(1)}, bf16[128,512]{1,0:T(8,128)(2,1)S(1)}, u32[]{:S(2)}, u32[]{:S(2)}) %collective-permute-start.8) | collective-permute-done | bytes 131104 | tf_op jit(solution)/shard_map/ppermute | solution.py:275
  28.5 2.2 %collective-permute-done.7.refs_0_ = bf16[128,512]{1,0:T(8,128)(2,1)S(1)} collective-permute-done((bf16[128,512]{1,0:T(8,128)(2,1)S(1)}, bf16[128,512]{1,0:T(8,128)(2,1)S(1)}, u32[]{:S(2)}, u32[]{:S(2)}) %collective-permute-start.7) | collective-permute-done | bytes 131104 | tf_op jit(solution)/shard_map/ppermute | solution.py:271
  30.8 0.7 %sum_parts.1 = bf16[1,128,512]{2,1,0:T(8,128)(2,1)} custom-call(s32[1]{0:T(128)S(6)} %copy.6.rows, f32[2,128,512]{2,1,0:T(8,128)S(1)} %get-tuple-element.29.kept, bf16[128,512]{1,0:T(8,128)(2,1)S(1)} %collective-permute-done.7.refs_0_, bf16[128,512]{1,0:T(8,128)(2,1)S(1)} %collective-permute-done.8.refs_1_), custom_call_target="tpu_custom_call" | custom-call | tf_op jit(solution)/shard_map/sum_parts/pallas_call | solution.py:185
  (1 shorter events, 0.0 us)
Async XLA Ops:
  0.0 14.0 %collective-permute-start.5 = (bf16[1,512,512]{2,1,0:T(8,128)(2,1)}, bf16[1,512,512]{2,1,0:T(8,128)(2,1)S(1)}, u32[]{:S(2)}, u32[]{:S(2)}) collective-permute-start(bf16[1,512,512]{2,1,0:T(8,128)(2,1)} %wave_hbm.3), channel_id=1, source_target_pairs={{0,1},{2,3},{1,0},{3,2},{4,5},{6,7},{5,4},{7,6},{8,9},{10,11},{9,8... | collective-permute-start | bytes 1572872 | tf_op jit(solution)/shard_map/ppermute | solution.py:207
  1.5 7.8 %collective-permute-start.1 = (bf16[176,512]{1,0:T(8,128)(2,1)S(1)}, bf16[176,512]{1,0:T(8,128)(2,1)S(1)}, u32[]{:S(2)}, u32[]{:S(2)}) collective-permute-start(bf16[176,512]{1,0:T(8,128)(2,1)S(1)} %get-tuple-element.20), channel_id=1, source_target_pairs={{0,2},{1,3},{2,0},{3,1},{4,6},{5,7},{6,4},{7,5},{8,10},{9,11},{10,... | collective-permute-start | bytes 540680 | tf_op jit(solution)/shard_map/ppermute | solution.py:207
  9.3 7.6 %collective-permute-start.2 = (bf16[176,512]{1,0:T(8,128)(2,1)S(1)}, bf16[176,512]{1,0:T(8,128)(2,1)S(1)}, u32[]{:S(2)}, u32[]{:S(2)}) collective-permute-start(bf16[176,512]{1,0:T(8,128)(2,1)S(1)} %collective-permute-done.1.refs_1_), channel_id=1, source_target_pairs={{0,4},{4,0},{8,12},{12,8},{1,5},{5,1},{9,13},{13,9},{2,6},{6,2},{1... | collective-permute-start | bytes 540680 | tf_op jit(solution)/shard_map/ppermute | solution.py:234
  11.1 5.7 %collective-permute-start.3 = (bf16[160,512]{1,0:T(8,128)(2,1)S(1)}, bf16[160,512]{1,0:T(8,128)(2,1)S(1)}, u32[]{:S(2)}, u32[]{:S(2)}) collective-permute-start(bf16[160,512]{1,0:T(8,128)(2,1)S(1)} %get-tuple-element.24), channel_id=1, source_target_pairs={{0,2},{1,3},{2,0},{3,1},{4,6},{5,7},{6,4},{7,5},{8,10},{9,11},{10,... | collective-permute-start | bytes 491528 | tf_op jit(solution)/shard_map/ppermute | solution.py:207
  12.6 1.4 %collective-permute-start.4 = (s32[1]{0:T(128)}, s32[1]{0:T(128)}, u32[]{:S(2)}, u32[]{:S(2)}) collective-permute-start(s32[1]{0:T(128)} %param.6), channel_id=1, source_target_pairs={{0,1},{2,3},{1,0},{3,2},{4,5},{6,7},{5,4},{7,6},{8,9},{10,11},{9,8... | collective-permute-start | bytes 20 | tf_op jit(solution)/shard_map/ppermute | solution.py:207
  12.6 4.2 %collective-permute-start = (s32[1]{0:T(128)}, s32[1]{0:T(128)}, u32[]{:S(2)}, u32[]{:S(2)}) collective-permute-start(s32[1]{0:T(128)} %param.6), channel_id=1, source_target_pairs={{0,2},{1,3},{2,0},{3,1},{4,6},{5,7},{6,4},{7,5},{8,10},{9,11},{10,... | collective-permute-start | bytes 20 | tf_op jit(solution)/shard_map/ppermute | solution.py:207
  18.1 5.0 %collective-permute-start.6 = (bf16[1,128,512]{2,1,0:T(8,128)(2,1)S(1)}, bf16[1,128,512]{2,1,0:T(8,128)(2,1)S(1)}, u32[]{:S(2)}, u32[]{:S(2)}) collective-permute-start(bf16[1,128,512]{2,1,0:T(8,128)(2,1)S(1)} %get-tuple-element.30), channel_id=1, source_target_pairs={{0,4},{4,0},{8,12},{12,8},{1,5},{5,1},{9,13},{13,9},{2,6},{6,2},{1... | collective-permute-start | bytes 393224 | tf_op jit(solution)/shard_map/ppermute | solution.py:253
  23.2 5.3 %collective-permute-start.8 = (bf16[128,512]{1,0:T(8,128)(2,1)S(1)}, bf16[128,512]{1,0:T(8,128)(2,1)S(1)}, u32[]{:S(2)}, u32[]{:S(2)}) collective-permute-start(bf16[128,512]{1,0:T(8,128)(2,1)S(1)} %get-tuple-element.32), channel_id=1, source_target_pairs={{0,4},{4,0},{8,12},{12,8},{1,5},{5,1},{9,13},{13,9},{2,6},{6,2},{1... | collective-permute-start | bytes 393224 | tf_op jit(solution)/shard_map/ppermute | solution.py:275
  23.7 7.0 %collective-permute-start.7 = (bf16[128,512]{1,0:T(8,128)(2,1)S(1)}, bf16[128,512]{1,0:T(8,128)(2,1)S(1)}, u32[]{:S(2)}, u32[]{:S(2)}) collective-permute-start(bf16[128,512]{1,0:T(8,128)(2,1)S(1)} %pass_on.1), channel_id=1, source_target_pairs={{0,8},{4,12},{8,0},{12,4},{1,9},{5,13},{9,1},{13,5},{2,10},{6,14},... | collective-permute-start | bytes 393224 | tf_op jit(solution)/shard_map/ppermute | solution.py:271

commit v5 on v4

--- a/solution.py
+++ b/solution.py
@@ -65,79 +65,66 @@
     )
 
 
-def mask_rows(block, rows, start=0):
-    row = start + lax.broadcasted_iota(jnp.int32, block.shape, 0)
+def mask_rows(block, rows):
+    row = lax.broadcasted_iota(jnp.int32, block.shape, 0)
     return jnp.where(row < rows, block, jnp.zeros((), block.dtype))
 
 
-def cut_kernel(shared, wave_hbm, first, rest, sems):
-    odd = lax.rem(lax.axis_index("term"), 2)
-    copies = [
-        pltpu.make_async_copy(wave_hbm.at[0, shard_rows(odd, shared)], first, sems.at[0]),
-        pltpu.make_async_copy(wave_hbm.at[0, pl.ds(2 * shared, rest.shape[0])], rest, sems.at[1]),
-    ]
+def fetch(left_hbm, right_hbm, left, right, sems):
+    copies = []
+    for term in range(left.shape[0]):
+        copies.append(pltpu.make_async_copy(left_hbm.at[term, 0], left.at[term], sems.at[0, term]))
+        copies.append(pltpu.make_async_copy(right_hbm.at[term, 0], right.at[term], sems.at[1, term]))
     for copy in copies:
         copy.start()
-    for copy in copies:
-        copy.wait()
-
-
-def own_kernel(classes_hbm, rows, wave_hbm, left_hbm, right_hbm, info, total, left, right, block, classes, sems):
+    return copies
+
+
+def bring_kernel(wave_hbm, left_hbm, right_hbm, wave, left, right, sems):
+    terms = left.shape[0]
+    get_wave = pltpu.make_async_copy(wave_hbm, wave, sems.at[0, terms])
+    get_wave.start()
+
+    @pl.when(lax.rem(lax.axis_index("sector"), 2) == 1)
+    def _():
+        for copy in fetch(left_hbm, right_hbm, left, right, sems):
+            copy.wait()
+
+    get_wave.wait()
+
+
+def near_kernel(slots, sectors, grid, count, classes_hbm, left_hbm, right_hbm, _, __, *refs):
+    rows, got = refs[:count], refs[count : 2 * count]
+    info, total, left, right, blocks, classes, sems = refs[2 * count :]
     terms = left.shape[0]
     get_classes = pltpu.make_async_copy(classes_hbm, classes, sems.at[0, terms])
-    get_block = pltpu.make_async_copy(wave_hbm.at[0], block, sems.at[1, terms])
     get_classes.start()
-    get_block.start()
-    copies = []
-    for term in range(terms):
-        pair = (
-            pltpu.make_async_copy(left_hbm.at[term, 0], left.at[term], sems.at[0, term]),
-            pltpu.make_async_copy(right_hbm.at[term, 0], right.at[term], sems.at[1, term]),
-        )
-        for copy in pair:
-            copy.start()
-        copies.append(pair)
+
+    @pl.when(lax.rem(lax.axis_index("sector"), 2) == 0)
+    def _():
+        for copy in fetch(left_hbm, right_hbm, left, right, sems):
+            copy.wait()
+
     total[...] = jnp.zeros_like(total)
+    for place in range(count):
+        blocks[place] = mask_rows(got[place][0], rows[place][0])
     get_classes.wait()
     for term in range(terms):
         info[term] = classes[term]
-    get_block.wait()
-    block[...] = mask_rows(block[...], rows[0])
-    for term, pair in enumerate(copies):
-        for copy in pair:
-            copy.wait()
-
-        @pl.when(classes[term] == 0)
-        def _():
-            total[...] += product(left[term], block[...], right[term])
-
-
-def near_kernel(slots, sectors, grid, count, info, *refs):
+
+    def add(term, block):
+        total[...] += product(left[term], block[...], right[term])
+
+    add_terms(classes, slots, sectors, grid, [blocks.at[place] for place in range(count)], left, right, add)
+
+
+def far_first_kernel(slots, sectors, grid, count, info, *refs):
     rows, got = refs[:count], refs[count : 2 * count]
-    left, right, before, total, blocks = refs[2 * count :]
+    left, right, before, sent, blocks, total = refs[2 * count :]
+    me = lax.axis_index("term")
+    partner = me + 1 - 2 * lax.rem(me, 2)
     for place in range(count):
         blocks[place] = mask_rows(got[place][0], rows[place][0])
-    total[...] = before[...]
-
-    def add(term, block):
-        total[...] += product(left[term], block[...], right[term])
-
-    add_terms(info, slots, sectors, grid, [blocks.at[place] for place in range(count)], left, right, add)
-
-
-def far_first_kernel(slots, sectors, grid, count, info, *refs):
-    rows, firsts, swapped, rests = (refs[i * count : (i + 1) * count] for i in range(4))
-    left, right, before, sent, blocks, total = refs[4 * count :]
-    me = lax.axis_index("term")
-    odd = lax.rem(me, 2)
-    partner = me + 1 - 2 * odd
-    shared = firsts[0].shape[0]
-    for place in range(count):
-        pieces = ((odd * shared, firsts), ((1 - odd) * shared, swapped), (2 * shared, rests))
-        for start, refs_of in pieces:
-            piece = refs_of[place]
-            rows_at = pl.ds(pl.multiple_of(start, 16), piece.shape[0])
-            blocks[place, rows_at, :] = mask_rows(piece[...], rows[place][0], start)
     passed, share = total.shape[0], total.shape[1]
     shards = [shard_rows(lax.rem(partner + 2 * (k + 1), 2 * (passed + 1)), share) for k in range(passed)]
     for k in range(passed):
@@ -181,13 +168,14 @@
     out[0] = jnp.where(row < rows[0], total, 0.0).astype(jnp.bfloat16)
 
 
-def call(kernel, name, shapes, in_specs, scratch, *args, out_specs=None):
+def call(kernel, name, shapes, in_specs, scratch, *args, out_specs=None, aliases=None):
     return pl.pallas_call(
         kernel,
         out_shape=[jax.ShapeDtypeStruct(shape, dtype) for shape, dtype in shapes],
         in_specs=in_specs,
         out_specs=out_specs or [VMEM] * len(shapes),
         scratch_shapes=scratch,
+        input_output_aliases=aliases or {},
         compiler_params=LIMIT,
         name=name,
     )(*args)
@@ -199,56 +187,51 @@
     sectors, parts = lax.axis_size("sector"), lax.axis_size("term")
     grid = max(2, sectors // 4)
     share = pad // parts
-    shared = 11 * pad // 512 * 16
     passed = parts // 2 - 1
     down, up = neighbour_moves(sectors, grid)
-    near_slots, far_slots = {1: 0, 2: len(down) - 1}, {3: 0, 4: len(up) - 1}
+    near_slots, far_slots = {0: 0, 1: 1, 2: len(down)}, {3: 0, 4: len(up) - 1}
     count = len(up)
     send = lambda array, pairs: lax.ppermute(array, "sector", pairs)
     swap = [(i, i ^ 1) for i in range(parts)]
     in_hbm = lambda array: pltpu.with_memory_space_constraint(array, pltpu.HBM)
     bf16, f32 = jnp.bfloat16, jnp.float32
 
-    first, rest = call(
-        functools.partial(cut_kernel, shared),
-        "cut",
-        [((shared, columns), bf16), ((pad - 2 * shared, columns), bf16)],
-        [HBM],
-        [pltpu.SemaphoreType.DMA((2,))],
-        in_hbm(wave_blocks),
-    )
-    firsts = [send(first, pairs) for pairs in up]
+    env_shape = ((terms, pad, pad), bf16)
+    env_hbm = (in_hbm(left_env), in_hbm(right_env))
     near_blocks = [send(wave_blocks, pairs) for pairs in down]
     near_rows = [send(sector_rows, pairs) for pairs in down]
+    wave, *env = call(
+        bring_kernel,
+        "bring",
+        [((1, pad, columns), bf16), env_shape, env_shape],
+        [HBM] * 3,
+        [pltpu.SemaphoreType.DMA((2, terms + 1))],
+        in_hbm(wave_blocks), *env_hbm,
+    )
+    far_blocks = [send(wave, pairs) for pairs in up]
     far_rows = [send(sector_rows, pairs) for pairs in up]
+    near_count = 1 + len(down)
     info, total, *env = call(
-        own_kernel,
-        "own_terms",
-        [((terms,), jnp.int32), ((pad, pad), f32), ((terms, pad, pad), bf16), ((terms, pad, pad), bf16)],
-        [HBM, SMEM] + [HBM] * 3,
-        [pltpu.VMEM((pad, columns), bf16), pltpu.SMEM((terms,), jnp.int32), pltpu.SemaphoreType.DMA((2, terms + 1))],
-        in_hbm(term_class), sector_rows, *(in_hbm(array) for array in (wave_blocks, left_env, right_env)),
+        functools.partial(near_kernel, near_slots, sectors, grid, near_count),
+        "near_terms",
+        [((terms,), jnp.int32), ((pad, pad), f32), env_shape, env_shape],
+        [HBM] * 3 + [VMEM] * 2 + [SMEM] * near_count + [VMEM] * near_count,
+        [
+            pltpu.VMEM((near_count, pad, columns), bf16),
+            pltpu.SMEM((terms,), jnp.int32),
+            pltpu.SemaphoreType.DMA((2, terms + 1)),
+        ],
+        in_hbm(term_class), *env_hbm, *env, sector_rows, *near_rows, wave, *near_blocks,
         out_specs=[SMEM] + [VMEM] * 3,
-    )
-    firsts, rest, total = lax.optimization_barrier((firsts, rest, total))
-    swapped = [lax.ppermute(array, "term", swap) for array in firsts]
-    rests = [send(rest, pairs) for pairs in up]
-
-    (total,) = call(
-        functools.partial(near_kernel, near_slots, sectors, grid, len(down)),
-        "near_terms",
-        [((pad, pad), f32)],
-        [SMEM] * (1 + len(down)) + [VMEM] * (len(down) + 3),
-        [pltpu.VMEM((len(down), pad, columns), bf16)],
-        info, *near_rows, *near_blocks, *env, total,
+        aliases={3: 2, 4: 3},
     )
     sent, blocks = call(
         functools.partial(far_first_kernel, far_slots, sectors, grid, count),
         "far_first",
         [((passed, share, pad), bf16), ((count, pad, columns), bf16)],
-        [SMEM] * (1 + count) + [VMEM] * (3 * count + 3),
+        [SMEM] * (1 + count) + [VMEM] * (count + 3),
         [pltpu.VMEM((passed, share, pad), f32)],
-        info, *far_rows, *firsts, *swapped, *rests, *env, total,
+        info, *far_rows, *far_blocks, *env, total,
     )
     got = lax.ppermute(sent, "term", swap)
     sent, kept = call(
@@ -259,6 +242,7 @@
         [pltpu.VMEM((pad, pad), f32)],
         info, blocks, *env, total,
     )
+    last = [lax.ppermute(sent, "term", swap)]
     sums = call(
         pass_kernel,
         "pass_on",
@@ -267,12 +251,8 @@
         [],
         kept, got,
     )
-    last = [
-        lax.ppermute(part, "term", [(i, (i + 2 * k) % parts) for i in range(parts)])
-        for k, part in enumerate(sums, 1)
-    ]
-    sent, *sums = lax.optimization_barrier((sent, *sums))
-    last.append(lax.ppermute(sent, "term", swap))
+    for k, part in enumerate(sums, 1):
+        last.append(lax.ppermute(part, "term", [(i, (i + 2 * k) % parts) for i in range(parts)]))
     (out,) = call(
         last_kernel,
         "sum_parts",

time: 31.9 us -> 35 us (1.097)
  waiting for transfers between devices: 9.87 us -> 14.1 us
  Pallas kernels: 9.55 us -> 9.01 us
  starting transfers between devices: 11.4 us -> 11 us
    ppermute x1, waiting for transfers between devices: 2.22 us -> 6.58 us  [per_device(): lax.ppermute(part, 'term', [(i, (i + 2 * k) % parts) for i in range(parts)])]
    ppermute x2 -> x1, starting transfers between devices: 2.34 us -> 0.08 us  [per_device(): last = [lax.ppermute(sent, 'term', swap)]]
    ppermute x1, starting transfers between devices: 0.52 us -> 2.49 us  [per_device(): got = lax.ppermute(sent, 'term', swap)]
    ppermute x5 -> x4, waiting for transfers between devices: 2.49 us -> 4.02 us  [per_device(): send = lambda array, pairs: lax.ppermute(array, 'sector', pairs)]
    ppermute x2 -> x1, waiting for transfers between devices: 1.36 us -> 0.01 us  [per_device(): last = [lax.ppermute(sent, 'term', swap)]]
    pallas_call x7 -> x6, Pallas kernels: 9.55 us -> 9.01 us  [call(): pl.pallas_call(kernel, out_shape=[jax.ShapeDtypeStruct(shape, dtype) for...]
    ppermute x5 -> x4, starting transfers between devices: 5.04 us -> 4.85 us  [per_device(): send = lambda array, pairs: lax.ppermute(array, 'sector', pairs)]
  transfers between devices with their start and end apart: 9 -> 7, of which waited for: 6 -> 3; matrix products, arithmetic and copies ran while one was open for 0% -> 0% of each run, Pallas kernels for 24% -> 20%
where the time goes in v5:
time: 35 us; the launch traced here: 34.8 us
  waiting for transfers between devices  14.1 us (40%)
  starting transfers between devices  11 us (31%)
  Pallas kernels  9.01 us (26%)
  between operations  0.73 us (2%)
    pallas_call x6, Pallas kernels, call(): pl.pallas_call(kernel, out_shape=[jax.ShapeDtypeStruct(shape, dtype) for...  9.01 us
    ppermute x1, waiting for transfers between devices, per_device(): lax.ppermute(part, 'term', [(i, (i + 2 * k) % parts) for i in range(parts)])  6.58 us
    ppermute x4, starting transfers between devices, per_device(): send = lambda array, pairs: lax.ppermute(array, 'sector', pairs)  4.85 us
    ppermute x4, waiting for transfers between devices, per_device(): send = lambda array, pairs: lax.ppermute(array, 'sector', pairs)  4.02 us
    ppermute x1, starting transfers between devices, per_device(): lax.ppermute(part, 'term', [(i, (i + 2 * k) % parts) for i in range(parts)])  3.54 us
    ppermute x1, waiting for transfers between devices, per_device(): got = lax.ppermute(sent, 'term', swap)  3.51 us
    ppermute x1, starting transfers between devices, per_device(): got = lax.ppermute(sent, 'term', swap)  2.49 us
  transfers between devices with their start and end apart: 7, of which 3 were waited for; matrix products, arithmetic and copies ran while one was open for 0% of the time, Pallas kernels for 20%

profile of v5, /device:TPU:0, one launch (start us, length us, event | category | flops | bytes accessed | tf_op | source)
XLA Modules:
  0.0 34.8 jit_solution(5459136746245381591)
XLA Ops:
  0.0 0.5 %collective-permute-start.1 = (bf16[1,512,512]{2,1,0:T(8,128)(2,1)}, bf16[1,512,512]{2,1,0:T(8,128)(2,1)S(1)}, u32[]{:S(2)}, u32[]{:S(2)}) collective-permute-start(bf16[1,512,512]{2,1,0:T(8,128)(2,1)} %wave_hbm.1), channel_id=1, source_target_pairs={{0,1},{2,3},{1,0},{3,2},{4,5},{6,7},{5,4},{7,6},{8,9},{10,11},{9,8... | collective-permute-start | bytes 1572872 | tf_op jit(solution)/shard_map/ppermute | solution.py:194
  0.5 1.1 %bring.1 = (bf16[1,512,512]{2,1,0:T(8,128)(2,1)S(1)}, bf16[4,512,512]{2,1,0:T(8,128)(2,1)S(1)}, bf16[4,512,512]{2,1,0:T(8,128)(2,1)S(1)}) custom-call(bf16[1,512,512]{2,1,0:T(8,128)(2,1)} %wave_hbm.1, bf16[4,1,512,512]{3,2,1,0:T(8,128)(2,1)} %left_hbm.3, bf16[4,1,512,512]{3,2,1,0:T(8,128)(2,1)} %right_hbm.3), custom_call_target="tpu_custom_call" | custom-call | tf_op jit(solution)/shard_map/bring/pallas_call | solution.py:172
  1.6 2.6 %collective-permute-start.3 = (bf16[1,512,512]{2,1,0:T(8,128)(2,1)S(1)}, bf16[1,512,512]{2,1,0:T(8,128)(2,1)S(1)}, u32[]{:S(2)}, u32[]{:S(2)}) collective-permute-start(bf16[1,512,512]{2,1,0:T(8,128)(2,1)S(1)} %get-tuple-element.18.refs_2_), channel_id=1, source_target_pairs={{0,2},{1,3},{2,0},{3,1},{4,6},{5,7},{6,4},{7,5},{8,10},{9,11},{10,... | collective-permute-start | bytes 1572872 | tf_op jit(solution)/shard_map/ppermute | solution.py:194
  4.1 1.5 %collective-permute-start = (s32[1]{0:T(128)}, s32[1]{0:T(128)}, u32[]{:S(2)}, u32[]{:S(2)}) collective-permute-start(s32[1]{0:T(128)} %param.6), channel_id=1, source_target_pairs={{0,1},{2,3},{1,0},{3,2},{4,5},{6,7},{5,4},{7,6},{8,9},{10,11},{9,8... | collective-permute-start | bytes 20 | tf_op jit(solution)/shard_map/ppermute | solution.py:194
  5.6 0.4 %collective-permute-start.2 = (s32[1]{0:T(128)}, s32[1]{0:T(128)}, u32[]{:S(2)}, u32[]{:S(2)}) collective-permute-start(s32[1]{0:T(128)} %param.6), channel_id=1, source_target_pairs={{0,2},{1,3},{2,0},{3,1},{4,6},{5,7},{6,4},{7,5},{8,10},{9,11},{10,... | collective-permute-start | bytes 20 | tf_op jit(solution)/shard_map/ppermute | solution.py:194
  6.7 0.0 collective-permute-done.refs_1_
  6.7 0.0 collective-permute-done.1.refs_3_
  6.7 5.1 %near_terms.1 = (s32[4]{0:T(128)S(1)}, f32[512,512]{1,0:T(8,128)S(1)}, bf16[4,512,512]{2,1,0:T(8,128)(2,1)S(1)}, bf16[4,512,512]{2,1,0:T(8,128)(2,1)S(1)}) custom-call(s32[4]{0:T(128)} %classes_hbm.1, bf16[4,1,512,512]{3,2,1,0:T(8,128)(2,1)} %left_hbm.3, bf16[4,1,512,512]{3,2,1,0:T(8,128)(2,1)} %right_hbm.3, ...), custom_call_target="tpu_custom_call", output_to_operand_aliasing={{2}: (3, {}), {3}: (4, {})} | custom-call | tf_op jit(solution)/shard_map/near_terms/pallas_call | solution.py:172
  11.9 4.0 %collective-permute-done.2.refs_0_ = s32[1]{0:T(128)} collective-permute-done((s32[1]{0:T(128)}, s32[1]{0:T(128)}, u32[]{:S(2)}, u32[]{:S(2)}) %collective-permute-start.2) | collective-permute-done | bytes 36 | tf_op jit(solution)/shard_map/ppermute | solution.py:194
  15.9 0.0 collective-permute-done.3.refs_1_
  15.9 1.3 %far_first.1 = (bf16[1,128,512]{2,1,0:T(8,128)(2,1)S(1)}, bf16[1,512,512]{2,1,0:T(8,128)(2,1)S(1)}) custom-call(s32[4]{0:T(128)S(1)} %get-tuple-element.19.info, s32[1]{0:T(128)} %collective-permute-done.2.refs_0_, bf16[1,512,512]{2,1,0:T(8,128)(2,1)S(1)} %collective-permute-done.3.refs_1_, bf16[4,512,512]{2,1,0:T(8,128)(2,1)S(1)} %get-tuple-element.20.refs_2_.left, ...), custom_call_target="tpu_custom_call" | custom-call | tf_op jit(solution)/shard_map/far_first/pallas_call | solution.py:172
  17.2 2.5 %collective-permute-start.5 = (bf16[1,128,512]{2,1,0:T(8,128)(2,1)S(1)}, bf16[1,128,512]{2,1,0:T(8,128)(2,1)S(1)}, u32[]{:S(2)}, u32[]{:S(2)}) collective-permute-start(bf16[1,128,512]{2,1,0:T(8,128)(2,1)S(1)} %get-tuple-element.26), channel_id=1, source_target_pairs={{0,4},{4,0},{8,12},{12,8},{1,5},{5,1},{9,13},{13,9},{2,6},{6,2},{1... | collective-permute-start | bytes 393224 | tf_op jit(solution)/shard_map/ppermute | solution.py:236
  19.6 0.7 %far_rest.1 = (bf16[128,512]{1,0:T(8,128)(2,1)S(1)}, f32[2,128,512]{2,1,0:T(8,128)S(1)}) custom-call(s32[4]{0:T(128)S(1)} %get-tuple-element.19.info, bf16[1,512,512]{2,1,0:T(8,128)(2,1)S(1)} %get-tuple-element.23.blocks, bf16[4,512,512]{2,1,0:T(8,128)(2,1)S(1)} %get-tuple-element.20.refs_2_.left, bf16[4,512,512]{2,1,0:T(8,128)(2,1)S(1)} %get-tuple-element.21.refs_3_.right, ...), custom_call_target="tpu_custom_call" | custom-call | tf_op jit(solution)/shard_map/far_rest/pallas_call | solution.py:172
  20.4 0.1 collective-permute-start.4
  20.4 3.5 %collective-permute-done.5.got = bf16[1,128,512]{2,1,0:T(8,128)(2,1)S(1)} collective-permute-done((bf16[1,128,512]{2,1,0:T(8,128)(2,1)S(1)}, bf16[1,128,512]{2,1,0:T(8,128)(2,1)S(1)}, u32[]{:S(2)}, u32[]{:S(2)}) %collective-permute-start.5) | collective-permute-done | bytes 131104 | tf_op jit(solution)/shard_map/ppermute | solution.py:236
  24.0 3.5 %collective-permute-start.6 = (bf16[128,512]{1,0:T(8,128)(2,1)S(1)}, bf16[128,512]{1,0:T(8,128)(2,1)S(1)}, u32[]{:S(2)}, u32[]{:S(2)}) collective-permute-start(bf16[128,512]{1,0:T(8,128)(2,1)S(1)} %pass_on.1), channel_id=1, source_target_pairs={{0,8},{4,12},{8,0},{12,4},{1,9},{5,13},{9,1},{13,5},{2,10},{6,14},... | collective-permute-start | bytes 393224 | tf_op jit(solution)/shard_map/ppermute | solution.py:255
  27.5 0.0 collective-permute-done.4.refs_0_
  27.5 6.6 %collective-permute-done.6.refs_1_ = bf16[128,512]{1,0:T(8,128)(2,1)S(1)} collective-permute-done((bf16[128,512]{1,0:T(8,128)(2,1)S(1)}, bf16[128,512]{1,0:T(8,128)(2,1)S(1)}, u32[]{:S(2)}, u32[]{:S(2)}) %collective-permute-start.6) | collective-permute-done | bytes 131104 | tf_op jit(solution)/shard_map/ppermute | solution.py:255
  34.1 0.7 %sum_parts.1 = bf16[1,128,512]{2,1,0:T(8,128)(2,1)} custom-call(s32[1]{0:T(128)S(6)} %copy.10.refs_0_.rows, f32[2,128,512]{2,1,0:T(8,128)S(1)} %get-tuple-element.24.kept, bf16[128,512]{1,0:T(8,128)(2,1)S(1)} %collective-permute-done.4.refs_0_, bf16[128,512]{1,0:T(8,128)(2,1)S(1)} %collective-permute-done.6.refs_1_), custom_call_target="tpu_custom_call" | custom-call | tf_op jit(solution)/shard_map/sum_parts/pallas_call | solution.py:172
  (1 shorter events, 0.0 us)
Async XLA Ops:
  0.0 6.7 %collective-permute-start.1 = (bf16[1,512,512]{2,1,0:T(8,128)(2,1)}, bf16[1,512,512]{2,1,0:T(8,128)(2,1)S(1)}, u32[]{:S(2)}, u32[]{:S(2)}) collective-permute-start(bf16[1,512,512]{2,1,0:T(8,128)(2,1)} %wave_hbm.1), channel_id=1, source_target_pairs={{0,1},{2,3},{1,0},{3,2},{4,5},{6,7},{5,4},{7,6},{8,9},{10,11},{9,8... | collective-permute-start | bytes 1572872 | tf_op jit(solution)/shard_map/ppermute | solution.py:194
  1.6 14.3 %collective-permute-start.3 = (bf16[1,512,512]{2,1,0:T(8,128)(2,1)S(1)}, bf16[1,512,512]{2,1,0:T(8,128)(2,1)S(1)}, u32[]{:S(2)}, u32[]{:S(2)}) collective-permute-start(bf16[1,512,512]{2,1,0:T(8,128)(2,1)S(1)} %get-tuple-element.18.refs_2_), channel_id=1, source_target_pairs={{0,2},{1,3},{2,0},{3,1},{4,6},{5,7},{6,4},{7,5},{8,10},{9,11},{10,... | collective-permute-start | bytes 1572872 | tf_op jit(solution)/shard_map/ppermute | solution.py:194
  4.1 2.6 %collective-permute-start = (s32[1]{0:T(128)}, s32[1]{0:T(128)}, u32[]{:S(2)}, u32[]{:S(2)}) collective-permute-start(s32[1]{0:T(128)} %param.6), channel_id=1, source_target_pairs={{0,1},{2,3},{1,0},{3,2},{4,5},{6,7},{5,4},{7,6},{8,9},{10,11},{9,8... | collective-permute-start | bytes 20 | tf_op jit(solution)/shard_map/ppermute | solution.py:194
  5.6 10.2 %collective-permute-start.2 = (s32[1]{0:T(128)}, s32[1]{0:T(128)}, u32[]{:S(2)}, u32[]{:S(2)}) collective-permute-start(s32[1]{0:T(128)} %param.6), channel_id=1, source_target_pairs={{0,2},{1,3},{2,0},{3,1},{4,6},{5,7},{6,4},{7,5},{8,10},{9,11},{10,... | collective-permute-start | bytes 20 | tf_op jit(solution)/shard_map/ppermute | solution.py:194
  17.2 6.8 %collective-permute-start.5 = (bf16[1,128,512]{2,1,0:T(8,128)(2,1)S(1)}, bf16[1,128,512]{2,1,0:T(8,128)(2,1)S(1)}, u32[]{:S(2)}, u32[]{:S(2)}) collective-permute-start(bf16[1,128,512]{2,1,0:T(8,128)(2,1)S(1)} %get-tuple-element.26), channel_id=1, source_target_pairs={{0,4},{4,0},{8,12},{12,8},{1,5},{5,1},{9,13},{13,9},{2,6},{6,2},{1... | collective-permute-start | bytes 393224 | tf_op jit(solution)/shard_map/ppermute | solution.py:236
  20.4 7.2 %collective-permute-start.4 = (bf16[128,512]{1,0:T(8,128)(2,1)S(1)}, bf16[128,512]{1,0:T(8,128)(2,1)S(1)}, u32[]{:S(2)}, u32[]{:S(2)}) collective-permute-start(bf16[128,512]{1,0:T(8,128)(2,1)S(1)} %get-tuple-element.25), channel_id=1, source_target_pairs={{0,4},{4,0},{8,12},{12,8},{1,5},{5,1},{9,13},{13,9},{2,6},{6,2},{1... | collective-permute-start | bytes 393224 | tf_op jit(solution)/shard_map/ppermute | solution.py:245
  24.0 10.1 %collective-permute-start.6 = (bf16[128,512]{1,0:T(8,128)(2,1)S(1)}, bf16[128,512]{1,0:T(8,128)(2,1)S(1)}, u32[]{:S(2)}, u32[]{:S(2)}) collective-permute-start(bf16[128,512]{1,0:T(8,128)(2,1)S(1)} %pass_on.1), channel_id=1, source_target_pairs={{0,8},{4,12},{8,0},{12,4},{1,9},{5,13},{9,1},{13,5},{2,10},{6,14},... | collective-permute-start | bytes 393224 | tf_op jit(solution)/shard_map/ppermute | solution.py:255

commit v6 on v5

--- a/solution.py
+++ b/solution.py
@@ -70,47 +70,34 @@
     return jnp.where(row < rows, block, jnp.zeros((), block.dtype))
 
 
-def fetch(left_hbm, right_hbm, left, right, sems):
-    copies = []
-    for term in range(left.shape[0]):
-        copies.append(pltpu.make_async_copy(left_hbm.at[term, 0], left.at[term], sems.at[0, term]))
-        copies.append(pltpu.make_async_copy(right_hbm.at[term, 0], right.at[term], sems.at[1, term]))
-    for copy in copies:
-        copy.start()
-    return copies
-
-
-def bring_kernel(wave_hbm, left_hbm, right_hbm, wave, left, right, sems):
-    terms = left.shape[0]
-    get_wave = pltpu.make_async_copy(wave_hbm, wave, sems.at[0, terms])
-    get_wave.start()
-
-    @pl.when(lax.rem(lax.axis_index("sector"), 2) == 1)
-    def _():
-        for copy in fetch(left_hbm, right_hbm, left, right, sems):
-            copy.wait()
-
-    get_wave.wait()
-
-
-def near_kernel(slots, sectors, grid, count, classes_hbm, left_hbm, right_hbm, _, __, *refs):
-    rows, got = refs[:count], refs[count : 2 * count]
-    info, total, left, right, blocks, classes, sems = refs[2 * count :]
+def near_kernel(slots, sectors, grid, count, classes_hbm, wave_hbm, left_hbm, right_hbm, *refs):
+    rows, got = refs[:count], refs[count : 2 * count - 1]
+    info, total, left, right, blocks, classes, sems = refs[2 * count - 1 :]
     terms = left.shape[0]
     get_classes = pltpu.make_async_copy(classes_hbm, classes, sems.at[0, terms])
+    get_block = pltpu.make_async_copy(wave_hbm.at[0], blocks.at[0], sems.at[1, terms])
     get_classes.start()
-
-    @pl.when(lax.rem(lax.axis_index("sector"), 2) == 0)
-    def _():
-        for copy in fetch(left_hbm, right_hbm, left, right, sems):
-            copy.wait()
-
+    get_block.start()
+    copies = []
+    for term in range(terms):
+        pair = (
+            pltpu.make_async_copy(left_hbm.at[term, 0], left.at[term], sems.at[0, term]),
+            pltpu.make_async_copy(right_hbm.at[term, 0], right.at[term], sems.at[1, term]),
+        )
+        for copy in pair:
+            copy.start()
+        copies.append(pair)
     total[...] = jnp.zeros_like(total)
-    for place in range(count):
-        blocks[place] = mask_rows(got[place][0], rows[place][0])
+    for place, block in enumerate(got, 1):
+        blocks[place] = mask_rows(block[0], rows[place][0])
     get_classes.wait()
     for term in range(terms):
         info[term] = classes[term]
+    get_block.wait()
+    blocks[0] = mask_rows(blocks[0], rows[0][0])
+    for pair in copies:
+        for copy in pair:
+            copy.wait()
 
     def add(term, block):
         total[...] += product(left[term], block[...], right[term])
@@ -168,14 +155,13 @@
     out[0] = jnp.where(row < rows[0], total, 0.0).astype(jnp.bfloat16)
 
 
-def call(kernel, name, shapes, in_specs, scratch, *args, out_specs=None, aliases=None):
+def call(kernel, name, shapes, in_specs, scratch, *args, out_specs=None):
     return pl.pallas_call(
         kernel,
         out_shape=[jax.ShapeDtypeStruct(shape, dtype) for shape, dtype in shapes],
         in_specs=in_specs,
         out_specs=out_specs or [VMEM] * len(shapes),
         scratch_shapes=scratch,
-        input_output_aliases=aliases or {},
         compiler_params=LIMIT,
         name=name,
     )(*args)
@@ -196,34 +182,24 @@
     in_hbm = lambda array: pltpu.with_memory_space_constraint(array, pltpu.HBM)
     bf16, f32 = jnp.bfloat16, jnp.float32
 
+    far_blocks = [send(wave_blocks, pairs) for pairs in up]
+    near_blocks = [send(wave_blocks, pairs) for pairs in down]
+    near_rows = [sector_rows] + [send(sector_rows, pairs) for pairs in down]
+    far_rows = [send(sector_rows, pairs) for pairs in up]
+    near_count = len(near_rows)
     env_shape = ((terms, pad, pad), bf16)
-    env_hbm = (in_hbm(left_env), in_hbm(right_env))
-    near_blocks = [send(wave_blocks, pairs) for pairs in down]
-    near_rows = [send(sector_rows, pairs) for pairs in down]
-    wave, *env = call(
-        bring_kernel,
-        "bring",
-        [((1, pad, columns), bf16), env_shape, env_shape],
-        [HBM] * 3,
-        [pltpu.SemaphoreType.DMA((2, terms + 1))],
-        in_hbm(wave_blocks), *env_hbm,
-    )
-    far_blocks = [send(wave, pairs) for pairs in up]
-    far_rows = [send(sector_rows, pairs) for pairs in up]
-    near_count = 1 + len(down)
     info, total, *env = call(
         functools.partial(near_kernel, near_slots, sectors, grid, near_count),
         "near_terms",
         [((terms,), jnp.int32), ((pad, pad), f32), env_shape, env_shape],
-        [HBM] * 3 + [VMEM] * 2 + [SMEM] * near_count + [VMEM] * near_count,
+        [HBM] * 4 + [SMEM] * near_count + [VMEM] * len(down),
         [
             pltpu.VMEM((near_count, pad, columns), bf16),
             pltpu.SMEM((terms,), jnp.int32),
             pltpu.SemaphoreType.DMA((2, terms + 1)),
         ],
-        in_hbm(term_class), *env_hbm, *env, sector_rows, *near_rows, wave, *near_blocks,
+        *(in_hbm(array) for array in (term_class, wave_blocks, left_env, right_env)), *near_rows, *near_blocks,
         out_specs=[SMEM] + [VMEM] * 3,
-        aliases={3: 2, 4: 3},
     )
     sent, blocks = call(
         functools.partial(far_first_kernel, far_slots, sectors, grid, count),

time: 35 us -> 32.3 us (0.923)
  starting transfers between devices: 11 us -> 7.61 us
  waiting for transfers between devices: 14.1 us -> 15.3 us
  Pallas kernels: 9.01 us -> 8.22 us
    ppermute x4, waiting for transfers between devices: 4.02 us -> 7.43 us  [per_device(): send = lambda array, pairs: lax.ppermute(array, 'sector', pairs)]
    ppermute x1, waiting for transfers between devices: 6.58 us -> 4.39 us  [per_device(): lax.ppermute(part, 'term', [(i, (i + 2 * k) % parts) for i in range(parts)])]
    ppermute x4, starting transfers between devices: 4.85 us -> 3.45 us  [per_device(): send = lambda array, pairs: lax.ppermute(array, 'sector', pairs)]
    ppermute x1, starting transfers between devices: 2.49 us -> 1.47 us  [per_device(): got = lax.ppermute(sent, 'term', swap)]
    ppermute x1, starting transfers between devices: 3.54 us -> 2.61 us  [per_device(): lax.ppermute(part, 'term', [(i, (i + 2 * k) % parts) for i in range(parts)])]
    ppermute x1, waiting for transfers between devices: 3.51 us -> 2.64 us  [per_device(): got = lax.ppermute(sent, 'term', swap)]
    ppermute x1, waiting for transfers between devices: 0.01 us -> 0.86 us  [per_device(): last = [lax.ppermute(sent, 'term', swap)]]
    pallas_call x6 -> x5, Pallas kernels: 9.01 us -> 8.22 us  [call(): pl.pallas_call(kernel, out_shape=[jax.ShapeDtypeStruct(shape, dtype) for...]
  transfers between devices with their start and end apart: 7 -> 7, of which waited for: 3 -> 4; matrix products, arithmetic and copies ran while one was open for 0% -> 0% of each run, Pallas kernels for 20% -> 18%
where the time goes in v6:
time: 32.3 us; the launch traced here: 31.9 us
  waiting for transfers between devices  15.3 us (47%)
  Pallas kernels  8.22 us (25%)
  starting transfers between devices  7.61 us (24%)
  between operations  0.73 us (2%)
    pallas_call x5, Pallas kernels, call(): pl.pallas_call(kernel, out_shape=[jax.ShapeDtypeStruct(shape, dtype) for...  8.22 us
    ppermute x4, waiting for transfers between devices, per_device(): send = lambda array, pairs: lax.ppermute(array, 'sector', pairs)  7.43 us
    ppermute x1, waiting for transfers between devices, per_device(): lax.ppermute(part, 'term', [(i, (i + 2 * k) % parts) for i in range(parts)])  4.39 us
    ppermute x4, starting transfers between devices, per_device(): send = lambda array, pairs: lax.ppermute(array, 'sector', pairs)  3.45 us
    ppermute x1, waiting for transfers between devices, per_device(): got = lax.ppermute(sent, 'term', swap)  2.64 us
    ppermute x1, starting transfers between devices, per_device(): lax.ppermute(part, 'term', [(i, (i + 2 * k) % parts) for i in range(parts)])  2.61 us
    ppermute x1, starting transfers between devices, per_device(): got = lax.ppermute(sent, 'term', swap)  1.47 us
    ppermute x1, waiting for transfers between devices, per_device(): last = [lax.ppermute(sent, 'term', swap)]  0.86 us
  transfers between devices with their start and end apart: 7, of which 4 were waited for; matrix products, arithmetic and copies ran while one was open for 0% of the time, Pallas kernels for 18%

profile of v6, /device:TPU:0, one launch (start us, length us, event | category | flops | bytes accessed | tf_op | source)
XLA Modules:
  0.0 31.9 jit_solution(5824341644867786307)
XLA Ops:
  0.0 0.5 %collective-permute-start.1 = (bf16[1,512,512]{2,1,0:T(8,128)(2,1)}, bf16[1,512,512]{2,1,0:T(8,128)(2,1)S(1)}, u32[]{:S(2)}, u32[]{:S(2)}) collective-permute-start(bf16[1,512,512]{2,1,0:T(8,128)(2,1)} %wave_hbm.1), channel_id=1, source_target_pairs={{0,1},{2,3},{1,0},{3,2},{4,5},{6,7},{5,4},{7,6},{8,9},{10,11},{9,8... | collective-permute-start | bytes 1572872 | tf_op jit(solution)/shard_map/ppermute | solution.py:180
  0.5 2.5 %collective-permute-start.3 = (bf16[1,512,512]{2,1,0:T(8,128)(2,1)}, bf16[1,512,512]{2,1,0:T(8,128)(2,1)S(1)}, u32[]{:S(2)}, u32[]{:S(2)}) collective-permute-start(bf16[1,512,512]{2,1,0:T(8,128)(2,1)} %wave_hbm.1), channel_id=1, source_target_pairs={{0,2},{1,3},{2,0},{3,1},{4,6},{5,7},{6,4},{7,5},{8,10},{9,11},{10,... | collective-permute-start | bytes 1572872 | tf_op jit(solution)/shard_map/ppermute | solution.py:180
  2.9 0.2 collective-permute-start
  3.2 0.3 collective-permute-start.2
  4.1 0.0 collective-permute-done.refs_1_
  4.2 0.0 collective-permute-done.1.refs_2_
  4.2 4.3 %near_terms.1 = (s32[4]{0:T(128)S(1)}, f32[512,512]{1,0:T(8,128)S(1)}, bf16[4,512,512]{2,1,0:T(8,128)(2,1)S(1)}, bf16[4,512,512]{2,1,0:T(8,128)(2,1)S(1)}) custom-call(s32[4]{0:T(128)} %classes_hbm.1, bf16[1,512,512]{2,1,0:T(8,128)(2,1)} %wave_hbm.1, bf16[4,1,512,512]{3,2,1,0:T(8,128)(2,1)} %left_hbm.1, bf16[4,1,512,512]{3,2,1,0:T(8,128)(2,1)} %right_hbm.1, ...), custom_call_target="tpu_custom_call" | custom-call | tf_op jit(solution)/shard_map/near_terms/pallas_call | solution.py:159
  8.5 7.4 %collective-permute-done.2.refs_0_ = s32[1]{0:T(128)} collective-permute-done((s32[1]{0:T(128)}, s32[1]{0:T(128)}, u32[]{:S(2)}, u32[]{:S(2)}) %collective-permute-start.2) | collective-permute-done | bytes 36 | tf_op jit(solution)/shard_map/ppermute | solution.py:180
  15.9 0.0 collective-permute-done.3.refs_1_
  15.9 1.7 %far_first.1 = (bf16[1,128,512]{2,1,0:T(8,128)(2,1)S(1)}, bf16[1,512,512]{2,1,0:T(8,128)(2,1)S(1)}) custom-call(s32[4]{0:T(128)S(1)} %get-tuple-element.13.info, s32[1]{0:T(128)} %collective-permute-done.2.refs_0_, bf16[1,512,512]{2,1,0:T(8,128)(2,1)S(1)} %collective-permute-done.3.refs_1_, bf16[4,512,512]{2,1,0:T(8,128)(2,1)S(1)} %get-tuple-element.14.refs_2_.left, ...), custom_call_target="tpu_custom_call" | custom-call | tf_op jit(solution)/shard_map/far_first/pallas_call | solution.py:159
  17.7 1.5 %collective-permute-start.5 = (bf16[1,128,512]{2,1,0:T(8,128)(2,1)S(1)}, bf16[1,128,512]{2,1,0:T(8,128)(2,1)S(1)}, u32[]{:S(2)}, u32[]{:S(2)}) collective-permute-start(bf16[1,128,512]{2,1,0:T(8,128)(2,1)S(1)} %get-tuple-element.20), channel_id=1, source_target_pairs={{0,4},{4,0},{8,12},{12,8},{1,5},{5,1},{9,13},{13,9},{2,6},{6,2},{1... | collective-permute-start | bytes 393224 | tf_op jit(solution)/shard_map/ppermute | solution.py:212
  19.1 1.4 %far_rest.1 = (bf16[128,512]{1,0:T(8,128)(2,1)S(1)}, f32[2,128,512]{2,1,0:T(8,128)S(1)}) custom-call(s32[4]{0:T(128)S(1)} %get-tuple-element.13.info, bf16[1,512,512]{2,1,0:T(8,128)(2,1)S(1)} %get-tuple-element.17.blocks, bf16[4,512,512]{2,1,0:T(8,128)(2,1)S(1)} %get-tuple-element.14.refs_2_.left, bf16[4,512,512]{2,1,0:T(8,128)(2,1)S(1)} %get-tuple-element.15.refs_3_.right, ...), custom_call_target="tpu_custom_call" | custom-call | tf_op jit(solution)/shard_map/far_rest/pallas_call | solution.py:159
  20.5 0.1 collective-permute-start.4
  20.6 2.6 %collective-permute-done.5.got = bf16[1,128,512]{2,1,0:T(8,128)(2,1)S(1)} collective-permute-done((bf16[1,128,512]{2,1,0:T(8,128)(2,1)S(1)}, bf16[1,128,512]{2,1,0:T(8,128)(2,1)S(1)}, u32[]{:S(2)}, u32[]{:S(2)}) %collective-permute-start.5) | collective-permute-done | bytes 131104 | tf_op jit(solution)/shard_map/ppermute | solution.py:212
  23.3 2.6 %collective-permute-start.6 = (bf16[128,512]{1,0:T(8,128)(2,1)S(1)}, bf16[128,512]{1,0:T(8,128)(2,1)S(1)}, u32[]{:S(2)}, u32[]{:S(2)}) collective-permute-start(bf16[128,512]{1,0:T(8,128)(2,1)S(1)} %pass_on.1), channel_id=1, source_target_pairs={{0,8},{4,12},{8,0},{12,4},{1,9},{5,13},{9,1},{13,5},{2,10},{6,14},... | collective-permute-start | bytes 393224 | tf_op jit(solution)/shard_map/ppermute | solution.py:231
  25.9 0.9 %collective-permute-done.4.refs_0_ = bf16[128,512]{1,0:T(8,128)(2,1)S(1)} collective-permute-done((bf16[128,512]{1,0:T(8,128)(2,1)S(1)}, bf16[128,512]{1,0:T(8,128)(2,1)S(1)}, u32[]{:S(2)}, u32[]{:S(2)}) %collective-permute-start.4) | collective-permute-done | bytes 131104 | tf_op jit(solution)/shard_map/ppermute | solution.py:221
  26.8 4.4 %collective-permute-done.6.refs_1_ = bf16[128,512]{1,0:T(8,128)(2,1)S(1)} collective-permute-done((bf16[128,512]{1,0:T(8,128)(2,1)S(1)}, bf16[128,512]{1,0:T(8,128)(2,1)S(1)}, u32[]{:S(2)}, u32[]{:S(2)}) %collective-permute-start.6) | collective-permute-done | bytes 131104 | tf_op jit(solution)/shard_map/ppermute | solution.py:231
  31.2 0.7 %sum_parts.1 = bf16[1,128,512]{2,1,0:T(8,128)(2,1)} custom-call(s32[1]{0:T(128)S(6)} %copy.6.refs_0_.rows, f32[2,128,512]{2,1,0:T(8,128)S(1)} %get-tuple-element.18.kept, bf16[128,512]{1,0:T(8,128)(2,1)S(1)} %collective-permute-done.4.refs_0_, bf16[128,512]{1,0:T(8,128)(2,1)S(1)} %collective-permute-done.6.refs_1_), custom_call_target="tpu_custom_call" | custom-call | tf_op jit(solution)/shard_map/sum_parts/pallas_call | solution.py:159
  (1 shorter events, 0.0 us)
Async XLA Ops:
  0.0 4.2 %collective-permute-start.1 = (bf16[1,512,512]{2,1,0:T(8,128)(2,1)}, bf16[1,512,512]{2,1,0:T(8,128)(2,1)S(1)}, u32[]{:S(2)}, u32[]{:S(2)}) collective-permute-start(bf16[1,512,512]{2,1,0:T(8,128)(2,1)} %wave_hbm.1), channel_id=1, source_target_pairs={{0,1},{2,3},{1,0},{3,2},{4,5},{6,7},{5,4},{7,6},{8,9},{10,11},{9,8... | collective-permute-start | bytes 1572872 | tf_op jit(solution)/shard_map/ppermute | solution.py:180
  0.5 15.5 %collective-permute-start.3 = (bf16[1,512,512]{2,1,0:T(8,128)(2,1)}, bf16[1,512,512]{2,1,0:T(8,128)(2,1)S(1)}, u32[]{:S(2)}, u32[]{:S(2)}) collective-permute-start(bf16[1,512,512]{2,1,0:T(8,128)(2,1)} %wave_hbm.1), channel_id=1, source_target_pairs={{0,2},{1,3},{2,0},{3,1},{4,6},{5,7},{6,4},{7,5},{8,10},{9,11},{10,... | collective-permute-start | bytes 1572872 | tf_op jit(solution)/shard_map/ppermute | solution.py:180
  2.9 1.2 %collective-permute-start = (s32[1]{0:T(128)}, s32[1]{0:T(128)}, u32[]{:S(2)}, u32[]{:S(2)}) collective-permute-start(s32[1]{0:T(128)} %param.6), channel_id=1, source_target_pairs={{0,1},{2,3},{1,0},{3,2},{4,5},{6,7},{5,4},{7,6},{8,9},{10,11},{9,8... | collective-permute-start | bytes 20 | tf_op jit(solution)/shard_map/ppermute | solution.py:180
  3.2 12.7 %collective-permute-start.2 = (s32[1]{0:T(128)}, s32[1]{0:T(128)}, u32[]{:S(2)}, u32[]{:S(2)}) collective-permute-start(s32[1]{0:T(128)} %param.6), channel_id=1, source_target_pairs={{0,2},{1,3},{2,0},{3,1},{4,6},{5,7},{6,4},{7,5},{8,10},{9,11},{10,... | collective-permute-start | bytes 20 | tf_op jit(solution)/shard_map/ppermute | solution.py:180
  17.7 5.6 %collective-permute-start.5 = (bf16[1,128,512]{2,1,0:T(8,128)(2,1)S(1)}, bf16[1,128,512]{2,1,0:T(8,128)(2,1)S(1)}, u32[]{:S(2)}, u32[]{:S(2)}) collective-permute-start(bf16[1,128,512]{2,1,0:T(8,128)(2,1)S(1)} %get-tuple-element.20), channel_id=1, source_target_pairs={{0,4},{4,0},{8,12},{12,8},{1,5},{5,1},{9,13},{13,9},{2,6},{6,2},{1... | collective-permute-start | bytes 393224 | tf_op jit(solution)/shard_map/ppermute | solution.py:212
  20.5 6.2 %collective-permute-start.4 = (bf16[128,512]{1,0:T(8,128)(2,1)S(1)}, bf16[128,512]{1,0:T(8,128)(2,1)S(1)}, u32[]{:S(2)}, u32[]{:S(2)}) collective-permute-start(bf16[128,512]{1,0:T(8,128)(2,1)S(1)} %get-tuple-element.19), channel_id=1, source_target_pairs={{0,4},{4,0},{8,12},{12,8},{1,5},{5,1},{9,13},{13,9},{2,6},{6,2},{1... | collective-permute-start | bytes 393224 | tf_op jit(solution)/shard_map/ppermute | solution.py:221
  23.3 7.9 %collective-permute-start.6 = (bf16[128,512]{1,0:T(8,128)(2,1)S(1)}, bf16[128,512]{1,0:T(8,128)(2,1)S(1)}, u32[]{:S(2)}, u32[]{:S(2)}) collective-permute-start(bf16[128,512]{1,0:T(8,128)(2,1)S(1)} %pass_on.1), channel_id=1, source_target_pairs={{0,8},{4,12},{8,0},{12,4},{1,9},{5,13},{9,1},{13,5},{2,10},{6,14},... | collective-permute-start | bytes 393224 | tf_op jit(solution)/shard_map/ppermute | solution.py:231

commit v7 on v4

--- a/solution.py
+++ b/solution.py
@@ -199,7 +199,7 @@
     sectors, parts = lax.axis_size("sector"), lax.axis_size("term")
     grid = max(2, sectors // 4)
     share = pad // parts
-    shared = 11 * pad // 512 * 16
+    shared = pad // 4
     passed = parts // 2 - 1
     down, up = neighbour_moves(sectors, grid)
     near_slots, far_slots = {1: 0, 2: len(down) - 1}, {3: 0, 4: len(up) - 1}
@@ -218,6 +218,7 @@
         in_hbm(wave_blocks),
     )
     firsts = [send(first, pairs) for pairs in up]
+    rests = [send(rest, pairs) for pairs in up]
     near_blocks = [send(wave_blocks, pairs) for pairs in down]
     near_rows = [send(sector_rows, pairs) for pairs in down]
     far_rows = [send(sector_rows, pairs) for pairs in up]
@@ -230,9 +231,8 @@
         in_hbm(term_class), sector_rows, *(in_hbm(array) for array in (wave_blocks, left_env, right_env)),
         out_specs=[SMEM] + [VMEM] * 3,
     )
-    firsts, rest, total = lax.optimization_barrier((firsts, rest, total))
+    firsts, total = lax.optimization_barrier((firsts, total))
     swapped = [lax.ppermute(array, "term", swap) for array in firsts]
-    rests = [send(rest, pairs) for pairs in up]
 
     (total,) = call(
         functools.partial(near_kernel, near_slots, sectors, grid, len(down)),
@@ -259,6 +259,7 @@
         [pltpu.VMEM((pad, pad), f32)],
         info, blocks, *env, total,
     )
+    last = [lax.ppermute(sent, "term", swap)]
     sums = call(
         pass_kernel,
         "pass_on",
@@ -267,12 +268,8 @@
         [],
         kept, got,
     )
-    last = [
-        lax.ppermute(part, "term", [(i, (i + 2 * k) % parts) for i in range(parts)])
-        for k, part in enumerate(sums, 1)
-    ]
-    sent, *sums = lax.optimization_barrier((sent, *sums))
-    last.append(lax.ppermute(sent, "term", swap))
+    for k, part in enumerate(sums, 1):
+        last.append(lax.ppermute(part, "term", [(i, (i + 2 * k) % parts) for i in range(parts)]))
     (out,) = call(
         last_kernel,
         "sum_parts",

time: 31.9 us -> 30.9 us (0.969)
  waiting for transfers between devices: 9.87 us -> 6.99 us
  starting transfers between devices: 11.4 us -> 12.8 us
  Pallas kernels: 9.55 us -> 9.91 us
    ppermute x1, waiting for transfers between devices: 3.81 us -> 1.09 us  [per_device(): got = lax.ppermute(sent, 'term', swap)]
    ppermute x1, waiting for transfers between devices: 2.22 us -> 3.97 us  [per_device(): lax.ppermute(part, 'term', [(i, (i + 2 * k) % parts) for i in range(parts)])]
    ppermute x1, starting transfers between devices: 0.52 us -> 2.12 us  [per_device(): got = lax.ppermute(sent, 'term', swap)]
    ppermute x5, waiting for transfers between devices: 2.49 us -> 0.93 us  [per_device(): send = lambda array, pairs: lax.ppermute(array, 'sector', pairs)]
    ppermute x5, starting transfers between devices: 5.04 us -> 4.58 us  [per_device(): send = lambda array, pairs: lax.ppermute(array, 'sector', pairs)]
    pallas_call x7, Pallas kernels: 9.55 us -> 9.91 us  [call(): pl.pallas_call(kernel, out_shape=[jax.ShapeDtypeStruct(shape, dtype) for...]
    ppermute x1, waiting for transfers between devices: 1.35 us -> 1 us  [per_device(): last = [lax.ppermute(sent, 'term', swap)]]
  transfers between devices with their start and end apart: 9 -> 9, of which waited for: 6 -> 5; matrix products, arithmetic and copies ran while one was open for 0% -> 0% of each run, Pallas kernels for 24% -> 24%
where the time goes in v7:
time: 30.9 us; the launch traced here: 30.4 us
  starting transfers between devices  12.8 us (41%)
  Pallas kernels  9.91 us (32%)
  waiting for transfers between devices  6.99 us (23%)
  between operations  0.7 us (2%)
    pallas_call x7, Pallas kernels, call(): pl.pallas_call(kernel, out_shape=[jax.ShapeDtypeStruct(shape, dtype) for...  9.91 us
    ppermute x5, starting transfers between devices, per_device(): send = lambda array, pairs: lax.ppermute(array, 'sector', pairs)  4.58 us
    ppermute x1, waiting for transfers between devices, per_device(): lax.ppermute(part, 'term', [(i, (i + 2 * k) % parts) for i in range(parts)])  3.97 us
    ppermute x1, starting transfers between devices, per_device(): lax.ppermute(part, 'term', [(i, (i + 2 * k) % parts) for i in range(parts)])  3.31 us
    ppermute x1, starting transfers between devices, per_device(): got = lax.ppermute(sent, 'term', swap)  2.12 us
    ppermute x1, starting transfers between devices, per_device(): swapped = [lax.ppermute(array, 'term', swap) for array in firsts]  2.03 us
    ppermute x1, waiting for transfers between devices, per_device(): got = lax.ppermute(sent, 'term', swap)  1.09 us
    ppermute x1, waiting for transfers between devices, per_device(): last = [lax.ppermute(sent, 'term', swap)]  1 us
  transfers between devices with their start and end apart: 9, of which 5 were waited for; matrix products, arithmetic and copies ran while one was open for 0% of the time, Pallas kernels for 24%

profile of v7, /device:TPU:0, one launch (start us, length us, event | category | flops | bytes accessed | tf_op | source)
XLA Modules:
  0.0 30.4 jit_solution(2926284053162026539)
XLA Ops:
  0.0 0.5 %collective-permute-start.5 = (bf16[1,512,512]{2,1,0:T(8,128)(2,1)}, bf16[1,512,512]{2,1,0:T(8,128)(2,1)S(1)}, u32[]{:S(2)}, u32[]{:S(2)}) collective-permute-start(bf16[1,512,512]{2,1,0:T(8,128)(2,1)} %wave_hbm.3), channel_id=1, source_target_pairs={{0,1},{2,3},{1,0},{3,2},{4,5},{6,7},{5,4},{7,6},{8,9},{10,11},{9,8... | collective-permute-start | bytes 1572872 | tf_op jit(solution)/shard_map/ppermute | solution.py:207
  0.5 1.0 %cut.1 = (bf16[128,512]{1,0:T(8,128)(2,1)S(1)}, bf16[256,512]{1,0:T(8,128)(2,1)S(1)}) custom-call(bf16[1,512,512]{2,1,0:T(8,128)(2,1)} %wave_hbm.3), custom_call_target="tpu_custom_call" | custom-call | tf_op jit(solution)/shard_map/cut/pallas_call | solution.py:185
  1.5 2.6 %collective-permute-start.1 = (bf16[128,512]{1,0:T(8,128)(2,1)S(1)}, bf16[128,512]{1,0:T(8,128)(2,1)S(1)}, u32[]{:S(2)}, u32[]{:S(2)}) collective-permute-start(bf16[128,512]{1,0:T(8,128)(2,1)S(1)} %get-tuple-element.18), channel_id=1, source_target_pairs={{0,2},{1,3},{2,0},{3,1},{4,6},{5,7},{6,4},{7,5},{8,10},{9,11},{10,... | collective-permute-start | bytes 393224 | tf_op jit(solution)/shard_map/ppermute | solution.py:207
  4.1 0.1 collective-permute-start.3
  4.8 3.0 %own_terms.1 = (s32[4]{0:T(128)S(1)}, f32[512,512]{1,0:T(8,128)S(1)}, bf16[4,512,512]{2,1,0:T(8,128)(2,1)S(1)}, bf16[4,512,512]{2,1,0:T(8,128)(2,1)S(1)}) custom-call(s32[4]{0:T(128)} %classes_hbm.1, s32[1]{0:T(128)S(6)} %copy.6.rows, bf16[1,512,512]{2,1,0:T(8,128)(2,1)} %wave_hbm.3, bf16[4,1,512,512]{3,2,1,0:T(8,128)(2,1)} %left_hbm.1, ...), custom_call_target="tpu_custom_call" | custom-call | tf_op jit(solution)/shard_map/own_terms/pallas_call | solution.py:185
  7.8 0.6 %collective-permute-done.1.refs_1_ = bf16[128,512]{1,0:T(8,128)(2,1)S(1)} collective-permute-done((bf16[128,512]{1,0:T(8,128)(2,1)S(1)}, bf16[128,512]{1,0:T(8,128)(2,1)S(1)}, u32[]{:S(2)}, u32[]{:S(2)}) %collective-permute-start.1) | collective-permute-done | bytes 131104 | tf_op jit(solution)/shard_map/ppermute | solution.py:207
  8.4 2.0 %collective-permute-start.2 = (bf16[128,512]{1,0:T(8,128)(2,1)S(1)}, bf16[128,512]{1,0:T(8,128)(2,1)S(1)}, u32[]{:S(2)}, u32[]{:S(2)}) collective-permute-start(bf16[128,512]{1,0:T(8,128)(2,1)S(1)} %collective-permute-done.1.refs_1_), channel_id=1, source_target_pairs={{0,4},{4,0},{8,12},{12,8},{1,5},{5,1},{9,13},{13,9},{2,6},{6,2},{1... | collective-permute-start | bytes 393224 | tf_op jit(solution)/shard_map/ppermute | solution.py:235
  10.4 0.0 collective-permute-start.4
  10.4 1.5 %collective-permute-start = (s32[1]{0:T(128)}, s32[1]{0:T(128)}, u32[]{:S(2)}, u32[]{:S(2)}) collective-permute-start(s32[1]{0:T(128)} %param.6), channel_id=1, source_target_pairs={{0,2},{1,3},{2,0},{3,1},{4,6},{5,7},{6,4},{7,5},{8,10},{9,11},{10,... | collective-permute-start | bytes 20 | tf_op jit(solution)/shard_map/ppermute | solution.py:207
  11.9 0.0 collective-permute-done.4.refs_0_
  11.9 0.0 collective-permute-done.5.refs_1_
  11.9 2.0 %near_terms.1.refs_6_.before = f32[512,512]{1,0:T(8,128)S(1)} custom-call(s32[4]{0:T(128)S(1)} %get-tuple-element.17.info, s32[1]{0:T(128)} %collective-permute-done.4.refs_0_, bf16[1,512,512]{2,1,0:T(8,128)(2,1)S(1)} %collective-permute-done.5.refs_1_, bf16[4,512,512]{2,1,0:T(8,128)(2,1)S(1)} %get-tuple-element.22.refs_2_.refs_4_.left, ...), custom_call_target="tpu_custom_call" | custom-call | tf_op jit(solution)/shard_map/near_terms/pallas_call | solution.py:185
  13.9 0.3 %collective-permute-done.refs_0_ = s32[1]{0:T(128)} collective-permute-done((s32[1]{0:T(128)}, s32[1]{0:T(128)}, u32[]{:S(2)}, u32[]{:S(2)}) %collective-permute-start) | collective-permute-done | bytes 36 | tf_op jit(solution)/shard_map/ppermute | solution.py:207
  14.2 0.0 collective-permute-done.2.refs_2_
  14.2 0.0 collective-permute-done.3.refs_3_
  14.2 1.8 %far_first.1 = (bf16[1,128,512]{2,1,0:T(8,128)(2,1)S(1)}, bf16[1,512,512]{2,1,0:T(8,128)(2,1)S(1)}) custom-call(s32[4]{0:T(128)S(1)} %get-tuple-element.17.info, s32[1]{0:T(128)} %collective-permute-done.refs_0_, bf16[128,512]{1,0:T(8,128)(2,1)S(1)} %collective-permute-done.1.refs_1_, bf16[128,512]{1,0:T(8,128)(2,1)S(1)} %collective-permute-done.2.refs_2_, ...), custom_call_target="tpu_custom_call" | custom-call | tf_op jit(solution)/shard_map/far_first/pallas_call | solution.py:185
  16.0 2.1 %collective-permute-start.7 = (bf16[1,128,512]{2,1,0:T(8,128)(2,1)S(1)}, bf16[1,128,512]{2,1,0:T(8,128)(2,1)S(1)}, u32[]{:S(2)}, u32[]{:S(2)}) collective-permute-start(bf16[1,128,512]{2,1,0:T(8,128)(2,1)S(1)} %get-tuple-element.28), channel_id=1, source_target_pairs={{0,4},{4,0},{8,12},{12,8},{1,5},{5,1},{9,13},{13,9},{2,6},{6,2},{1... | collective-permute-start | bytes 393224 | tf_op jit(solution)/shard_map/ppermute | solution.py:253
  18.1 1.4 %far_rest.1 = (bf16[128,512]{1,0:T(8,128)(2,1)S(1)}, f32[2,128,512]{2,1,0:T(8,128)S(1)}) custom-call(s32[4]{0:T(128)S(1)} %get-tuple-element.17.info, bf16[1,512,512]{2,1,0:T(8,128)(2,1)S(1)} %get-tuple-element.25.blocks, bf16[4,512,512]{2,1,0:T(8,128)(2,1)S(1)} %get-tuple-element.22.refs_2_.refs_4_.left, ...), custom_call_target="tpu_custom_call" | custom-call | tf_op jit(solution)/shard_map/far_rest/pallas_call | solution.py:185
  19.5 0.8 %collective-permute-start.6 = (bf16[128,512]{1,0:T(8,128)(2,1)S(1)}, bf16[128,512]{1,0:T(8,128)(2,1)S(1)}, u32[]{:S(2)}, u32[]{:S(2)}) collective-permute-start(bf16[128,512]{1,0:T(8,128)(2,1)S(1)} %get-tuple-element.27), channel_id=1, source_target_pairs={{0,4},{4,0},{8,12},{12,8},{1,5},{5,1},{9,13},{13,9},{2,6},{6,2},{1... | collective-permute-start | bytes 393224 | tf_op jit(solution)/shard_map/ppermute | solution.py:262
  20.3 1.1 %collective-permute-done.7.got = bf16[1,128,512]{2,1,0:T(8,128)(2,1)S(1)} collective-permute-done((bf16[1,128,512]{2,1,0:T(8,128)(2,1)S(1)}, bf16[1,128,512]{2,1,0:T(8,128)(2,1)S(1)}, u32[]{:S(2)}, u32[]{:S(2)}) %collective-permute-start.7) | collective-permute-done | bytes 131104 | tf_op jit(solution)/shard_map/ppermute | solution.py:253
  21.4 3.3 %collective-permute-start.8 = (bf16[128,512]{1,0:T(8,128)(2,1)S(1)}, bf16[128,512]{1,0:T(8,128)(2,1)S(1)}, u32[]{:S(2)}, u32[]{:S(2)}) collective-permute-start(bf16[128,512]{1,0:T(8,128)(2,1)S(1)} %pass_on.1), channel_id=1, source_target_pairs={{0,8},{4,12},{8,0},{12,4},{1,9},{5,13},{9,1},{13,5},{2,10},{6,14},... | collective-permute-start | bytes 393224 | tf_op jit(solution)/shard_map/ppermute | solution.py:272
  24.7 1.0 %collective-permute-done.6.refs_0_ = bf16[128,512]{1,0:T(8,128)(2,1)S(1)} collective-permute-done((bf16[128,512]{1,0:T(8,128)(2,1)S(1)}, bf16[128,512]{1,0:T(8,128)(2,1)S(1)}, u32[]{:S(2)}, u32[]{:S(2)}) %collective-permute-start.6) | collective-permute-done | bytes 131104 | tf_op jit(solution)/shard_map/ppermute | solution.py:262
  25.7 4.0 %collective-permute-done.8.refs_1_ = bf16[128,512]{1,0:T(8,128)(2,1)S(1)} collective-permute-done((bf16[128,512]{1,0:T(8,128)(2,1)S(1)}, bf16[128,512]{1,0:T(8,128)(2,1)S(1)}, u32[]{:S(2)}, u32[]{:S(2)}) %collective-permute-start.8) | collective-permute-done | bytes 131104 | tf_op jit(solution)/shard_map/ppermute | solution.py:272
  29.7 0.7 %sum_parts.1 = bf16[1,128,512]{2,1,0:T(8,128)(2,1)} custom-call(s32[1]{0:T(128)S(6)} %copy.6.rows, f32[2,128,512]{2,1,0:T(8,128)S(1)} %get-tuple-element.26.kept, bf16[128,512]{1,0:T(8,128)(2,1)S(1)} %collective-permute-done.6.refs_0_, bf16[128,512]{1,0:T(8,128)(2,1)S(1)} %collective-permute-done.8.refs_1_), custom_call_target="tpu_custom_call" | custom-call | tf_op jit(solution)/shard_map/sum_parts/pallas_call | solution.py:185
  (1 shorter events, 0.0 us)
Async XLA Ops:
  0.0 11.9 %collective-permute-start.5 = (bf16[1,512,512]{2,1,0:T(8,128)(2,1)}, bf16[1,512,512]{2,1,0:T(8,128)(2,1)S(1)}, u32[]{:S(2)}, u32[]{:S(2)}) collective-permute-start(bf16[1,512,512]{2,1,0:T(8,128)(2,1)} %wave_hbm.3), channel_id=1, source_target_pairs={{0,1},{2,3},{1,0},{3,2},{4,5},{6,7},{5,4},{7,6},{8,9},{10,11},{9,8... | collective-permute-start | bytes 1572872 | tf_op jit(solution)/shard_map/ppermute | solution.py:207
  1.5 6.9 %collective-permute-start.1 = (bf16[128,512]{1,0:T(8,128)(2,1)S(1)}, bf16[128,512]{1,0:T(8,128)(2,1)S(1)}, u32[]{:S(2)}, u32[]{:S(2)}) collective-permute-start(bf16[128,512]{1,0:T(8,128)(2,1)S(1)} %get-tuple-element.18), channel_id=1, source_target_pairs={{0,2},{1,3},{2,0},{3,1},{4,6},{5,7},{6,4},{7,5},{8,10},{9,11},{10,... | collective-permute-start | bytes 393224 | tf_op jit(solution)/shard_map/ppermute | solution.py:207
  4.1 10.2 %collective-permute-start.3 = (bf16[256,512]{1,0:T(8,128)(2,1)S(1)}, bf16[256,512]{1,0:T(8,128)(2,1)S(1)}, u32[]{:S(2)}, u32[]{:S(2)}) collective-permute-start(bf16[256,512]{1,0:T(8,128)(2,1)S(1)} %get-tuple-element.21), channel_id=1, source_target_pairs={{0,2},{1,3},{2,0},{3,1},{4,6},{5,7},{6,4},{7,5},{8,10},{9,11},{10,... | collective-permute-start | bytes 786440 | tf_op jit(solution)/shard_map/ppermute | solution.py:207
  8.4 5.8 %collective-permute-start.2 = (bf16[128,512]{1,0:T(8,128)(2,1)S(1)}, bf16[128,512]{1,0:T(8,128)(2,1)S(1)}, u32[]{:S(2)}, u32[]{:S(2)}) collective-permute-start(bf16[128,512]{1,0:T(8,128)(2,1)S(1)} %collective-permute-done.1.refs_1_), channel_id=1, source_target_pairs={{0,4},{4,0},{8,12},{12,8},{1,5},{5,1},{9,13},{13,9},{2,6},{6,2},{1... | collective-permute-start | bytes 393224 | tf_op jit(solution)/shard_map/ppermute | solution.py:235
  10.4 1.5 %collective-permute-start.4 = (s32[1]{0:T(128)}, s32[1]{0:T(128)}, u32[]{:S(2)}, u32[]{:S(2)}) collective-permute-start(s32[1]{0:T(128)} %param.6), channel_id=1, source_target_pairs={{0,1},{2,3},{1,0},{3,2},{4,5},{6,7},{5,4},{7,6},{8,9},{10,11},{9,8... | collective-permute-start | bytes 20 | tf_op jit(solution)/shard_map/ppermute | solution.py:207
  10.4 3.8 %collective-permute-start = (s32[1]{0:T(128)}, s32[1]{0:T(128)}, u32[]{:S(2)}, u32[]{:S(2)}) collective-permute-start(s32[1]{0:T(128)} %param.6), channel_id=1, source_target_pairs={{0,2},{1,3},{2,0},{3,1},{4,6},{5,7},{6,4},{7,5},{8,10},{9,11},{10,... | collective-permute-start | bytes 20 | tf_op jit(solution)/shard_map/ppermute | solution.py:207
  16.0 5.4 %collective-permute-start.7 = (bf16[1,128,512]{2,1,0:T(8,128)(2,1)S(1)}, bf16[1,128,512]{2,1,0:T(8,128)(2,1)S(1)}, u32[]{:S(2)}, u32[]{:S(2)}) collective-permute-start(bf16[1,128,512]{2,1,0:T(8,128)(2,1)S(1)} %get-tuple-element.28), channel_id=1, source_target_pairs={{0,4},{4,0},{8,12},{12,8},{1,5},{5,1},{9,13},{13,9},{2,6},{6,2},{1... | collective-permute-start | bytes 393224 | tf_op jit(solution)/shard_map/ppermute | solution.py:253
  19.5 6.2 %collective-permute-start.6 = (bf16[128,512]{1,0:T(8,128)(2,1)S(1)}, bf16[128,512]{1,0:T(8,128)(2,1)S(1)}, u32[]{:S(2)}, u32[]{:S(2)}) collective-permute-start(bf16[128,512]{1,0:T(8,128)(2,1)S(1)} %get-tuple-element.27), channel_id=1, source_target_pairs={{0,4},{4,0},{8,12},{12,8},{1,5},{5,1},{9,13},{13,9},{2,6},{6,2},{1... | collective-permute-start | bytes 393224 | tf_op jit(solution)/shard_map/ppermute | solution.py:262
  21.4 8.3 %collective-permute-start.8 = (bf16[128,512]{1,0:T(8,128)(2,1)S(1)}, bf16[128,512]{1,0:T(8,128)(2,1)S(1)}, u32[]{:S(2)}, u32[]{:S(2)}) collective-permute-start(bf16[128,512]{1,0:T(8,128)(2,1)S(1)} %pass_on.1), channel_id=1, source_target_pairs={{0,8},{4,12},{8,0},{12,4},{1,9},{5,13},{9,1},{13,5},{2,10},{6,14},... | collective-permute-start | bytes 393224 | tf_op jit(solution)/shard_map/ppermute | solution.py:272

commit v8 on v7

--- a/solution.py
+++ b/solution.py
@@ -125,12 +125,13 @@
     add_terms(info, slots, sectors, grid, [blocks.at[place] for place in range(count)], left, right, add)
 
 
-def far_first_kernel(slots, sectors, grid, count, info, *refs):
+def far_kernel(slots, sectors, grid, count, info, *refs):
     rows, firsts, swapped, rests = (refs[i * count : (i + 1) * count] for i in range(4))
-    left, right, before, sent, blocks, total = refs[4 * count :]
+    left, right, before, kept = refs[4 * count : 4 * count + 4]
+    sent = refs[4 * count + 4 : -2]
+    blocks, total = refs[-2:]
     me = lax.axis_index("term")
     odd = lax.rem(me, 2)
-    partner = me + 1 - 2 * odd
     shared = firsts[0].shape[0]
     for place in range(count):
         pieces = ((odd * shared, firsts), ((1 - odd) * shared, swapped), (2 * shared, rests))
@@ -138,42 +139,25 @@
             piece = refs_of[place]
             rows_at = pl.ds(pl.multiple_of(start, 16), piece.shape[0])
             blocks[place, rows_at, :] = mask_rows(piece[...], rows[place][0], start)
-    passed, share = total.shape[0], total.shape[1]
-    shards = [shard_rows(lax.rem(partner + 2 * (k + 1), 2 * (passed + 1)), share) for k in range(passed)]
-    for k in range(passed):
-        total[k] = before[shards[k], :]
-
-    def add(term, block):
-        for k in range(passed):
-            total[k] += product(left[term, shards[k], :], block[...], right[term])
-
-    add_terms(info, slots, sectors, grid, [blocks.at[place] for place in range(count)], left, right, add)
-    sent[...] = total[...].astype(jnp.bfloat16)
-
-
-def far_rest_kernel(slots, sectors, grid, count, info, blocks, left, right, before, sent, kept, total):
-    me = lax.axis_index("term")
-    partner = me + 1 - 2 * lax.rem(me, 2)
-    own_shards, share = kept.shape[0], kept.shape[1]
     total[...] = before[...]
 
     def add(term, block):
         total[...] += product(left[term], block[...], right[term])
 
     add_terms(info, slots, sectors, grid, [blocks.at[place] for place in range(count)], left, right, add)
-    sent[...] = total[shard_rows(partner, share), :].astype(jnp.bfloat16)
-    for k in range(own_shards):
-        kept[k] = total[shard_rows(lax.rem(me + 2 * k, 2 * own_shards), share), :]
-
-
-def pass_kernel(kept, got, *sent):
-    for k, part in enumerate(sent):
-        part[...] = (kept[k + 1] + got[k].astype(jnp.float32)).astype(jnp.bfloat16)
+    parts, share = len(sent) + 1, kept.shape[0]
+    kept[...] = total[shard_rows(me, share), :]
+    for step, part in enumerate(sent, 1):
+        part[...] = total[shard_rows(me ^ step, share), :].astype(jnp.bfloat16)
+
+
+def half_kernel(kept, got, total):
+    total[...] = kept[...] + got[...].astype(jnp.float32)
 
 
 def last_kernel(rows, kept, *refs):
     got, out = refs[:-1], refs[-1]
-    total = kept[0]
+    total = kept[...]
     for part in got:
         total = total + part[...].astype(jnp.float32)
     share = total.shape[0]
@@ -200,7 +184,6 @@
     grid = max(2, sectors // 4)
     share = pad // parts
     shared = pad // 4
-    passed = parts // 2 - 1
     down, up = neighbour_moves(sectors, grid)
     near_slots, far_slots = {1: 0, 2: len(down) - 1}, {3: 0, 4: len(up) - 1}
     count = len(up)
@@ -242,41 +225,27 @@
         [pltpu.VMEM((len(down), pad, columns), bf16)],
         info, *near_rows, *near_blocks, *env, total,
     )
-    sent, blocks = call(
-        functools.partial(far_first_kernel, far_slots, sectors, grid, count),
-        "far_first",
-        [((passed, share, pad), bf16), ((count, pad, columns), bf16)],
+    kept, *sent = call(
+        functools.partial(far_kernel, far_slots, sectors, grid, count),
+        "far_terms",
+        [((share, pad), f32)] + [((share, pad), bf16)] * (parts - 1),
         [SMEM] * (1 + count) + [VMEM] * (3 * count + 3),
-        [pltpu.VMEM((passed, share, pad), f32)],
+        [pltpu.VMEM((count, pad, columns), bf16), pltpu.VMEM((pad, pad), f32)],
         info, *far_rows, *firsts, *swapped, *rests, *env, total,
     )
-    got = lax.ppermute(sent, "term", swap)
-    sent, kept = call(
-        functools.partial(far_rest_kernel, far_slots, sectors, grid, count),
-        "far_rest",
-        [((share, pad), bf16), ((passed + 1, share, pad), f32)],
-        [SMEM] + [VMEM] * 4,
-        [pltpu.VMEM((pad, pad), f32)],
-        info, blocks, *env, total,
-    )
-    last = [lax.ppermute(sent, "term", swap)]
-    sums = call(
-        pass_kernel,
-        "pass_on",
-        [((share, pad), bf16)] * passed,
-        [VMEM] * 2,
-        [],
-        kept, got,
-    )
-    for k, part in enumerate(sums, 1):
-        last.append(lax.ppermute(part, "term", [(i, (i + 2 * k) % parts) for i in range(parts)]))
+    turned = [
+        lax.ppermute(part, "term", [(i, i ^ step) for i in range(parts)])
+        for step, part in enumerate(sent, 1)
+    ]
+    half = turned.pop(parts // 2 - 1)
+    (kept,) = call(half_kernel, "sum_half", [((share, pad), f32)], [VMEM] * 2, [], kept, half)
     (out,) = call(
         last_kernel,
         "sum_parts",
         [((1, share, pad), bf16)],
-        [SMEM] + [VMEM] * (1 + len(last)),
+        [SMEM] + [VMEM] * (1 + len(turned)),
         [],
-        sector_rows, kept, *last,
+        sector_rows, kept, *turned,
     )
     return out
 

time: 30.9 us -> 30.5 us (0.987); the launches traced: 30.4 us -> 30.4 us
  waiting for transfers between devices: 6.99 us -> 9.38 us
  Pallas kernels: 9.91 us -> 8.2 us
  starting transfers between devices: 12.8 us -> 12.2 us
    ppermute x3, waiting for transfers between devices: 6.06 us -> 8.67 us  [per_device(): lax.ppermute(part, 'term', [(i, i ^ step) for i in range(parts)])]
    pallas_call x7 -> x6, Pallas kernels: 9.91 us -> 8.2 us  [call(): pl.pallas_call(kernel, out_shape=[jax.ShapeDtypeStruct(shape, dtype) for...]
    ppermute x3, starting transfers between devices: 6.22 us -> 5.55 us  [per_device(): lax.ppermute(part, 'term', [(i, i ^ step) for i in range(parts)])]
  transfers between devices with their start and end apart: 9 -> 9, of which waited for: 5 -> 4; matrix products, arithmetic and copies ran while one was open for 0% -> 0% of each run, Pallas kernels for 24% -> 20%
where the time goes in v8:
time: 30.5 us; the launch traced here: 30.4 us
  starting transfers between devices  12.2 us (40%)
  waiting for transfers between devices  9.38 us (31%)
  Pallas kernels  8.2 us (27%)
  between operations  0.7 us (2%)
    ppermute x3, waiting for transfers between devices, per_device(): lax.ppermute(part, 'term', [(i, i ^ step) for i in range(parts)])  8.67 us
    pallas_call x6, Pallas kernels, call(): pl.pallas_call(kernel, out_shape=[jax.ShapeDtypeStruct(shape, dtype) for...  8.2 us
    ppermute x3, starting transfers between devices, per_device(): lax.ppermute(part, 'term', [(i, i ^ step) for i in range(parts)])  5.55 us
    ppermute x5, starting transfers between devices, per_device(): send = lambda array, pairs: lax.ppermute(array, 'sector', pairs)  4.58 us
    ppermute x1, starting transfers between devices, per_device(): swapped = [lax.ppermute(array, 'term', swap) for array in firsts]  2.03 us
    ppermute x5, waiting for transfers between devices, per_device(): send = lambda array, pairs: lax.ppermute(array, 'sector', pairs)  0.71 us
  transfers between devices with their start and end apart: 9, of which 4 were waited for; matrix products, arithmetic and copies ran while one was open for 0% of the time, Pallas kernels for 20%

profile of v8, /device:TPU:0, one launch (start us, length us, event | category | flops | bytes accessed | tf_op | source)
XLA Modules:
  0.0 30.4 jit_solution(6722347775308502261)
XLA Ops:
  0.0 0.5 %collective-permute-start.5 = (bf16[1,512,512]{2,1,0:T(8,128)(2,1)}, bf16[1,512,512]{2,1,0:T(8,128)(2,1)S(1)}, u32[]{:S(2)}, u32[]{:S(2)}) collective-permute-start(bf16[1,512,512]{2,1,0:T(8,128)(2,1)} %wave_hbm.3), channel_id=1, source_target_pairs={{0,1},{2,3},{1,0},{3,2},{4,5},{6,7},{5,4},{7,6},{8,9},{10,11},{9,8... | collective-permute-start | bytes 1572872 | tf_op jit(solution)/shard_map/ppermute | solution.py:190
  0.5 1.0 %cut.1 = (bf16[128,512]{1,0:T(8,128)(2,1)S(1)}, bf16[256,512]{1,0:T(8,128)(2,1)S(1)}) custom-call(bf16[1,512,512]{2,1,0:T(8,128)(2,1)} %wave_hbm.3), custom_call_target="tpu_custom_call" | custom-call | tf_op jit(solution)/shard_map/cut/pallas_call | solution.py:169
  1.5 2.6 %collective-permute-start.1 = (bf16[128,512]{1,0:T(8,128)(2,1)S(1)}, bf16[128,512]{1,0:T(8,128)(2,1)S(1)}, u32[]{:S(2)}, u32[]{:S(2)}) collective-permute-start(bf16[128,512]{1,0:T(8,128)(2,1)S(1)} %get-tuple-element.18), channel_id=1, source_target_pairs={{0,2},{1,3},{2,0},{3,1},{4,6},{5,7},{6,4},{7,5},{8,10},{9,11},{10,... | collective-permute-start | bytes 393224 | tf_op jit(solution)/shard_map/ppermute | solution.py:190
  4.1 0.1 collective-permute-start.3
  4.8 3.0 %own_terms.1 = (s32[4]{0:T(128)S(1)}, f32[512,512]{1,0:T(8,128)S(1)}, bf16[4,512,512]{2,1,0:T(8,128)(2,1)S(1)}, bf16[4,512,512]{2,1,0:T(8,128)(2,1)S(1)}) custom-call(s32[4]{0:T(128)} %classes_hbm.1, s32[1]{0:T(128)S(6)} %copy.6.rows, bf16[1,512,512]{2,1,0:T(8,128)(2,1)} %wave_hbm.3, bf16[4,1,512,512]{3,2,1,0:T(8,128)(2,1)} %left_hbm.1, ...), custom_call_target="tpu_custom_call" | custom-call | tf_op jit(solution)/shard_map/own_terms/pallas_call | solution.py:169
  7.8 0.6 %collective-permute-done.1.refs_1_ = bf16[128,512]{1,0:T(8,128)(2,1)S(1)} collective-permute-done((bf16[128,512]{1,0:T(8,128)(2,1)S(1)}, bf16[128,512]{1,0:T(8,128)(2,1)S(1)}, u32[]{:S(2)}, u32[]{:S(2)}) %collective-permute-start.1) | collective-permute-done | bytes 131104 | tf_op jit(solution)/shard_map/ppermute | solution.py:190
  8.4 2.0 %collective-permute-start.2 = (bf16[128,512]{1,0:T(8,128)(2,1)S(1)}, bf16[128,512]{1,0:T(8,128)(2,1)S(1)}, u32[]{:S(2)}, u32[]{:S(2)}) collective-permute-start(bf16[128,512]{1,0:T(8,128)(2,1)S(1)} %collective-permute-done.1.refs_1_), channel_id=1, source_target_pairs={{0,4},{4,0},{8,12},{12,8},{1,5},{5,1},{9,13},{13,9},{2,6},{6,2},{1... | collective-permute-start | bytes 393224 | tf_op jit(solution)/shard_map/ppermute | solution.py:218
  10.4 0.0 collective-permute-start.4
  10.4 1.5 %collective-permute-start = (s32[1]{0:T(128)}, s32[1]{0:T(128)}, u32[]{:S(2)}, u32[]{:S(2)}) collective-permute-start(s32[1]{0:T(128)} %param.6), channel_id=1, source_target_pairs={{0,2},{1,3},{2,0},{3,1},{4,6},{5,7},{6,4},{7,5},{8,10},{9,11},{10,... | collective-permute-start | bytes 20 | tf_op jit(solution)/shard_map/ppermute | solution.py:190
  11.9 0.0 collective-permute-done.4.refs_0_
  11.9 0.0 collective-permute-done.5.refs_1_
  11.9 2.0 %near_terms.1.refs_6_ = f32[512,512]{1,0:T(8,128)S(1)} custom-call(s32[4]{0:T(128)S(1)} %get-tuple-element.17.info, s32[1]{0:T(128)} %collective-permute-done.4.refs_0_, bf16[1,512,512]{2,1,0:T(8,128)(2,1)S(1)} %collective-permute-done.5.refs_1_, bf16[4,512,512]{2,1,0:T(8,128)(2,1)S(1)} %get-tuple-element.22.refs_2_.refs_4_, ...), custom_call_target="tpu_custom_call" | custom-call | tf_op jit(solution)/shard_map/near_terms/pallas_call | solution.py:169
  14.0 0.1 collective-permute-done.refs_0_
  14.1 0.0 collective-permute-done.2.refs_2_
  14.1 0.0 collective-permute-done.3.refs_3_
  14.1 1.4 %far_terms.1 = (f32[128,512]{1,0:T(8,128)S(1)}, bf16[128,512]{1,0:T(8,128)(2,1)S(1)}, bf16[128,512]{1,0:T(8,128)(2,1)S(1)}, bf16[128,512]{1,0:T(8,128)(2,1)S(1)}) custom-call(s32[4]{0:T(128)S(1)} %get-tuple-element.17.info, s32[1]{0:T(128)} %collective-permute-done.refs_0_, bf16[128,512]{1,0:T(8,128)(2,1)S(1)} %collective-permute-done.1.refs_1_, ...), custom_call_target="tpu_custom_call" | custom-call | tf_op jit(solution)/shard_map/far_terms/pallas_call | solution.py:169
  15.5 4.0 %collective-permute-start.6 = (bf16[128,512]{1,0:T(8,128)(2,1)S(1)}, bf16[128,512]{1,0:T(8,128)(2,1)S(1)}, u32[]{:S(2)}, u32[]{:S(2)}) collective-permute-start(bf16[128,512]{1,0:T(8,128)(2,1)S(1)} %get-tuple-element.26), channel_id=1, source_target_pairs={{0,8},{4,12},{8,0},{12,4},{1,9},{5,13},{9,1},{13,5},{2,10},{6,14},... | collective-permute-start | bytes 393224 | tf_op jit(solution)/shard_map/ppermute | solution.py:237
  19.5 1.0 %collective-permute-start.7 = (bf16[128,512]{1,0:T(8,128)(2,1)S(1)}, bf16[128,512]{1,0:T(8,128)(2,1)S(1)}, u32[]{:S(2)}, u32[]{:S(2)}) collective-permute-start(bf16[128,512]{1,0:T(8,128)(2,1)S(1)} %get-tuple-element.27), channel_id=1, source_target_pairs={{0,4},{4,0},{8,12},{12,8},{1,5},{5,1},{9,13},{13,9},{2,6},{6,2},{1... | collective-permute-start | bytes 393224 | tf_op jit(solution)/shard_map/ppermute | solution.py:237
  20.5 0.5 %collective-permute-start.8 = (bf16[128,512]{1,0:T(8,128)(2,1)S(1)}, bf16[128,512]{1,0:T(8,128)(2,1)S(1)}, u32[]{:S(2)}, u32[]{:S(2)}) collective-permute-start(bf16[128,512]{1,0:T(8,128)(2,1)S(1)} %get-tuple-element.28), channel_id=1, source_target_pairs={{0,12},{4,8},{8,4},{12,0},{1,13},{5,9},{9,5},{13,1},{2,14},{6,10},... | collective-permute-start | bytes 393224 | tf_op jit(solution)/shard_map/ppermute | solution.py:237
  21.0 6.6 %collective-permute-done.6.got = bf16[128,512]{1,0:T(8,128)(2,1)S(1)} collective-permute-done((bf16[128,512]{1,0:T(8,128)(2,1)S(1)}, bf16[128,512]{1,0:T(8,128)(2,1)S(1)}, u32[]{:S(2)}, u32[]{:S(2)}) %collective-permute-start.6) | collective-permute-done | bytes 131104 | tf_op jit(solution)/shard_map/ppermute | solution.py:237
  27.7 0.0 collective-permute-done.7.refs_0_
  27.7 2.0 %collective-permute-done.8.refs_1_ = bf16[128,512]{1,0:T(8,128)(2,1)S(1)} collective-permute-done((bf16[128,512]{1,0:T(8,128)(2,1)S(1)}, bf16[128,512]{1,0:T(8,128)(2,1)S(1)}, u32[]{:S(2)}, u32[]{:S(2)}) %collective-permute-start.8) | collective-permute-done | bytes 131104 | tf_op jit(solution)/shard_map/ppermute | solution.py:237
  29.7 0.7 %sum_parts.1 = bf16[1,128,512]{2,1,0:T(8,128)(2,1)} custom-call(s32[1]{0:T(128)S(6)} %copy.6.rows, f32[128,512]{1,0:T(8,128)S(1)} %sum_half.1.kept, bf16[128,512]{1,0:T(8,128)(2,1)S(1)} %collective-permute-done.7.refs_0_, bf16[128,512]{1,0:T(8,128)(2,1)S(1)} %collective-permute-done.8.refs_1_), custom_call_target="tpu_custom_call" | custom-call | tf_op jit(solution)/shard_map/sum_parts/pallas_call | solution.py:169
  (1 shorter events, 0.0 us)
Async XLA Ops:
  0.0 11.9 %collective-permute-start.5 = (bf16[1,512,512]{2,1,0:T(8,128)(2,1)}, bf16[1,512,512]{2,1,0:T(8,128)(2,1)S(1)}, u32[]{:S(2)}, u32[]{:S(2)}) collective-permute-start(bf16[1,512,512]{2,1,0:T(8,128)(2,1)} %wave_hbm.3), channel_id=1, source_target_pairs={{0,1},{2,3},{1,0},{3,2},{4,5},{6,7},{5,4},{7,6},{8,9},{10,11},{9,8... | collective-permute-start | bytes 1572872 | tf_op jit(solution)/shard_map/ppermute | solution.py:190
  1.5 6.9 %collective-permute-start.1 = (bf16[128,512]{1,0:T(8,128)(2,1)S(1)}, bf16[128,512]{1,0:T(8,128)(2,1)S(1)}, u32[]{:S(2)}, u32[]{:S(2)}) collective-permute-start(bf16[128,512]{1,0:T(8,128)(2,1)S(1)} %get-tuple-element.18), channel_id=1, source_target_pairs={{0,2},{1,3},{2,0},{3,1},{4,6},{5,7},{6,4},{7,5},{8,10},{9,11},{10,... | collective-permute-start | bytes 393224 | tf_op jit(solution)/shard_map/ppermute | solution.py:190
  4.1 10.0 %collective-permute-start.3 = (bf16[256,512]{1,0:T(8,128)(2,1)S(1)}, bf16[256,512]{1,0:T(8,128)(2,1)S(1)}, u32[]{:S(2)}, u32[]{:S(2)}) collective-permute-start(bf16[256,512]{1,0:T(8,128)(2,1)S(1)} %get-tuple-element.21), channel_id=1, source_target_pairs={{0,2},{1,3},{2,0},{3,1},{4,6},{5,7},{6,4},{7,5},{8,10},{9,11},{10,... | collective-permute-start | bytes 786440 | tf_op jit(solution)/shard_map/ppermute | solution.py:190
  8.4 5.7 %collective-permute-start.2 = (bf16[128,512]{1,0:T(8,128)(2,1)S(1)}, bf16[128,512]{1,0:T(8,128)(2,1)S(1)}, u32[]{:S(2)}, u32[]{:S(2)}) collective-permute-start(bf16[128,512]{1,0:T(8,128)(2,1)S(1)} %collective-permute-done.1.refs_1_), channel_id=1, source_target_pairs={{0,4},{4,0},{8,12},{12,8},{1,5},{5,1},{9,13},{13,9},{2,6},{6,2},{1... | collective-permute-start | bytes 393224 | tf_op jit(solution)/shard_map/ppermute | solution.py:218
  10.4 1.5 %collective-permute-start.4 = (s32[1]{0:T(128)}, s32[1]{0:T(128)}, u32[]{:S(2)}, u32[]{:S(2)}) collective-permute-start(s32[1]{0:T(128)} %param.6), channel_id=1, source_target_pairs={{0,1},{2,3},{1,0},{3,2},{4,5},{6,7},{5,4},{7,6},{8,9},{10,11},{9,8... | collective-permute-start | bytes 20 | tf_op jit(solution)/shard_map/ppermute | solution.py:190
  10.4 3.6 %collective-permute-start = (s32[1]{0:T(128)}, s32[1]{0:T(128)}, u32[]{:S(2)}, u32[]{:S(2)}) collective-permute-start(s32[1]{0:T(128)} %param.6), channel_id=1, source_target_pairs={{0,2},{1,3},{2,0},{3,1},{4,6},{5,7},{6,4},{7,5},{8,10},{9,11},{10,... | collective-permute-start | bytes 20 | tf_op jit(solution)/shard_map/ppermute | solution.py:190
  15.5 12.2 %collective-permute-start.6 = (bf16[128,512]{1,0:T(8,128)(2,1)S(1)}, bf16[128,512]{1,0:T(8,128)(2,1)S(1)}, u32[]{:S(2)}, u32[]{:S(2)}) collective-permute-start(bf16[128,512]{1,0:T(8,128)(2,1)S(1)} %get-tuple-element.26), channel_id=1, source_target_pairs={{0,8},{4,12},{8,0},{12,4},{1,9},{5,13},{9,1},{13,5},{2,10},{6,14},... | collective-permute-start | bytes 393224 | tf_op jit(solution)/shard_map/ppermute | solution.py:237
  19.5 8.2 %collective-permute-start.7 = (bf16[128,512]{1,0:T(8,128)(2,1)S(1)}, bf16[128,512]{1,0:T(8,128)(2,1)S(1)}, u32[]{:S(2)}, u32[]{:S(2)}) collective-permute-start(bf16[128,512]{1,0:T(8,128)(2,1)S(1)} %get-tuple-element.27), channel_id=1, source_target_pairs={{0,4},{4,0},{8,12},{12,8},{1,5},{5,1},{9,13},{13,9},{2,6},{6,2},{1... | collective-permute-start | bytes 393224 | tf_op jit(solution)/shard_map/ppermute | solution.py:237
  20.5 9.2 %collective-permute-start.8 = (bf16[128,512]{1,0:T(8,128)(2,1)S(1)}, bf16[128,512]{1,0:T(8,128)(2,1)S(1)}, u32[]{:S(2)}, u32[]{:S(2)}) collective-permute-start(bf16[128,512]{1,0:T(8,128)(2,1)S(1)} %get-tuple-element.28), channel_id=1, source_target_pairs={{0,12},{4,8},{8,4},{12,0},{1,13},{5,9},{9,5},{13,1},{2,14},{6,10},... | collective-permute-start | bytes 393224 | tf_op jit(solution)/shard_map/ppermute | solution.py:237

commit v9 on v8

--- a/solution.py
+++ b/solution.py
@@ -114,10 +114,9 @@
 
 def near_kernel(slots, sectors, grid, count, info, *refs):
     rows, got = refs[:count], refs[count : 2 * count]
-    left, right, before, total, blocks = refs[2 * count :]
+    left, right, _, total, blocks = refs[2 * count :]
     for place in range(count):
         blocks[place] = mask_rows(got[place][0], rows[place][0])
-    total[...] = before[...]
 
     def add(term, block):
         total[...] += product(left[term], block[...], right[term])
@@ -127,9 +126,9 @@
 
 def far_kernel(slots, sectors, grid, count, info, *refs):
     rows, firsts, swapped, rests = (refs[i * count : (i + 1) * count] for i in range(4))
-    left, right, before, kept = refs[4 * count : 4 * count + 4]
-    sent = refs[4 * count + 4 : -2]
-    blocks, total = refs[-2:]
+    left, right, _, total, kept = refs[4 * count : 4 * count + 5]
+    sent = refs[4 * count + 5 : -1]
+    blocks = refs[-1]
     me = lax.axis_index("term")
     odd = lax.rem(me, 2)
     shared = firsts[0].shape[0]
@@ -139,7 +138,6 @@
             piece = refs_of[place]
             rows_at = pl.ds(pl.multiple_of(start, 16), piece.shape[0])
             blocks[place, rows_at, :] = mask_rows(piece[...], rows[place][0], start)
-    total[...] = before[...]
 
     def add(term, block):
         total[...] += product(left[term], block[...], right[term])
@@ -165,13 +163,14 @@
     out[0] = jnp.where(row < rows[0], total, 0.0).astype(jnp.bfloat16)
 
 
-def call(kernel, name, shapes, in_specs, scratch, *args, out_specs=None):
+def call(kernel, name, shapes, in_specs, scratch, *args, out_specs=None, aliases=None):
     return pl.pallas_call(
         kernel,
         out_shape=[jax.ShapeDtypeStruct(shape, dtype) for shape, dtype in shapes],
         in_specs=in_specs,
         out_specs=out_specs or [VMEM] * len(shapes),
         scratch_shapes=scratch,
+        input_output_aliases=aliases or {},
         compiler_params=LIMIT,
         name=name,
     )(*args)
@@ -224,14 +223,16 @@
         [SMEM] * (1 + len(down)) + [VMEM] * (len(down) + 3),
         [pltpu.VMEM((len(down), pad, columns), bf16)],
         info, *near_rows, *near_blocks, *env, total,
-    )
-    kept, *sent = call(
+        aliases={3 + 2 * len(down): 0},
+    )
+    _, kept, *sent = call(
         functools.partial(far_kernel, far_slots, sectors, grid, count),
         "far_terms",
-        [((share, pad), f32)] + [((share, pad), bf16)] * (parts - 1),
+        [((pad, pad), f32), ((share, pad), f32)] + [((share, pad), bf16)] * (parts - 1),
         [SMEM] * (1 + count) + [VMEM] * (3 * count + 3),
-        [pltpu.VMEM((count, pad, columns), bf16), pltpu.VMEM((pad, pad), f32)],
+        [pltpu.VMEM((count, pad, columns), bf16)],
         info, *far_rows, *firsts, *swapped, *rests, *env, total,
+        aliases={3 + 4 * count: 0},
     )
     turned = [
         lax.ppermute(part, "term", [(i, i ^ step) for i in range(parts)])

time: 30.5 us -> 31.7 us (1.039); the launches traced: 30.4 us -> 31 us
  Pallas kernels: 8.2 us -> 9.17 us
  starting transfers between devices: 12.2 us -> 11.7 us
    ppermute x3, starting transfers between devices: 5.55 us -> 4.45 us  [per_device(): lax.ppermute(part, 'term', [(i, i ^ step) for i in range(parts)])]
    pallas_call x6, Pallas kernels: 8.2 us -> 9.17 us  [call(): pl.pallas_call(kernel, out_shape=[jax.ShapeDtypeStruct(shape, dtype) for...]
    ppermute x5, waiting for transfers between devices: 0.71 us -> 1.61 us  [per_device(): send = lambda array, pairs: lax.ppermute(array, 'sector', pairs)]
    ppermute x3, waiting for transfers between devices: 8.67 us -> 7.79 us  [per_device(): lax.ppermute(part, 'term', [(i, i ^ step) for i in range(parts)])]
    ppermute x1, starting transfers between devices: 2.03 us -> 2.68 us  [per_device(): swapped = [lax.ppermute(array, 'term', swap) for array in firsts]]
  transfers between devices with their start and end apart: 9 -> 9, of which waited for: 4 -> 3; matrix products, arithmetic and copies ran while one was open for 0% -> 0% of each run, Pallas kernels for 20% -> 23%
where the time goes in v9:
time: 31.7 us; the launch traced here: 31 us
  starting transfers between devices  11.7 us (37%)
  waiting for transfers between devices  9.4 us (30%)
  Pallas kernels  9.17 us (29%)
  between operations  0.73 us (2%)
    pallas_call x6, Pallas kernels, call(): pl.pallas_call(kernel, out_shape=[jax.ShapeDtypeStruct(shape, dtype) for...  9.17 us
    ppermute x3, waiting for transfers between devices, per_device(): lax.ppermute(part, 'term', [(i, i ^ step) for i in range(parts)])  7.79 us
    ppermute x5, starting transfers between devices, per_device(): send = lambda array, pairs: lax.ppermute(array, 'sector', pairs)  4.58 us
    ppermute x3, starting transfers between devices, per_device(): lax.ppermute(part, 'term', [(i, i ^ step) for i in range(parts)])  4.45 us
    ppermute x1, starting transfers between devices, per_device(): swapped = [lax.ppermute(array, 'term', swap) for array in firsts]  2.68 us
    ppermute x5, waiting for transfers between devices, per_device(): send = lambda array, pairs: lax.ppermute(array, 'sector', pairs)  1.61 us
  transfers between devices with their start and end apart: 9, of which 3 were waited for; matrix products, arithmetic and copies ran while one was open for 0% of the time, Pallas kernels for 23%

profile of v9, /device:TPU:0, one launch (start us, length us, event | category | flops | bytes accessed | tf_op | source)
XLA Modules:
  0.0 31.0 jit_solution(12957889181250386172)
XLA Ops:
  0.0 0.5 %collective-permute-start.5 = (bf16[1,512,512]{2,1,0:T(8,128)(2,1)}, bf16[1,512,512]{2,1,0:T(8,128)(2,1)S(1)}, u32[]{:S(2)}, u32[]{:S(2)}) collective-permute-start(bf16[1,512,512]{2,1,0:T(8,128)(2,1)} %wave_hbm.3), channel_id=1, source_target_pairs={{0,1},{2,3},{1,0},{3,2},{4,5},{6,7},{5,4},{7,6},{8,9},{10,11},{9,8... | collective-permute-start | bytes 1572872 | tf_op jit(solution)/shard_map/ppermute | solution.py:189
  0.5 1.0 %cut.1 = (bf16[128,512]{1,0:T(8,128)(2,1)S(1)}, bf16[256,512]{1,0:T(8,128)(2,1)S(1)}) custom-call(bf16[1,512,512]{2,1,0:T(8,128)(2,1)} %wave_hbm.3), custom_call_target="tpu_custom_call" | custom-call | tf_op jit(solution)/shard_map/cut/pallas_call | solution.py:167
  1.5 2.6 %collective-permute-start.1 = (bf16[128,512]{1,0:T(8,128)(2,1)S(1)}, bf16[128,512]{1,0:T(8,128)(2,1)S(1)}, u32[]{:S(2)}, u32[]{:S(2)}) collective-permute-start(bf16[128,512]{1,0:T(8,128)(2,1)S(1)} %get-tuple-element.18), channel_id=1, source_target_pairs={{0,2},{1,3},{2,0},{3,1},{4,6},{5,7},{6,4},{7,5},{8,10},{9,11},{10,... | collective-permute-start | bytes 393224 | tf_op jit(solution)/shard_map/ppermute | solution.py:189
  4.1 0.1 collective-permute-start.3
  4.8 3.4 %own_terms.1 = (s32[4]{0:T(128)S(1)}, f32[512,512]{1,0:T(8,128)S(1)}, bf16[4,512,512]{2,1,0:T(8,128)(2,1)S(1)}, bf16[4,512,512]{2,1,0:T(8,128)(2,1)S(1)}) custom-call(s32[4]{0:T(128)} %classes_hbm.1, s32[1]{0:T(128)S(6)} %copy.10.rows, bf16[1,512,512]{2,1,0:T(8,128)(2,1)} %wave_hbm.3, bf16[4,1,512,512]{3,2,1,0:T(8,128)(2,1)} %left_hbm.1, ...), custom_call_target="tpu_custom_call" | custom-call | tf_op jit(solution)/shard_map/own_terms/pallas_call | solution.py:167
  8.2 0.2 collective-permute-done.1.refs_1_
  8.4 2.7 %collective-permute-start.2 = (bf16[128,512]{1,0:T(8,128)(2,1)S(1)}, bf16[128,512]{1,0:T(8,128)(2,1)S(1)}, u32[]{:S(2)}, u32[]{:S(2)}) collective-permute-start(bf16[128,512]{1,0:T(8,128)(2,1)S(1)} %collective-permute-done.1.refs_1_), channel_id=1, source_target_pairs={{0,4},{4,0},{8,12},{12,8},{1,5},{5,1},{9,13},{13,9},{2,6},{6,2},{1... | collective-permute-start | bytes 393224 | tf_op jit(solution)/shard_map/ppermute | solution.py:217
  11.1 1.5 %collective-permute-start = (s32[1]{0:T(128)}, s32[1]{0:T(128)}, u32[]{:S(2)}, u32[]{:S(2)}) collective-permute-start(s32[1]{0:T(128)} %param.6), channel_id=1, source_target_pairs={{0,2},{1,3},{2,0},{3,1},{4,6},{5,7},{6,4},{7,5},{8,10},{9,11},{10,... | collective-permute-start | bytes 20 | tf_op jit(solution)/shard_map/ppermute | solution.py:189
  12.6 0.0 collective-permute-start.4
  12.6 1.4 %collective-permute-done.4.refs_0_ = s32[1]{0:T(128)} collective-permute-done((s32[1]{0:T(128)}, s32[1]{0:T(128)}, u32[]{:S(2)}, u32[]{:S(2)}) %collective-permute-start.4) | collective-permute-done | bytes 36 | tf_op jit(solution)/shard_map/ppermute | solution.py:189
  14.0 0.0 collective-permute-done.5.refs_1_
  14.0 2.7 %near_terms.1.refs_6_ = f32[512,512]{1,0:T(8,128)S(1)} custom-call(s32[4]{0:T(128)S(1)} %get-tuple-element.17.info, s32[1]{0:T(128)} %collective-permute-done.4.refs_0_, bf16[1,512,512]{2,1,0:T(8,128)(2,1)S(1)} %collective-permute-done.5.refs_1_, bf16[4,512,512]{2,1,0:T(8,128)(2,1)S(1)} %get-tuple-element.22.refs_2_.refs_4_, ...), custom_call_target="tpu_custom_call", output_to_operand_aliasing={{}: (5, {})} | custom-call | tf_op jit(solution)/shard_map/near_terms/pallas_call | solution.py:167
  16.7 0.0 collective-permute-done.refs_0_
  16.7 0.0 collective-permute-done.3.refs_3_
  16.7 0.0 collective-permute-done.2.refs_2_
  16.7 1.3 %far_terms.1 = (f32[512,512]{1,0:T(8,128)S(1)}, f32[128,512]{1,0:T(8,128)S(1)}, bf16[128,512]{1,0:T(8,128)(2,1)S(1)}, bf16[128,512]{1,0:T(8,128)(2,1)S(1)}, bf16[128,512]{1,0:T(8,128)(2,1)S(1)}) custom-call(s32[4]{0:T(128)S(1)} %get-tuple-element.17.info, s32[1]{0:T(128)} %collective-permute-done.refs_0_, ...), custom_call_target="tpu_custom_call", output_to_operand_aliasing={{0}: (7, {})} | custom-call | tf_op jit(solution)/shard_map/far_terms/pallas_call | solution.py:167
  18.0 1.3 %collective-permute-start.6 = (bf16[128,512]{1,0:T(8,128)(2,1)S(1)}, bf16[128,512]{1,0:T(8,128)(2,1)S(1)}, u32[]{:S(2)}, u32[]{:S(2)}) collective-permute-start(bf16[128,512]{1,0:T(8,128)(2,1)S(1)} %get-tuple-element.26), channel_id=1, source_target_pairs={{0,8},{4,12},{8,0},{12,4},{1,9},{5,13},{9,1},{13,5},{2,10},{6,14},... | collective-permute-start | bytes 393224 | tf_op jit(solution)/shard_map/ppermute | solution.py:238
  19.3 1.8 %collective-permute-start.7 = (bf16[128,512]{1,0:T(8,128)(2,1)S(1)}, bf16[128,512]{1,0:T(8,128)(2,1)S(1)}, u32[]{:S(2)}, u32[]{:S(2)}) collective-permute-start(bf16[128,512]{1,0:T(8,128)(2,1)S(1)} %get-tuple-element.27), channel_id=1, source_target_pairs={{0,4},{4,0},{8,12},{12,8},{1,5},{5,1},{9,13},{13,9},{2,6},{6,2},{1... | collective-permute-start | bytes 393224 | tf_op jit(solution)/shard_map/ppermute | solution.py:238
  21.1 1.4 %collective-permute-start.8 = (bf16[128,512]{1,0:T(8,128)(2,1)S(1)}, bf16[128,512]{1,0:T(8,128)(2,1)S(1)}, u32[]{:S(2)}, u32[]{:S(2)}) collective-permute-start(bf16[128,512]{1,0:T(8,128)(2,1)S(1)} %get-tuple-element.28), channel_id=1, source_target_pairs={{0,12},{4,8},{8,4},{12,0},{1,13},{5,9},{9,5},{13,1},{2,14},{6,10},... | collective-permute-start | bytes 393224 | tf_op jit(solution)/shard_map/ppermute | solution.py:238
  22.5 7.8 %collective-permute-done.6.got = bf16[128,512]{1,0:T(8,128)(2,1)S(1)} collective-permute-done((bf16[128,512]{1,0:T(8,128)(2,1)S(1)}, bf16[128,512]{1,0:T(8,128)(2,1)S(1)}, u32[]{:S(2)}, u32[]{:S(2)}) %collective-permute-start.6) | collective-permute-done | bytes 131104 | tf_op jit(solution)/shard_map/ppermute | solution.py:238
  30.3 0.0 collective-permute-done.7.refs_0_
  30.3 0.0 collective-permute-done.8.refs_1_
  30.3 0.7 %sum_parts.1 = bf16[1,128,512]{2,1,0:T(8,128)(2,1)} custom-call(s32[1]{0:T(128)S(6)} %copy.10.rows, f32[128,512]{1,0:T(8,128)S(1)} %sum_half.1.kept, bf16[128,512]{1,0:T(8,128)(2,1)S(1)} %collective-permute-done.7.refs_0_, bf16[128,512]{1,0:T(8,128)(2,1)S(1)} %collective-permute-done.8.refs_1_), custom_call_target="tpu_custom_call" | custom-call | tf_op jit(solution)/shard_map/sum_parts/pallas_call | solution.py:167
  (1 shorter events, 0.0 us)
Async XLA Ops:
  0.0 14.0 %collective-permute-start.5 = (bf16[1,512,512]{2,1,0:T(8,128)(2,1)}, bf16[1,512,512]{2,1,0:T(8,128)(2,1)S(1)}, u32[]{:S(2)}, u32[]{:S(2)}) collective-permute-start(bf16[1,512,512]{2,1,0:T(8,128)(2,1)} %wave_hbm.3), channel_id=1, source_target_pairs={{0,1},{2,3},{1,0},{3,2},{4,5},{6,7},{5,4},{7,6},{8,9},{10,11},{9,8... | collective-permute-start | bytes 1572872 | tf_op jit(solution)/shard_map/ppermute | solution.py:189
  1.5 6.9 %collective-permute-start.1 = (bf16[128,512]{1,0:T(8,128)(2,1)S(1)}, bf16[128,512]{1,0:T(8,128)(2,1)S(1)}, u32[]{:S(2)}, u32[]{:S(2)}) collective-permute-start(bf16[128,512]{1,0:T(8,128)(2,1)S(1)} %get-tuple-element.18), channel_id=1, source_target_pairs={{0,2},{1,3},{2,0},{3,1},{4,6},{5,7},{6,4},{7,5},{8,10},{9,11},{10,... | collective-permute-start | bytes 393224 | tf_op jit(solution)/shard_map/ppermute | solution.py:189
  4.1 12.6 %collective-permute-start.3 = (bf16[256,512]{1,0:T(8,128)(2,1)S(1)}, bf16[256,512]{1,0:T(8,128)(2,1)S(1)}, u32[]{:S(2)}, u32[]{:S(2)}) collective-permute-start(bf16[256,512]{1,0:T(8,128)(2,1)S(1)} %get-tuple-element.21), channel_id=1, source_target_pairs={{0,2},{1,3},{2,0},{3,1},{4,6},{5,7},{6,4},{7,5},{8,10},{9,11},{10,... | collective-permute-start | bytes 786440 | tf_op jit(solution)/shard_map/ppermute | solution.py:189
  8.4 8.3 %collective-permute-start.2 = (bf16[128,512]{1,0:T(8,128)(2,1)S(1)}, bf16[128,512]{1,0:T(8,128)(2,1)S(1)}, u32[]{:S(2)}, u32[]{:S(2)}) collective-permute-start(bf16[128,512]{1,0:T(8,128)(2,1)S(1)} %collective-permute-done.1.refs_1_), channel_id=1, source_target_pairs={{0,4},{4,0},{8,12},{12,8},{1,5},{5,1},{9,13},{13,9},{2,6},{6,2},{1... | collective-permute-start | bytes 393224 | tf_op jit(solution)/shard_map/ppermute | solution.py:217
  11.1 5.6 %collective-permute-start = (s32[1]{0:T(128)}, s32[1]{0:T(128)}, u32[]{:S(2)}, u32[]{:S(2)}) collective-permute-start(s32[1]{0:T(128)} %param.6), channel_id=1, source_target_pairs={{0,2},{1,3},{2,0},{3,1},{4,6},{5,7},{6,4},{7,5},{8,10},{9,11},{10,... | collective-permute-start | bytes 20 | tf_op jit(solution)/shard_map/ppermute | solution.py:189
  12.6 1.4 %collective-permute-start.4 = (s32[1]{0:T(128)}, s32[1]{0:T(128)}, u32[]{:S(2)}, u32[]{:S(2)}) collective-permute-start(s32[1]{0:T(128)} %param.6), channel_id=1, source_target_pairs={{0,1},{2,3},{1,0},{3,2},{4,5},{6,7},{5,4},{7,6},{8,9},{10,11},{9,8... | collective-permute-start | bytes 20 | tf_op jit(solution)/shard_map/ppermute | solution.py:189
  18.0 12.2 %collective-permute-start.6 = (bf16[128,512]{1,0:T(8,128)(2,1)S(1)}, bf16[128,512]{1,0:T(8,128)(2,1)S(1)}, u32[]{:S(2)}, u32[]{:S(2)}) collective-permute-start(bf16[128,512]{1,0:T(8,128)(2,1)S(1)} %get-tuple-element.26), channel_id=1, source_target_pairs={{0,8},{4,12},{8,0},{12,4},{1,9},{5,13},{9,1},{13,5},{2,10},{6,14},... | collective-permute-start | bytes 393224 | tf_op jit(solution)/shard_map/ppermute | solution.py:238
  19.3 11.0 %collective-permute-start.7 = (bf16[128,512]{1,0:T(8,128)(2,1)S(1)}, bf16[128,512]{1,0:T(8,128)(2,1)S(1)}, u32[]{:S(2)}, u32[]{:S(2)}) collective-permute-start(bf16[128,512]{1,0:T(8,128)(2,1)S(1)} %get-tuple-element.27), channel_id=1, source_target_pairs={{0,4},{4,0},{8,12},{12,8},{1,5},{5,1},{9,13},{13,9},{2,6},{6,2},{1... | collective-permute-start | bytes 393224 | tf_op jit(solution)/shard_map/ppermute | solution.py:238
  21.1 9.2 %collective-permute-start.8 = (bf16[128,512]{1,0:T(8,128)(2,1)S(1)}, bf16[128,512]{1,0:T(8,128)(2,1)S(1)}, u32[]{:S(2)}, u32[]{:S(2)}) collective-permute-start(bf16[128,512]{1,0:T(8,128)(2,1)S(1)} %get-tuple-element.28), channel_id=1, source_target_pairs={{0,12},{4,8},{8,4},{12,0},{1,13},{5,9},{9,5},{13,1},{2,14},{6,10},... | collective-permute-start | bytes 393224 | tf_op jit(solution)/shard_map/ppermute | solution.py:238

commit v10 on v8

--- a/solution.py
+++ b/solution.py
@@ -148,7 +148,7 @@
     parts, share = len(sent) + 1, kept.shape[0]
     kept[...] = total[shard_rows(me, share), :]
     for step, part in enumerate(sent, 1):
-        part[...] = total[shard_rows(me ^ step, share), :].astype(jnp.bfloat16)
+        part[...] = total[shard_rows(lax.rem(me + step, parts), share), :].astype(jnp.bfloat16)
 
 
 def half_kernel(kept, got, total):
@@ -234,7 +234,7 @@
         info, *far_rows, *firsts, *swapped, *rests, *env, total,
     )
     turned = [
-        lax.ppermute(part, "term", [(i, i ^ step) for i in range(parts)])
+        lax.ppermute(part, "term", [(i, (i + step) % parts) for i in range(parts)])
         for step, part in enumerate(sent, 1)
     ]
     half = turned.pop(parts // 2 - 1)

time: 30.5 us -> 30.8 us (level)
  waiting for transfers between devices: 9.38 us -> 7.79 us
  starting transfers between devices: 12.2 us -> 13.2 us
  Pallas kernels: 8.2 us -> 8.92 us
    ppermute x3, waiting for transfers between devices: 8.67 us -> 6.86 us  [per_device(): lax.ppermute(part, 'term', [(i, (i + step) % parts) for i in range(parts)])]
    ppermute x3, starting transfers between devices: 5.55 us -> 6.74 us  [per_device(): lax.ppermute(part, 'term', [(i, (i + step) % parts) for i in range(parts)])]
    pallas_call x6, Pallas kernels: 8.2 us -> 8.92 us  [call(): pl.pallas_call(kernel, out_shape=[jax.ShapeDtypeStruct(shape, dtype) for...]
where the time goes in v10:
time: 30.8 us; the launch traced here: 30.7 us
  starting transfers between devices  13.2 us (43%)
  Pallas kernels  8.92 us (29%)
  waiting for transfers between devices  7.79 us (25%)
  between operations  0.71 us (2%)
    pallas_call x6, Pallas kernels, call(): pl.pallas_call(kernel, out_shape=[jax.ShapeDtypeStruct(shape, dtype) for...  8.92 us
    ppermute x3, waiting for transfers between devices, per_device(): lax.ppermute(part, 'term', [(i, (i + step) % parts) for i in range(parts)])  6.86 us
    ppermute x3, starting transfers between devices, per_device(): lax.ppermute(part, 'term', [(i, (i + step) % parts) for i in range(parts)])  6.74 us
    ppermute x5, starting transfers between devices, per_device(): send = lambda array, pairs: lax.ppermute(array, 'sector', pairs)  4.58 us
    ppermute x1, starting transfers between devices, per_device(): swapped = [lax.ppermute(array, 'term', swap) for array in firsts]  1.93 us
    ppermute x5, waiting for transfers between devices, per_device(): send = lambda array, pairs: lax.ppermute(array, 'sector', pairs)  0.79 us
  transfers between devices with their start and end apart: 9, of which 4 were waited for; matrix products, arithmetic and copies ran while one was open for 0% of the time, Pallas kernels for 20%

profile of v10, /device:TPU:0, one launch (start us, length us, event | category | flops | bytes accessed | tf_op | source)
XLA Modules:
  0.0 30.7 jit_solution(2512427247301358348)
XLA Ops:
  0.0 0.5 %collective-permute-start.5 = (bf16[1,512,512]{2,1,0:T(8,128)(2,1)}, bf16[1,512,512]{2,1,0:T(8,128)(2,1)S(1)}, u32[]{:S(2)}, u32[]{:S(2)}) collective-permute-start(bf16[1,512,512]{2,1,0:T(8,128)(2,1)} %wave_hbm.3), channel_id=1, source_target_pairs={{0,1},{2,3},{1,0},{3,2},{4,5},{6,7},{5,4},{7,6},{8,9},{10,11},{9,8... | collective-permute-start | bytes 1572872 | tf_op jit(solution)/shard_map/ppermute | solution.py:190
  0.5 1.0 %cut.1 = (bf16[128,512]{1,0:T(8,128)(2,1)S(1)}, bf16[256,512]{1,0:T(8,128)(2,1)S(1)}) custom-call(bf16[1,512,512]{2,1,0:T(8,128)(2,1)} %wave_hbm.3), custom_call_target="tpu_custom_call" | custom-call | tf_op jit(solution)/shard_map/cut/pallas_call | solution.py:169
  1.5 2.6 %collective-permute-start.1 = (bf16[128,512]{1,0:T(8,128)(2,1)S(1)}, bf16[128,512]{1,0:T(8,128)(2,1)S(1)}, u32[]{:S(2)}, u32[]{:S(2)}) collective-permute-start(bf16[128,512]{1,0:T(8,128)(2,1)S(1)} %get-tuple-element.18), channel_id=1, source_target_pairs={{0,2},{1,3},{2,0},{3,1},{4,6},{5,7},{6,4},{7,5},{8,10},{9,11},{10,... | collective-permute-start | bytes 393224 | tf_op jit(solution)/shard_map/ppermute | solution.py:190
  4.1 0.1 collective-permute-start.3
  4.8 3.7 %own_terms.1 = (s32[4]{0:T(128)S(1)}, f32[512,512]{1,0:T(8,128)S(1)}, bf16[4,512,512]{2,1,0:T(8,128)(2,1)S(1)}, bf16[4,512,512]{2,1,0:T(8,128)(2,1)S(1)}) custom-call(s32[4]{0:T(128)} %classes_hbm.1, s32[1]{0:T(128)S(6)} %copy.6.rows, bf16[1,512,512]{2,1,0:T(8,128)(2,1)} %wave_hbm.3, bf16[4,1,512,512]{3,2,1,0:T(8,128)(2,1)} %left_hbm.1, ...), custom_call_target="tpu_custom_call" | custom-call | tf_op jit(solution)/shard_map/own_terms/pallas_call | solution.py:169
  8.5 0.0 collective-permute-done.1.refs_1_
  8.5 1.9 %collective-permute-start.2 = (bf16[128,512]{1,0:T(8,128)(2,1)S(1)}, bf16[128,512]{1,0:T(8,128)(2,1)S(1)}, u32[]{:S(2)}, u32[]{:S(2)}) collective-permute-start(bf16[128,512]{1,0:T(8,128)(2,1)S(1)} %collective-permute-done.1.refs_1_), channel_id=1, source_target_pairs={{0,4},{4,0},{8,12},{12,8},{1,5},{5,1},{9,13},{13,9},{2,6},{6,2},{1... | collective-permute-start | bytes 393224 | tf_op jit(solution)/shard_map/ppermute | solution.py:218
  10.4 0.0 collective-permute-start.4
  10.4 1.5 %collective-permute-start = (s32[1]{0:T(128)}, s32[1]{0:T(128)}, u32[]{:S(2)}, u32[]{:S(2)}) collective-permute-start(s32[1]{0:T(128)} %param.6), channel_id=1, source_target_pairs={{0,2},{1,3},{2,0},{3,1},{4,6},{5,7},{6,4},{7,5},{8,10},{9,11},{10,... | collective-permute-start | bytes 20 | tf_op jit(solution)/shard_map/ppermute | solution.py:190
  11.9 0.0 collective-permute-done.4.refs_0_
  11.9 0.0 collective-permute-done.5.refs_1_
  11.9 1.3 %near_terms.1.refs_6_ = f32[512,512]{1,0:T(8,128)S(1)} custom-call(s32[4]{0:T(128)S(1)} %get-tuple-element.17.info, s32[1]{0:T(128)} %collective-permute-done.4.refs_0_, bf16[1,512,512]{2,1,0:T(8,128)(2,1)S(1)} %collective-permute-done.5.refs_1_, bf16[4,512,512]{2,1,0:T(8,128)(2,1)S(1)} %get-tuple-element.22.refs_2_.refs_4_, ...), custom_call_target="tpu_custom_call" | custom-call | tf_op jit(solution)/shard_map/near_terms/pallas_call | solution.py:169
  13.3 0.8 %collective-permute-done.refs_0_ = s32[1]{0:T(128)} collective-permute-done((s32[1]{0:T(128)}, s32[1]{0:T(128)}, u32[]{:S(2)}, u32[]{:S(2)}) %collective-permute-start) | collective-permute-done | bytes 36 | tf_op jit(solution)/shard_map/ppermute | solution.py:190
  14.1 0.1 collective-permute-done.2.refs_2_
  14.2 0.0 collective-permute-done.3.refs_3_
  14.2 2.1 %far_terms.1 = (f32[128,512]{1,0:T(8,128)S(1)}, bf16[128,512]{1,0:T(8,128)(2,1)S(1)}, bf16[128,512]{1,0:T(8,128)(2,1)S(1)}, bf16[128,512]{1,0:T(8,128)(2,1)S(1)}) custom-call(s32[4]{0:T(128)S(1)} %get-tuple-element.17.info, s32[1]{0:T(128)} %collective-permute-done.refs_0_, bf16[128,512]{1,0:T(8,128)(2,1)S(1)} %collective-permute-done.1.refs_1_, ...), custom_call_target="tpu_custom_call" | custom-call | tf_op jit(solution)/shard_map/far_terms/pallas_call | solution.py:169
  16.3 2.9 %collective-permute-start.6 = (bf16[128,512]{1,0:T(8,128)(2,1)S(1)}, bf16[128,512]{1,0:T(8,128)(2,1)S(1)}, u32[]{:S(2)}, u32[]{:S(2)}) collective-permute-start(bf16[128,512]{1,0:T(8,128)(2,1)S(1)} %get-tuple-element.26), channel_id=1, source_target_pairs={{0,8},{4,12},{8,0},{12,4},{1,9},{5,13},{9,1},{13,5},{2,10},{6,14},... | collective-permute-start | bytes 393224 | tf_op jit(solution)/shard_map/ppermute | solution.py:237
  19.2 0.5 %collective-permute-start.7 = (bf16[128,512]{1,0:T(8,128)(2,1)S(1)}, bf16[128,512]{1,0:T(8,128)(2,1)S(1)}, u32[]{:S(2)}, u32[]{:S(2)}) collective-permute-start(bf16[128,512]{1,0:T(8,128)(2,1)S(1)} %get-tuple-element.27), channel_id=1, source_target_pairs={{0,4},{4,8},{8,12},{12,0},{1,5},{5,9},{9,13},{13,1},{2,6},{6,10},{... | collective-permute-start | bytes 393224 | tf_op jit(solution)/shard_map/ppermute | solution.py:237
  19.7 3.3 %collective-permute-start.8 = (bf16[128,512]{1,0:T(8,128)(2,1)S(1)}, bf16[128,512]{1,0:T(8,128)(2,1)S(1)}, u32[]{:S(2)}, u32[]{:S(2)}) collective-permute-start(bf16[128,512]{1,0:T(8,128)(2,1)S(1)} %get-tuple-element.28), channel_id=1, source_target_pairs={{0,12},{4,0},{8,4},{12,8},{1,13},{5,1},{9,5},{13,9},{2,14},{6,2},{... | collective-permute-start | bytes 393224 | tf_op jit(solution)/shard_map/ppermute | solution.py:237
  23.1 5.9 %collective-permute-done.6.got = bf16[128,512]{1,0:T(8,128)(2,1)S(1)} collective-permute-done((bf16[128,512]{1,0:T(8,128)(2,1)S(1)}, bf16[128,512]{1,0:T(8,128)(2,1)S(1)}, u32[]{:S(2)}, u32[]{:S(2)}) %collective-permute-start.6) | collective-permute-done | bytes 131104 | tf_op jit(solution)/shard_map/ppermute | solution.py:237
  29.0 0.0 collective-permute-done.7.refs_0_
  29.0 0.9 %collective-permute-done.8.refs_1_ = bf16[128,512]{1,0:T(8,128)(2,1)S(1)} collective-permute-done((bf16[128,512]{1,0:T(8,128)(2,1)S(1)}, bf16[128,512]{1,0:T(8,128)(2,1)S(1)}, u32[]{:S(2)}, u32[]{:S(2)}) %collective-permute-start.8) | collective-permute-done | bytes 131104 | tf_op jit(solution)/shard_map/ppermute | solution.py:237
  30.0 0.7 %sum_parts.1 = bf16[1,128,512]{2,1,0:T(8,128)(2,1)} custom-call(s32[1]{0:T(128)S(6)} %copy.6.rows, f32[128,512]{1,0:T(8,128)S(1)} %sum_half.1.kept, bf16[128,512]{1,0:T(8,128)(2,1)S(1)} %collective-permute-done.7.refs_0_, bf16[128,512]{1,0:T(8,128)(2,1)S(1)} %collective-permute-done.8.refs_1_), custom_call_target="tpu_custom_call" | custom-call | tf_op jit(solution)/shard_map/sum_parts/pallas_call | solution.py:169
  (1 shorter events, 0.0 us)
Async XLA Ops:
  0.0 11.9 %collective-permute-start.5 = (bf16[1,512,512]{2,1,0:T(8,128)(2,1)}, bf16[1,512,512]{2,1,0:T(8,128)(2,1)S(1)}, u32[]{:S(2)}, u32[]{:S(2)}) collective-permute-start(bf16[1,512,512]{2,1,0:T(8,128)(2,1)} %wave_hbm.3), channel_id=1, source_target_pairs={{0,1},{2,3},{1,0},{3,2},{4,5},{6,7},{5,4},{7,6},{8,9},{10,11},{9,8... | collective-permute-start | bytes 1572872 | tf_op jit(solution)/shard_map/ppermute | solution.py:190
  1.5 7.0 %collective-permute-start.1 = (bf16[128,512]{1,0:T(8,128)(2,1)S(1)}, bf16[128,512]{1,0:T(8,128)(2,1)S(1)}, u32[]{:S(2)}, u32[]{:S(2)}) collective-permute-start(bf16[128,512]{1,0:T(8,128)(2,1)S(1)} %get-tuple-element.18), channel_id=1, source_target_pairs={{0,2},{1,3},{2,0},{3,1},{4,6},{5,7},{6,4},{7,5},{8,10},{9,11},{10,... | collective-permute-start | bytes 393224 | tf_op jit(solution)/shard_map/ppermute | solution.py:190
  4.1 10.1 %collective-permute-start.3 = (bf16[256,512]{1,0:T(8,128)(2,1)S(1)}, bf16[256,512]{1,0:T(8,128)(2,1)S(1)}, u32[]{:S(2)}, u32[]{:S(2)}) collective-permute-start(bf16[256,512]{1,0:T(8,128)(2,1)S(1)} %get-tuple-element.21), channel_id=1, source_target_pairs={{0,2},{1,3},{2,0},{3,1},{4,6},{5,7},{6,4},{7,5},{8,10},{9,11},{10,... | collective-permute-start | bytes 786440 | tf_op jit(solution)/shard_map/ppermute | solution.py:190
  8.5 5.7 %collective-permute-start.2 = (bf16[128,512]{1,0:T(8,128)(2,1)S(1)}, bf16[128,512]{1,0:T(8,128)(2,1)S(1)}, u32[]{:S(2)}, u32[]{:S(2)}) collective-permute-start(bf16[128,512]{1,0:T(8,128)(2,1)S(1)} %collective-permute-done.1.refs_1_), channel_id=1, source_target_pairs={{0,4},{4,0},{8,12},{12,8},{1,5},{5,1},{9,13},{13,9},{2,6},{6,2},{1... | collective-permute-start | bytes 393224 | tf_op jit(solution)/shard_map/ppermute | solution.py:218
  10.4 1.5 %collective-permute-start.4 = (s32[1]{0:T(128)}, s32[1]{0:T(128)}, u32[]{:S(2)}, u32[]{:S(2)}) collective-permute-start(s32[1]{0:T(128)} %param.6), channel_id=1, source_target_pairs={{0,1},{2,3},{1,0},{3,2},{4,5},{6,7},{5,4},{7,6},{8,9},{10,11},{9,8... | collective-permute-start | bytes 20 | tf_op jit(solution)/shard_map/ppermute | solution.py:190
  10.4 3.6 %collective-permute-start = (s32[1]{0:T(128)}, s32[1]{0:T(128)}, u32[]{:S(2)}, u32[]{:S(2)}) collective-permute-start(s32[1]{0:T(128)} %param.6), channel_id=1, source_target_pairs={{0,2},{1,3},{2,0},{3,1},{4,6},{5,7},{6,4},{7,5},{8,10},{9,11},{10,... | collective-permute-start | bytes 20 | tf_op jit(solution)/shard_map/ppermute | solution.py:190
  16.3 12.7 %collective-permute-start.6 = (bf16[128,512]{1,0:T(8,128)(2,1)S(1)}, bf16[128,512]{1,0:T(8,128)(2,1)S(1)}, u32[]{:S(2)}, u32[]{:S(2)}) collective-permute-start(bf16[128,512]{1,0:T(8,128)(2,1)S(1)} %get-tuple-element.26), channel_id=1, source_target_pairs={{0,8},{4,12},{8,0},{12,4},{1,9},{5,13},{9,1},{13,5},{2,10},{6,14},... | collective-permute-start | bytes 393224 | tf_op jit(solution)/shard_map/ppermute | solution.py:237
  19.2 9.8 %collective-permute-start.7 = (bf16[128,512]{1,0:T(8,128)(2,1)S(1)}, bf16[128,512]{1,0:T(8,128)(2,1)S(1)}, u32[]{:S(2)}, u32[]{:S(2)}) collective-permute-start(bf16[128,512]{1,0:T(8,128)(2,1)S(1)} %get-tuple-element.27), channel_id=1, source_target_pairs={{0,4},{4,8},{8,12},{12,0},{1,5},{5,9},{9,13},{13,1},{2,6},{6,10},{... | collective-permute-start | bytes 393224 | tf_op jit(solution)/shard_map/ppermute | solution.py:237
  19.7 10.2 %collective-permute-start.8 = (bf16[128,512]{1,0:T(8,128)(2,1)S(1)}, bf16[128,512]{1,0:T(8,128)(2,1)S(1)}, u32[]{:S(2)}, u32[]{:S(2)}) collective-permute-start(bf16[128,512]{1,0:T(8,128)(2,1)S(1)} %get-tuple-element.28), channel_id=1, source_target_pairs={{0,12},{4,0},{8,4},{12,8},{1,13},{5,1},{9,5},{13,9},{2,14},{6,2},{... | collective-permute-start | bytes 393224 | tf_op jit(solution)/shard_map/ppermute | solution.py:237
